TPU v7x, 32 devices: a whole 2x2x4 slice. The times are simulated.
32 devices in a mesh: ep: 8 (over y, x, core), dp: 4 (over z).
Axes of the slice: x: 2, y: 2, z: 4, core: 2. Of those that a mesh axis runs over, the one named last changes fastest.
Arguments:
- tokens: bfloat16 [8192, 1280], P(('ep', 'dp')), may hold values from -6 to 6
- expert_index: int32 [8192, 7], P(('ep', 'dp')), may hold values from 0 to 15, all different within a row; in each aligned block of 256 rows (0 to 255, 256 to 511, ...) at most 224 rows name the same one
- cotangent: bfloat16 [8192, 1280], P(('ep', 'dp')), may hold values from -6 to 6
- gains: float32 [1280, 2], P(('ep', 'dp')), may hold values from 0.5 to 1.5
- w_qkv: float32 [1280, 3840], P(('ep', 'dp')), may hold values from -0.15625 to 0.15625
- w_attn_out: float32 [1280, 1280], P(('ep', 'dp')), may hold values from -2.5 to 2.5
- w_router: float32 [1280, 16], P(('ep', 'dp')), may hold values from -0.078125 to 0.078125
- w_shared_in: float32 [1280, 1792], P(('ep', 'dp')), may hold values from -0.15625 to 0.15625
- w_shared_out: float32 [896, 1280], P(('ep', 'dp')), may hold values from -0.375 to 0.375
- w_expert_in: float32 [16, 1280, 1792], P('ep', 'dp'), may hold values from -0.15625 to 0.15625
- w_expert_out: float32 [16, 896, 1280], P('ep', 'dp'), may hold values from -2 to 2
Outputs:
- layer_out: bfloat16 [8192, 1280], P(('ep', 'dp'))
- tokens_grad: bfloat16 [8192, 1280], P(('ep', 'dp'))
- gains_grad: float32 [1280, 2], P(('ep', 'dp'))
- w_qkv_grad: float32 [1280, 3840], P(('ep', 'dp'))
- w_attn_out_grad: float32 [1280, 1280], P(('ep', 'dp'))
- w_router_grad: float32 [1280, 16], P(('ep', 'dp'))
- w_shared_in_grad: float32 [1280, 1792], P(('ep', 'dp'))
- w_shared_out_grad: float32 [896, 1280], P(('ep', 'dp'))
- w_expert_in_grad: float32 [16, 1280, 1792], P('ep', 'dp')
- w_expert_out_grad: float32 [16, 896, 1280], P('ep', 'dp')
Inputs may be any that keep to these rules, and one draw needn't show every extreme that they name: `expert_index`: each token names 7 different experts. Among the 256 rows of one device (aligned blocks of rows) no expert is named more than 224 times, and in every draw some expert is named exactly 224 times by the rows of some device.
All inputs are finite; a program needn't handle non-finite values.
Results may differ from a plain program's by a relative error of at most 0.024.
Values may be sent and summed in bfloat16 or wider, within the bound.
No kernel may reach another device: no remote copies, remote signals or barrier semaphores. Data moves between devices by JAX's collectives and lax.ppermute only.
A program may use at most 320 MiB of HBM per device.

v0:
```python
import jax
import jax.numpy as jnp
from jax import lax
from jax.sharding import PartitionSpec as P

H = 10
DH = 128
EFF = 896


EPS = 1e-06


def rope_tables(positions, head_size):
    frequency = 10000.0 ** (-2.0 * jnp.arange(head_size // 2, dtype=jnp.float32) / head_size)
    angles = positions[:, None] * frequency[None, :]
    return (jnp.cos(angles)[:, None, :], jnp.sin(angles)[:, None, :])


def rotate(values, cosine_table, sine_table):
    half_size = values.shape[-1] // 2
    first_half = values[..., :half_size]
    second_half = values[..., half_size:]
    return jnp.concatenate(
        [
            first_half * cosine_table - second_half * sine_table,
            first_half * sine_table + second_half * cosine_table,
        ],
        axis=-1,
    )


def unrotate(gradient, cosine_table, sine_table):
    half_size = gradient.shape[-1] // 2
    first_half = gradient[..., :half_size]
    second_half = gradient[..., half_size:]
    return jnp.concatenate(
        [
            first_half * cosine_table + second_half * sine_table,
            second_half * cosine_table - first_half * sine_table,
        ],
        axis=-1,
    )


def contract_rows(left_side, right_side):
    return lax.dot_general(
        left_side, right_side, (((0,), (0,)), ((), ())), preferred_element_type=jnp.float32
    )


def times_transposed(left_side, right_side):
    return lax.dot_general(
        left_side, right_side, (((1,), (1,)), ((), ())), preferred_element_type=jnp.float32
    )


def swiglu_back(gate_part, up_part, act_grad):
    sigma_gate = jax.nn.sigmoid(gate_part)
    silu_gate = gate_part * sigma_gate
    slope = sigma_gate * (1.0 + gate_part * (1.0 - sigma_gate))
    return jnp.concatenate([act_grad * up_part * slope, act_grad * silu_gate], axis=-1)


def per_device(
    tokens,
    expert_index,
    cotangent,
    gains,
    w_qkv,
    w_attn_out,
    w_router,
    w_shared_in,
    w_shared_out,
    w_expert_in,
    w_expert_out,
):
    bf16 = jnp.bfloat16
    f32 = jnp.float32
    tok_rows, model_width = tokens.shape
    head_count = H
    head_size = DH
    top_count = expert_index.shape[1]
    experts_here = w_expert_in.shape[0]
    experts = experts_here * lax.axis_size("ep")
    capacity = min(tok_rows, 2 * tok_rows * top_count // experts)
    score_scale = head_size ** (-0.5)
    gain_pair, qkv_weight, attn_weight, router_weight, shared_in_weight, shared_out_weight = (
        lax.all_gather(gains.astype(bf16), ("ep", "dp"), axis=0, tiled=True),
        lax.all_gather(w_qkv.astype(bf16), ("ep", "dp"), axis=0, tiled=True),
        lax.all_gather(w_attn_out.astype(bf16), ("ep", "dp"), axis=0, tiled=True),
        lax.all_gather(w_router.astype(bf16), ("ep", "dp"), axis=0, tiled=True),
        lax.all_gather(w_shared_in.astype(bf16), ("ep", "dp"), axis=0, tiled=True),
        lax.all_gather(w_shared_out.astype(bf16), ("ep", "dp"), axis=0, tiled=True),
    )
    gain_attn = gain_pair[:, 0].astype(f32)
    gain_ffn = gain_pair[:, 1].astype(f32)
    expert_in_weight, expert_out_weight = (
        lax.all_gather(w_expert_in.astype(bf16), "dp", axis=1, tiled=True),
        lax.all_gather(w_expert_out.astype(bf16), "dp", axis=1, tiled=True),
    )
    inputs = tokens.astype(f32)
    inv_first = lax.rsqrt(jnp.mean(inputs * inputs, axis=-1, keepdims=True) + EPS)
    normed_first = inputs * inv_first
    attn_in = (normed_first * gain_attn).astype(bf16)
    projected = jnp.dot(attn_in, qkv_weight, preferred_element_type=f32)
    offset = lax.axis_index("dp") * tok_rows
    query_pos = offset + jnp.arange(tok_rows, dtype=jnp.int32)
    cosine_table, sine_table = rope_tables(query_pos.astype(f32), head_size)
    queries = rotate(
        projected[:, :model_width].reshape(tok_rows, head_count, head_size),
        cosine_table,
        sine_table,
    ).astype(bf16)
    keys_local = (
        rotate(
            projected[:, model_width : 2 * model_width].reshape(tok_rows, head_count, head_size),
            cosine_table,
            sine_table,
        )
        .astype(bf16)
        .reshape(tok_rows, model_width)
    )
    values_local = projected[:, 2 * model_width :].astype(bf16)
    row_max = jnp.full((tok_rows, head_count), -1e30, f32)
    key_block = lax.all_gather(keys_local, "dp", axis=0, tiled=True).reshape(
        -1, head_count, head_size
    )
    value_block = lax.all_gather(values_local, "dp", axis=0, tiled=True).reshape(
        -1, head_count, head_size
    )
    scores = (
        jnp.einsum("qhd,khd->qhk", queries, key_block, preferred_element_type=f32) * score_scale
    )
    key_pos = jnp.arange(key_block.shape[0], dtype=jnp.int32)
    allowed = (key_pos[None, :] <= query_pos[:, None])[:, None, :]
    scores = jnp.where(allowed, scores, -1e30)
    new_max = jnp.maximum(row_max, jnp.max(scores, axis=-1))
    weights = jnp.where(allowed, jnp.exp(scores - new_max[..., None]), 0.0)
    row_sum = jnp.sum(weights, axis=-1)
    accumulated = jnp.einsum(
        "qhk,khd->qhd", weights.astype(bf16), value_block, preferred_element_type=f32
    )
    row_max, row_sum, accumulated = (new_max, row_sum, accumulated)
    attended = accumulated / row_sum[..., None]
    log_total = row_max + jnp.log(row_sum)
    attended_low = attended.reshape(tok_rows, model_width).astype(bf16)
    branch = jnp.dot(attended_low, attn_weight, preferred_element_type=f32)
    hidden = inputs + branch
    inv_second = lax.rsqrt(jnp.mean(hidden * hidden, axis=-1, keepdims=True) + EPS)
    normed_second = hidden * inv_second
    ffn_in = (normed_second * gain_ffn).astype(bf16)
    logits = jnp.dot(ffn_in, router_weight, preferred_element_type=f32)
    logit_exp = jnp.exp(logits - jnp.max(logits, axis=-1, keepdims=True))
    router_probs = logit_exp / jnp.sum(logit_exp, axis=-1, keepdims=True)
    choose = (expert_index[:, :, None] == jnp.arange(experts, dtype=jnp.int32)).astype(f32)
    gate_values = jnp.sum(choose * router_probs[:, None, :], axis=-1)
    shared_pre = jnp.dot(ffn_in, shared_in_weight, preferred_element_type=f32)
    shared_gate = shared_pre[:, :EFF]
    shared_up = shared_pre[:, EFF:]
    shared_act = (jax.nn.silu(shared_gate) * shared_up).astype(bf16)
    shared_out = jnp.dot(shared_act, shared_out_weight, preferred_element_type=f32)
    copies = tok_rows * top_count
    flat_choice = expert_index.reshape(-1)
    expert_hits = (flat_choice[:, None] == jnp.arange(experts, dtype=jnp.int32)).astype(jnp.int32)
    earlier = jnp.cumsum(expert_hits, axis=0) - expert_hits
    slot_index = jnp.sum(earlier * expert_hits, axis=1)
    slot_place = flat_choice * capacity + slot_index
    source = (
        jnp.zeros((experts * capacity,), jnp.int32)
        .at[slot_place]
        .set(jnp.arange(copies, dtype=jnp.int32) + 1)
    )
    filled = (source > 0)[:, None]
    copy_index = jnp.maximum(source - 1, 0)
    send_rows = jnp.where(filled, ffn_in[copy_index // top_count], jnp.zeros((), bf16)).reshape(
        experts, capacity, model_width
    )
    received = lax.all_to_all(send_rows, "ep", split_axis=0, concat_axis=1, tiled=True)
    expert_pre = jnp.einsum("erd,edf->erf", received, expert_in_weight, preferred_element_type=f32)
    expert_gate = expert_pre[..., :EFF]
    expert_up = expert_pre[..., EFF:]
    expert_act = (jax.nn.silu(expert_gate) * expert_up).astype(bf16)
    expert_result = jnp.einsum(
        "erf,efd->erd", expert_act, expert_out_weight, preferred_element_type=f32
    ).astype(bf16)
    returned = lax.all_to_all(expert_result, "ep", split_axis=1, concat_axis=0, tiled=True)
    picked = (
        returned.reshape(experts * capacity, model_width)[slot_place]
        .reshape(tok_rows, top_count, model_width)
        .astype(f32)
    )
    routed = jnp.sum(gate_values[..., None] * picked, axis=1)
    layer_out = (hidden + shared_out + routed).astype(bf16)
    upstream = cotangent.astype(f32)
    copy_grad = (
        (gate_values[..., None] * upstream[:, None, :]).astype(bf16).reshape(copies, model_width)
    )
    gate_grad = jnp.sum(picked * upstream[:, None, :], axis=-1)
    send_grad = jnp.where(filled, copy_grad[copy_index], jnp.zeros((), bf16)).reshape(
        experts, capacity, model_width
    )
    result_grad = lax.all_to_all(send_grad, "ep", split_axis=0, concat_axis=1, tiled=True)
    act_grad = jnp.einsum(
        "erd,efd->erf", result_grad, expert_out_weight, preferred_element_type=f32
    )
    pre_grad = swiglu_back(expert_gate, expert_up, act_grad).astype(bf16)
    expert_out_grad = jnp.einsum(
        "erf,erd->efd", expert_act, result_grad, preferred_element_type=f32
    )
    expert_in_grad = jnp.einsum("erd,erf->edf", received, pre_grad, preferred_element_type=f32)
    received_grad = jnp.einsum(
        "erf,edf->erd", pre_grad, expert_in_weight, preferred_element_type=f32
    ).astype(bf16)
    sent_grad = lax.all_to_all(received_grad, "ep", split_axis=1, concat_axis=0, tiled=True)
    routed_in_grad = jnp.sum(
        sent_grad.reshape(experts * capacity, model_width)[slot_place]
        .reshape(tok_rows, top_count, model_width)
        .astype(f32),
        axis=1,
    )
    expert_in_part, expert_out_part = (
        lax.psum_scatter(
            expert_in_grad.astype(jnp.bfloat16), "dp", scatter_dimension=1, tiled=True
        ).astype(jnp.float32),
        lax.psum_scatter(
            expert_out_grad.astype(jnp.bfloat16), "dp", scatter_dimension=1, tiled=True
        ).astype(jnp.float32),
    )
    prob_grad = jnp.sum(choose * gate_grad[..., None], axis=1)
    logit_grad = (
        router_probs * (prob_grad - jnp.sum(router_probs * prob_grad, axis=-1, keepdims=True))
    ).astype(bf16)
    router_grad = contract_rows(ffn_in, logit_grad)
    shared_act_grad = times_transposed(cotangent, shared_out_weight)
    shared_pre_grad = swiglu_back(shared_gate, shared_up, shared_act_grad).astype(bf16)
    shared_out_grad = contract_rows(shared_act, cotangent)
    shared_in_grad = contract_rows(ffn_in, shared_pre_grad)
    ffn_in_grad = (
        routed_in_grad
        + times_transposed(logit_grad, router_weight)
        + times_transposed(shared_pre_grad, shared_in_weight)
    )
    gain_ffn_grad = jnp.sum(ffn_in_grad * normed_second, axis=0)
    scaled_second = ffn_in_grad * gain_ffn
    hidden_grad = upstream + inv_second * (
        scaled_second
        - normed_second * jnp.mean(scaled_second * normed_second, axis=-1, keepdims=True)
    )
    branch_grad = hidden_grad.astype(bf16)
    attn_out_grad = contract_rows(attended_low, branch_grad)
    attended_grad = (
        times_transposed(branch_grad, attn_weight)
        .astype(bf16)
        .reshape(tok_rows, head_count, head_size)
    )
    mean_term = jnp.sum(attended_grad.astype(f32) * attended, axis=-1)
    seq_len = tok_rows * lax.axis_size("dp")
    all_keys, all_values = (
        lax.all_gather(keys_local, "dp", axis=0, tiled=True),
        lax.all_gather(values_local, "dp", axis=0, tiled=True),
    )
    block_len = min(512, seq_len)
    block_count = seq_len // block_len

    def key_step(query_grad, block_item):
        key_rows, value_rows, first_row = block_item
        key_block = key_rows.reshape(block_len, head_count, head_size)
        value_block = value_rows.reshape(block_len, head_count, head_size)
        scores = (
            jnp.einsum("qhd,khd->qhk", queries, key_block, preferred_element_type=f32) * score_scale
        )
        key_pos = first_row + jnp.arange(block_len, dtype=jnp.int32)
        allowed = (key_pos[None, :] <= query_pos[:, None])[:, None, :]
        weights = jnp.where(
            allowed, jnp.exp(jnp.where(allowed, scores, -1e30) - log_total[..., None]), 0.0
        )
        weight_grad = jnp.einsum(
            "qhd,khd->qhk", attended_grad, value_block, preferred_element_type=f32
        )
        score_grad = (weights * (weight_grad - mean_term[..., None])).astype(bf16)
        value_step = jnp.einsum(
            "qhk,qhd->khd", weights.astype(bf16), attended_grad, preferred_element_type=f32
        )
        key_step_grad = (
            jnp.einsum("qhk,qhd->khd", score_grad, queries, preferred_element_type=f32)
            * score_scale
        )
        query_grad = (
            query_grad
            + jnp.einsum("qhk,khd->qhd", score_grad, key_block, preferred_element_type=f32)
            * score_scale
        )
        return (
            query_grad,
            (
                key_step_grad.reshape(block_len, model_width),
                value_step.reshape(block_len, model_width),
            ),
        )

    query_grad, (key_terms, value_terms) = lax.scan(
        key_step,
        jnp.zeros((tok_rows, head_count, head_size), f32),
        (
            all_keys.reshape(block_count, block_len, model_width),
            all_values.reshape(block_count, block_len, model_width),
            jnp.arange(block_count, dtype=jnp.int32) * block_len,
        ),
    )
    key_grad, value_grad = (
        lax.psum_scatter(
            key_terms.reshape(seq_len, model_width).astype(jnp.bfloat16),
            "dp",
            scatter_dimension=0,
            tiled=True,
        ).astype(jnp.float32),
        lax.psum_scatter(
            value_terms.reshape(seq_len, model_width).astype(jnp.bfloat16),
            "dp",
            scatter_dimension=0,
            tiled=True,
        ).astype(jnp.float32),
    )
    query_pre = unrotate(query_grad, cosine_table, sine_table).reshape(tok_rows, model_width)
    key_pre = unrotate(
        key_grad.reshape(tok_rows, head_count, head_size), cosine_table, sine_table
    ).reshape(tok_rows, model_width)
    projected_grad = jnp.concatenate([query_pre, key_pre, value_grad], axis=1).astype(bf16)
    qkv_grad = contract_rows(attn_in, projected_grad)
    attn_in_grad = times_transposed(projected_grad, qkv_weight)
    gain_attn_grad = jnp.sum(attn_in_grad * normed_first, axis=0)
    scaled_first = attn_in_grad * gain_attn
    input_grad = hidden_grad + inv_first * (
        scaled_first - normed_first * jnp.mean(scaled_first * normed_first, axis=-1, keepdims=True)
    )
    gain_grad = jnp.stack([gain_attn_grad, gain_ffn_grad], axis=1)
    shards = (
        lax.psum_scatter(gain_grad, ("ep", "dp"), scatter_dimension=0, tiled=True),
        lax.psum_scatter(qkv_grad, ("ep", "dp"), scatter_dimension=0, tiled=True),
        lax.psum_scatter(attn_out_grad, ("ep", "dp"), scatter_dimension=0, tiled=True),
        lax.psum_scatter(router_grad, ("ep", "dp"), scatter_dimension=0, tiled=True),
        lax.psum_scatter(shared_in_grad, ("ep", "dp"), scatter_dimension=0, tiled=True),
        lax.psum_scatter(shared_out_grad, ("ep", "dp"), scatter_dimension=0, tiled=True),
    )
    return (
        layer_out,
        input_grad.astype(bf16),
        shards[0],
        shards[1],
        shards[2],
        shards[3],
        shards[4],
        shards[5],
        expert_in_part,
        expert_out_part,
    )


def solution(mesh):
    return jax.shard_map(
        per_device,
        mesh=mesh,
        in_specs=(
            P(("ep", "dp"), None),
            P(("ep", "dp"), None),
            P(("ep", "dp"), None),
            P(("ep", "dp"), None),
            P(("ep", "dp"), None),
            P(("ep", "dp"), None),
            P(("ep", "dp"), None),
            P(("ep", "dp"), None),
            P(("ep", "dp"), None),
            P("ep", "dp", None),
            P("ep", "dp", None),
        ),
        out_specs=(
            P(("ep", "dp"), None),
            P(("ep", "dp"), None),
            P(("ep", "dp"), None),
            P(("ep", "dp"), None),
            P(("ep", "dp"), None),
            P(("ep", "dp"), None),
            P(("ep", "dp"), None),
            P(("ep", "dp"), None),
            P("ep", "dp", None),
            P("ep", "dp", None),
        ),
        check_vma=False,
    )
```

profile of v0, /device:TPU:0, one launch (start us, length us, event | category | flops | bytes accessed | tf_op | source)
XLA Modules:
  0.0 2122.3 jit_solution(14169294589857015597)
XLA Ops:
  9.8 69.8 %all-gather = bf16[32,40,2]{1,2,0:T(2,128)(2,1)S(1)} all-gather(bf16[1,40,2]{1,2,0:T(2,128)(2,1)S(1)} %convert_bitcast_fusion.2), channel_id=1, replica_groups=mesh['ep'=8,'dp'=4] {'ep','dp'}, dimensions={0}, use_global_device_ids=true | all-gather | bytes 5280 | tf_op jit(solution)/shard_map/all_gather | solution.py:89
  81.7 16.2 all-gather.12.cloned.1.call-done
  147.1 69.0 %all-gather.2 = bf16[32,40,16]{1,2,0:T(8,128)(2,1)S(1)} all-gather(bf16[1,40,16]{1,2,0:T(8,128)(2,1)S(1)} %convert_bitcast_fusion.1), channel_id=1, replica_groups=mesh['ep'=8,'dp'=4] {'ep','dp'}, dimensions={0}, use_global_device_ids=true | all-gather | bytes 42240 | tf_op jit(solution)/shard_map/all_gather | solution.py:92
  221.6 10.2 mul.417
  255.7 42.0 %all-gather.18.cloned.1.call-done = bf16[1280,1280]{1,0:T(8,128)(2,1)} async-done(((bf16[40,1280]{1,0:T(8,128)(2,1)}), bf16[1280,1280]{1,0:T(8,128)(2,1)}) %all-gather.18.cloned.1.call-update) | async-done | bytes 3276816 | tf_op jit(solution)/shard_map/all_gather | solution.py:91
  303.6 12.4 gather_fusion
  322.4 22.3 %gather_fusion.2 = bf16[3584,1280]{1,0:T(8,128)(2,1)} fusion(bf16[1792,1280]{1,0:T(8,128)(2,1)} %multiply_convert_fusion.3, s32[4096]{0:T(1024)S(1)} %copy-done.64), kind=kCustom, calls=%fused_computation.2 | custom fusion | bytes 18364416 | tf_op jit(solution)/shard_map/gather | solution.py:200
  344.7 10.0 broadcast_select_fusion
  354.6 105.9 %all_to_all.66 = bf16[16,224,1280]{2,1,0:T(8,128)(2,1)} all-to-all(bf16[16,224,1280]{2,1,0:T(8,128)(2,1)S(1)} %get-tuple-element.242), channel_id=1, replica_groups=mesh['ep'=8,'dp'=4] {'ep'}, dimensions={0} | all-to-all | bytes 18350080 | tf_op jit(solution)/shard_map/all_to_all | solution.py:179
  474.6 93.6 %all-to-all-done.2 = bf16[16,224,1280]{2,1,0:T(8,128)(2,1)} async-done(((bf16[16,224,1280]{2,1,0:T(8,128)(2,1)}), bf16[16,224,1280]{2,1,0:T(8,128)(2,1)}, u32[]{:S(2)}, u32[]{:S(2)}) %all-to-all-start.2) | async-done | bytes 9175072 | tf_op jit(solution)/shard_map/all_to_all | solution.py:203
  576.0 25.4 %fusion.90 = f32[2,1792,1792]{1,2,0:T(8,128)} fusion(bf16[2,1792,1280]{2,1,0:T(8,128)(2,1)} %bitcast.214, bf16[2,1280,1792]{2,1,0:T(8,128)(2,1)} %all-gather.22.cloned.1.call-done), kind=kOutput, calls=%fused_computation.188 | convolution fusion | flops 16441671680 | bytes 44040192 | tf_op jit(solution)/shard_map/erd,edf->erf/dot_general | solution.py:180
  601.4 25.8 %multiply_convert_fusion.1 = (bf16[2,1792,896]{1,2,0:T(8,128)(2,1)}, bf16[2,1792,896]{1,2,0:T(8,128)(2,1)}, bf16[2,1792,896]{1,2,0:T(8,128)(2,1)}) fusion(f32[2,1792,1792]{1,2,0:T(8,128)} %fusion.90, bf16[2,1792,1280]{2,1,0:T(8,128)(2,1)} %bitcast.216, bf16[2,896,1280]{2,1,0:T(8,128)(2,1)} %all-gather.24.cloned.1.call-done), kind=kOutput, calls=%fused_computation.36 | convolution fusion | flops 8269004800 | bytes 58720256 | tf_op jit(solution)/shard_map/erd,efd->erf/dot_general | solution.py:204
  627.3 13.2 convolution_convert_fusion.2
  640.5 30.3 %copy.212 = bf16[2,1792,1280]{2,0,1:T(2,128)(2,1)} copy(bf16[2,1792,1280]{2,1,0:T(8,128)(2,1)S(1)} %convolution_convert_fusion.2) | data formatting | bytes 18350080 | tf_op jit(solution)/shard_map/convert_element_type | solution.py:186
  677.5 24.4 %convolution_convert_fusion.1 = bf16[2,1792,1280]{2,1,0:T(8,128)(2,1)S(1)} fusion(bf16[2,1280,1792]{2,1,0:T(8,128)(2,1)} %all-gather.22.cloned.1.call-done, bf16[2,1792,896]{1,2,0:T(8,128)(2,1)} %get-tuple-element.214, bf16[2,1792,896]{1,2,0:T(8,128)(2,1)} %get-tuple-element.213), kind=kOutput, calls=%fused_computation.41 | convolution fusion | flops 16471949312 | bytes 31195136 | tf_op jit(solution)/shard_map/erf,edf->erd/dot_general | solution.py:212
  701.9 30.3 %copy.217 = bf16[2,1792,1280]{2,0,1:T(2,128)(2,1)} copy(bf16[2,1792,1280]{2,1,0:T(8,128)(2,1)S(1)} %convolution_convert_fusion.1) | data formatting | bytes 18350080 | tf_op jit(solution)/shard_map/convert_element_type | solution.py:214
  732.1 54.0 %all-to-all-done.1 = bf16[2,1792,1280]{2,0,1:T(2,128)(2,1)} async-done(((bf16[2,1792,1280]{2,0,1:T(2,128)(2,1)}), bf16[2,1792,1280]{2,0,1:T(2,128)(2,1)}, u32[]{:S(2)}, u32[]{:S(2)}) %all-to-all-start.1) | async-done | bytes 9175072 | tf_op jit(solution)/shard_map/all_to_all | solution.py:187
  800.6 72.3 %all-gather.20.cloned.1.call-done = bf16[1280,1792]{1,0:T(8,128)(2,1)} async-done(((bf16[40,1792]{1,0:T(8,128)(2,1)}), bf16[1280,1792]{1,0:T(8,128)(2,1)}) %all-gather.20.cloned.1.call-update) | async-done | bytes 4587536 | tf_op jit(solution)/shard_map/all_gather | solution.py:93
  889.8 15.0 gather_fusion.1
  933.2 15.0 gather_fusion.3
  973.3 65.3 %while.15 = (s32[]{:T(128)}, f32[256,10,128]{0,2,1:T(8,128)}, bf16[2,512,1280]{2,1,0:T(8,128)(2,1)}, bf16[2,512,1280]{2,1,0:T(8,128)(2,1)}, bf16[2,512,1280]{1,2...) while((s32[]{:T(128)}, f32[256,10,128]{0,2,1:T(8,128)}, ...), condition=%wide.region_19.20_spmd.clone, body=%wide.region_18.19_spmd.clone.sunk | while | flops 1695875840 | bytes 83006256 | solution.py:302
  1043.9 14.7 convolution_convert_fusion.3
  1058.7 25.2 %convolution_convert_fusion = bf16[2,1280,1792]{2,1,0:T(8,128)(2,1)} fusion(bf16[2,1792,1280]{2,1,0:T(8,128)(2,1)} %bitcast.215, bf16[2,1792,896]{1,2,0:T(8,128)(2,1)} %get-tuple-element.214, bf16[2,1792,896]{1,2,0:T(8,128)(2,1)} %get-tuple-element.213), kind=kOutput, calls=%fused_computation.40 | convolution fusion | flops 16471949312 | bytes 31195136 | tf_op jit(solution)/shard_map/erd,erf->edf/dot_general | solution.py:211
  1107.9 35.3 %reduce-scatter.14.cloned.1.call-done = bf16[256,1280]{0,1:T(8,128)(2,1)} async-done(((bf16[1024,1280]{0,1:T(8,128)(2,1)}), bf16[256,1280]{0,1:T(8,128)(2,1)}) %reduce-scatter.14.cloned.1.call-update) | async-done | bytes 655376 | tf_op jit(solution)/shard_map/reduce_scatter | solution.py:318
  1143.2 10.7 fusion.50
  1158.1 122.9 %fusion.2 = f32[32,1280]{1,0:T(8,128)S(1)} fusion(f32[896,1280]{1,0:T(8,128)} %fusion.91), kind=kCustom, calls=%all-reduce-scatter | all-reduce-scatter fusion | flops 1310721 | bytes 4751360
  1313.9 57.8 %reduce-scatter.24.cloned.1.call-done = bf16[2,224,1280]{2,1,0:T(8,128)(2,1)} async-done(((bf16[2,896,1280]{2,1,0:T(8,128)(2,1)}), bf16[2,224,1280]{2,1,0:T(8,128)(2,1)}) %reduce-scatter.24.cloned.1.call-update) | async-done | bytes 1146896 | tf_op jit(solution)/shard_map/reduce_scatter | solution.py:226
  1382.6 47.0 %all-reduce = f32[1280,2]{0,1:T(2,128)S(1)} all-reduce(f32[1280,2]{0,1:T(2,128)S(1)} %pad_maximum_fusion.13), channel_id=4, replica_groups=mesh['ep'=8,'dp'=4] {'ep','dp'}, use_global_device_ids=true, to_apply=%region_25.26.clone | all-reduce | flops 2560 | bytes 20480
  1432.8 99.7 %reduce-scatter.22.cloned.1.call-done = bf16[2,320,1792]{2,1,0:T(8,128)(2,1)} async-done(((bf16[2,1280,1792]{2,1,0:T(8,128)(2,1)}), bf16[2,320,1792]{2,1,0:T(8,128)(2,1)}) %reduce-scatter.22.cloned.1.call-update) | async-done | bytes 2293776 | tf_op jit(solution)/shard_map/reduce_scatter | solution.py:223
  1536.7 201.5 %reduce-scatter.20.cloned.1.call-done = f32[40,1792]{1,0:T(8,128)} async-done(((f32[1280,1792]{1,0:T(8,128)}), f32[40,1792]{1,0:T(8,128)}) %reduce-scatter.20.cloned.1.call-update) | async-done | bytes 286736 | tf_op jit(solution)/shard_map/reduce_scatter | solution.py:343
  1738.2 160.8 %reduce-scatter.18.cloned.1.call-done = f32[40,1280]{1,0:T(8,128)} async-done(((f32[1280,1280]{1,0:T(8,128)}), f32[40,1280]{1,0:T(8,128)}) %reduce-scatter.18.cloned.1.call-update) | async-done | bytes 204816 | tf_op jit(solution)/shard_map/reduce_scatter | solution.py:341
  1899.0 216.2 %reduce-scatter.16.cloned.1.call-done = f32[40,3840]{1,0:T(8,128)} async-done(((f32[1280,3840]{1,0:T(8,128)}), f32[40,3840]{1,0:T(8,128)}) %reduce-scatter.16.cloned.1.call-update) | async-done | bytes 614416 | tf_op jit(solution)/shard_map/reduce_scatter | solution.py:340
  (386 shorter events, 357.4 us)
Async XLA Ops:
  7.2 90.8 %all-gather.12.cloned.1.call-start = ((), (), s32[]{:S(2)}) async-start(), calls=%async_computation.11 | async-start | bytes 10137600 | tf_op jit(solution)/shard_map/all_gather | solution.py:90
  9.1 224.4 %all-gather.16.cloned.1.call-start = ((), (), s32[]{:S(2)}) async-start(), calls=%async_computation.13 | async-start | bytes 3276800 | tf_op jit(solution)/shard_map/all_gather | solution.py:126
  79.8 221.2 %copy-start.57 = (f32[1280]{0:T(1024)}, f32[1280]{0:T(1024)S(1)}, u32[]{:S(2)}) copy-start(f32[1280]{0:T(1024)S(1)} %get-tuple-element.185) | copy-start | bytes 15364
  126.2 118.4 %all-gather.14.cloned.1.call-start = ((), (), s32[]{:S(2)}) async-start(), calls=%async_computation.12 | async-start | bytes 3276800 | tf_op jit(solution)/shard_map/all_gather | solution.py:129
  128.5 169.2 %all-gather.18.cloned.1.call-start = ((), (), s32[]{:S(2)}) async-start(), calls=%async_computation.14 | async-start | bytes 3379200 | tf_op jit(solution)/shard_map/all_gather | solution.py:91
  129.3 446.7 %all-gather.22.cloned.1.call-start = ((), (), s32[]{:S(2)}) async-start(), calls=%async_computation.16 | async-start | bytes 11468800 | tf_op jit(solution)/shard_map/all_gather | solution.py:99
  133.3 83.6 %copy-start.15 = (bf16[256,1280]{1,0:T(8,128)(2,1)S(1)}, bf16[256,1280]{1,0:T(8,128)(2,1)}, u32[]{:S(2)}) copy-start(bf16[256,1280]{1,0:T(8,128)(2,1)} %param.15) | copy-start | bytes 1966084
  460.5 107.7 %all-to-all-start.2 = ((bf16[16,224,1280]{2,1,0:T(8,128)(2,1)}), bf16[16,224,1280]{2,1,0:T(8,128)(2,1)}, u32[]{:S(2)}, u32[]{:S(2)}) async-start(bf16[16,224,1280]{2,1,0:T(8,128)(2,1)} %get-tuple-element.241), calls=%async_computation.2 | async-start | bytes 18350080 | tf_op jit(solution)/shard_map/all_to_all | solution.py:203
  465.7 135.7 %all-gather.24.cloned.1.call-start = ((), (), s32[]{:S(2)}) async-start(), calls=%async_computation.17 | async-start | bytes 5734400 | tf_op jit(solution)/shard_map/all_gather | solution.py:100
  670.8 115.4 %all-to-all-start.1 = ((bf16[2,1792,1280]{2,0,1:T(2,128)(2,1)}), bf16[2,1792,1280]{2,0,1:T(2,128)(2,1)}, u32[]{:S(2)}, u32[]{:S(2)}) async-start(bf16[2,1792,1280]{2,0,1:T(2,128)(2,1)} %copy.212), calls=%async_computation.1 | async-start | bytes 18350080 | tf_op jit(solution)/shard_map/all_to_all | solution.py:187
  676.0 116.0 %all-gather.26.cloned.1.call-start = ((), (), s32[]{:S(2)}) async-start(), calls=%async_computation.25 | async-start | bytes 2703360 | tf_op jit(solution)/shard_map/all_gather | solution.py:94
  676.7 196.2 %all-gather.20.cloned.1.call-start = ((), (), s32[]{:S(2)}) async-start(), calls=%async_computation.15 | async-start | bytes 4730880 | tf_op jit(solution)/shard_map/all_gather | solution.py:93
  786.1 138.3 %all-to-all-start.3 = ((bf16[2,1792,1280]{2,0,1:T(2,128)(2,1)}), bf16[2,1792,1280]{2,0,1:T(2,128)(2,1)}, u32[]{:S(2)}, u32[]{:S(2)}) async-start(bf16[2,1792,1280]{2,0,1:T(2,128)(2,1)} %copy.217), calls=%async_computation.3 | async-start | bytes 18350080 | tf_op jit(solution)/shard_map/all_to_all | solution.py:215
  791.2 305.6 %reduce-scatter.12.cloned.1.call-start = ((), (), s32[]{:S(2)}) async-start(), calls=%async_computation.18 | async-start | bytes 3276800 | tf_op jit(solution)/shard_map/reduce_scatter | solution.py:312
  791.9 97.9 %copy-start.60 = (s32[2048]{0:T(1024)}, s32[2048]{0:T(1024)S(1)}, u32[]{:S(2)}) copy-start(s32[2048]{0:T(1024)S(1)} %pad_clamp_fusion.2) | copy-start | bytes 24580
  796.5 76.4 %copy-start.1 = (bf16[256,1280]{1,0:T(8,128)(2,1)S(1)}, bf16[256,1280]{1,0:T(8,128)(2,1)}, u32[]{:S(2)}) copy-start(bf16[256,1280]{1,0:T(8,128)(2,1)} %copy-done) | copy-start | bytes 1966084
  1038.6 104.6 %reduce-scatter.14.cloned.1.call-start = ((), (), s32[]{:S(2)}) async-start(), calls=%async_computation.19 | async-start | bytes 3276800 | tf_op jit(solution)/shard_map/reduce_scatter | solution.py:318
  1042.9 269.5 %all-reduce.6.cloned.1.call-start = ((), (), s32[]{:S(2)}) async-start(), calls=%async_computation.26 | async-start | bytes 163840
  1043.9 327.9 %reduce-scatter.24.cloned.1.call-start = ((), (), s32[]{:S(2)}) async-start(), calls=%async_computation.24 | async-start | bytes 5734400 | tf_op jit(solution)/shard_map/reduce_scatter | solution.py:226
  1058.6 473.9 %reduce-scatter.22.cloned.1.call-start = ((), (), s32[]{:S(2)}) async-start(), calls=%async_computation.23 | async-start | bytes 11468800 | tf_op jit(solution)/shard_map/reduce_scatter | solution.py:223
  1083.9 654.3 %reduce-scatter.20.cloned.1.call-start = ((), (), s32[]{:S(2)}) async-start(), calls=%async_computation.22 | async-start | bytes 9461760 | tf_op jit(solution)/shard_map/reduce_scatter | solution.py:343
  1089.9 809.1 %reduce-scatter.18.cloned.1.call-start = ((), (), s32[]{:S(2)}) async-start(), calls=%async_computation.21 | async-start | bytes 6758400 | tf_op jit(solution)/shard_map/reduce_scatter | solution.py:341
  1095.1 1020.2 %reduce-scatter.16.cloned.1.call-start = ((), (), s32[]{:S(2)}) async-start(), calls=%async_computation.20 | async-start | bytes 20275200 | tf_op jit(solution)/shard_map/reduce_scatter | solution.py:340
  1158.1 150.8 %copy-start.68 = (f32[1280]{0:T(1024)S(1)}, f32[1280]{0:T(1024)}, u32[]{:S(2)}) copy-start(f32[1280]{0:T(1024)} %get-tuple-element.181) | copy-start | bytes 15364
  1158.1 150.9 %copy-start.11 = (f32[256,1280]{1,0:T(8,128)S(1)}, f32[256,1280]{1,0:T(8,128)}, u32[]{:S(2)}) copy-start(f32[256,1280]{1,0:T(8,128)} %copy-done.9) | copy-start | bytes 3932164
  1158.1 150.9 %copy-start.23 = (f32[256,1280]{1,0:T(8,128)S(1)}, f32[256,1280]{1,0:T(8,128)}, u32[]{:S(2)}) copy-start(f32[256,1280]{1,0:T(8,128)} %get-tuple-element.180) | copy-start | bytes 3932164
  1281.0 12.0 collective-permute-start
  1283.2 9.9 collective-permute-start.1
  1285.2 14.0 collective-permute-start.2
  1289.1 3.9 collective-permute-start.3
  1312.4 62.1 %copy-start.28 = (bf16[256,10,128]{0,2,1:T(8,128)(2,1)S(1)}, bf16[256,10,128]{0,2,1:T(8,128)(2,1)}, u32[]{:S(2)}) copy-start(bf16[256,10,128]{0,2,1:T(8,128)(2,1)} %copy-done.27) | copy-start | bytes 1966084
  1312.4 62.1 %copy-start.30 = (bf16[256,10,128]{0,2,1:T(8,128)(2,1)S(1)}, bf16[256,10,128]{0,2,1:T(8,128)(2,1)}, u32[]{:S(2)}) copy-start(bf16[256,10,128]{0,2,1:T(8,128)(2,1)} %copy-done.29) | copy-start | bytes 1966084
  (78 other events, 855.1 us)
Sparse Core Ops, SparseCore 0:
  11.4 86.5 all-gather.11
  126.3 54.5 all-gather.15
  182.4 54.1 all-gather.13
  239.9 57.7 all-gather.17
  299.6 161.3 all-gather.21
  468.4 87.4 all-gather.23
  680.2 82.0 all-gather.25
  765.7 107.1 all-gather.19
  1038.7 49.9 reduce-scatter.11
  1091.4 51.7 reduce-scatter.13
  1148.8 128.1 all-reduce.5
  1279.2 92.4 reduce-scatter.23
  1374.1 158.3 reduce-scatter.21
  1535.3 202.8 reduce-scatter.19
  1740.9 158.0 reduce-scatter.17
  1905.9 209.3 reduce-scatter.15
where the time goes:
time: 2130 us; the launch traced here: 2120 us
  waiting for transfers between devices  1060 us (50%)
  blocking collectives  415 us (19%)
  local copies, waits for them, and re-layouts  292 us (14%)
  matrix products  237 us (11%)
  other arithmetic  79.6 us (4%)
  starting transfers between devices  27.2 us (1%)
    reduce_scatter x1, waiting for transfers between devices, per_device(): lax.psum_scatter(qkv_grad, ('ep', 'dp'), scatter_dimension=0, tiled=True)  216 us
    reduce_scatter x1, waiting for transfers between devices, per_device(): lax.psum_scatter(shared_in_grad, ('ep', 'dp'), scatter_dimension=0, tiled...  202 us
    unnamed x2, blocking collectives  170 us
    reduce_scatter x1, waiting for transfers between devices, per_device(): lax.psum_scatter(attn_out_grad, ('ep', 'dp'), scatter_dimension=0, tiled=...  161 us
    all_to_all x1, blocking collectives, per_device(): lax.all_to_all(send_rows, 'ep', split_axis=0, concat_axis=1, tiled=True)  106 us
    reduce_scatter x1, waiting for transfers between devices, per_device(): lax.psum_scatter(expert_in_grad.astype(jnp.bfloat16), 'dp', scatter_dimen...  99.7 us
    all_to_all x1, waiting for transfers between devices, per_device(): lax.all_to_all(send_grad, 'ep', split_axis=0, concat_axis=1, tiled=True)  93.6 us
    all_gather x1, waiting for transfers between devices, per_device(): lax.all_gather(w_shared_in.astype(bf16), ('ep', 'dp'), axis=0, tiled=True)  72.3 us
  transfers between devices with their start and end apart: 23, of which 14 were waited for; matrix products, arithmetic and copies ran while one was open for 24% of the time, Pallas kernels for 0%

commit v1 on v0

v1 whole, which is shorter than its diff:
```python
import functools

import jax
import jax.numpy as jnp
from jax import lax
from jax.experimental import pallas as pl
from jax.experimental.pallas import tpu as pltpu
from jax.sharding import PartitionSpec as P

H = 10
DH = 128
EFF = 896
EPS = 1e-06
NEG = -1e30
FAR = 1 << 30

bf16 = jnp.bfloat16
f32 = jnp.float32


def contract_rows(left_side, right_side):
    return lax.dot_general(
        left_side, right_side, (((0,), (0,)), ((), ())), preferred_element_type=f32
    )


def times_transposed(left_side, right_side):
    return lax.dot_general(
        left_side, right_side, (((1,), (1,)), ((), ())), preferred_element_type=f32
    )


def matmul(left_side, right_side):
    return jnp.dot(left_side, right_side, preferred_element_type=f32)


def swiglu_back(gate_part, up_part, act_grad):
    sigma_gate = jax.nn.sigmoid(gate_part)
    silu_gate = gate_part * sigma_gate
    slope = sigma_gate * (1.0 + gate_part * (1.0 - sigma_gate))
    return jnp.concatenate([act_grad * up_part * slope, act_grad * silu_gate], axis=-1)


def flip(x, bit):
    count = lax.axis_size("ep")
    return lax.ppermute(x, "ep", [(i, i ^ bit) for i in range(count)])


def turn(x, step):
    count = lax.axis_size("dp")
    return lax.ppermute(x, "dp", [(i, (i + step) % count) for i in range(count)])


def earlier_blocks(x):
    count = lax.axis_size("dp")
    blocks = [x]
    for hop in range(1, count):
        blocks.append(lax.ppermute(blocks[-1], "dp", [(i, i + 1) for i in range(hop - 1, count - 1)]))
    return blocks


def sum_to_owner(parts):
    count = lax.axis_size("dp")
    total = parts[count - 1]
    for k in range(count - 1, 0, -1):
        arrived = lax.ppermute(total.astype(bf16), "dp", [(i, i - 1) for i in range(k, count)])
        total = parts[k - 1] + arrived.astype(f32)
    return total


def gather_ep(x):
    half = x.shape[0] // 2
    core = flip(x, 1)
    side = flip(x, 2)
    down = flip(x, 4)
    far = [flip(down[:half], 2), flip(side[half:], 4)]
    side_core = flip(side, 1)
    down_core = flip(down, 1)
    far_core = [flip(far[0], 1), flip(far[1], 1)]
    return [[x], [core], [side], [side_core], [down], [down_core], far, far_core]


def scatter_ep(kept, sent):
    add = lambda a, b: a.astype(f32) + b.astype(f32)
    mine = add(kept, flip(sent, 1)).astype(bf16)
    half = mine.shape[1] // 2
    left, right = mine[:, :half], mine[:, half:]
    left_two = add(left[0::2], flip(left[1::2], 2)).astype(bf16)
    right_two = add(right[:2], flip(right[2:], 4)).astype(bf16)
    left_one = add(left_two[0], flip(left_two[1], 4))
    right_one = add(right_two[0], flip(right_two[1], 2))
    return jnp.concatenate([left_one, right_one], axis=0)


def gather_dp(x):
    count = lax.axis_size("dp")
    if count != 4:
        return lax.all_gather(x, "dp", axis=0, tiled=False)
    place = lax.axis_index("dp")
    width = x.shape[-1]
    half = (width // 256) * 128
    behind = turn(x, 1)
    ahead = turn(x, -1)
    across = jnp.concatenate([turn(behind[..., :half], 1), turn(ahead[..., half:], -1)], axis=-1)
    whole = jnp.zeros((count,) + x.shape, x.dtype)
    for step, block in ((0, x), (1, behind), (2, across), (3, ahead)):
        whole = lax.dynamic_update_slice(
            whole, block[None], (lax.rem(place - step + count, count),) + (0,) * x.ndim
        )
    return whole


def gather_rows(x):
    rows, width = x.shape
    here = lax.axis_index("ep")
    line = gather_dp(x)
    places = line.shape[0]
    blocks = gather_ep(line)
    whole = jnp.zeros((len(blocks), places, rows, width), x.dtype)
    for k, pieces in enumerate(blocks):
        start = 0
        for piece in pieces:
            whole = lax.dynamic_update_slice(whole, piece[None], (here ^ k, start, 0, 0))
            start += piece.shape[0]
    return whole.reshape(len(blocks) * places * rows, width)


def pick(x, index, axis):
    return lax.dynamic_index_in_dim(x, index, axis, keepdims=False)


def scatter_rows(x):
    ways, places = lax.axis_size("ep"), lax.axis_size("dp")
    rows, width = x.shape[0] // (ways * places), x.shape[1]
    here, place = lax.axis_index("ep"), lax.axis_index("dp")
    core, side, down = here & 1, (here >> 1) & 1, (here >> 2) & 1
    add = lambda a, b: a.astype(f32) + b.astype(f32)
    blocks = x.astype(bf16).reshape(2, 2, 2, places, rows, width)
    one = add(pick(blocks, core, 2), flip(pick(blocks, 1 - core, 2), 1)).astype(bf16)
    half = places // 2
    left, right = one[:, :, :half], one[:, :, half:]
    left = add(pick(left, side, 1), flip(pick(left, 1 - side, 1), 2)).astype(bf16)
    right = add(pick(right, down, 0), flip(pick(right, 1 - down, 0), 4)).astype(bf16)
    left = add(pick(left, down, 0), flip(pick(left, 1 - down, 0), 4)).astype(bf16)
    right = add(pick(right, side, 0), flip(pick(right, 1 - side, 0), 2)).astype(bf16)
    line = jnp.concatenate([left, right], axis=0)
    if places != 4:
        return lax.psum_scatter(
            line.reshape(places * rows, width), "dp", scatter_dimension=0, tiled=True
        ).astype(f32)
    cut = (width // 256) * 128
    at = lambda step: pick(line, lax.rem(place + step, places), 0)
    across = at(2)
    first = turn(across[:, :cut], 1)
    second = turn(across[:, cut:], -1)
    ahead, behind = at(1), at(3)
    ahead = jnp.concatenate([add(ahead[:, :cut], first).astype(bf16), ahead[:, cut:]], axis=1)
    behind = jnp.concatenate([behind[:, :cut], add(behind[:, cut:], second).astype(bf16)], axis=1)
    return at(0).astype(f32) + add(turn(ahead, 1), turn(behind, -1))


def spin(x, cosine, sine):
    return x * cosine + pltpu.roll(x, DH // 2, 1) * sine


def unspin(x, cosine, sine):
    return x * cosine - pltpu.roll(x, DH // 2, 1) * sine


def attend_kernel(
    x_ref, wq_ref, wk_ref, wv_ref, cos_ref, sin_ref, kpos_ref, qpos_ref, o_ref, q_ref, k_ref, v_ref
):
    rows = o_ref.shape[0]
    scale = DH ** (-0.5)
    keys = matmul(x_ref[...], wk_ref[...])
    values = matmul(x_ref[...], wv_ref[...]).astype(bf16)
    queries = matmul(x_ref[:rows], wq_ref[...])
    v_ref[...] = values
    allowed = kpos_ref[...] <= qpos_ref[...]
    for head in range(keys.shape[1] // DH):
        part = slice(head * DH, (head + 1) * DH)
        k = spin(keys[:, part], cos_ref[...], sin_ref[...]).astype(bf16)
        q = spin(queries[:, part], cos_ref[:rows], sin_ref[:rows]).astype(bf16)
        k_ref[:, part] = k
        q_ref[:, part] = q
        scores = jnp.where(allowed, times_transposed(q, k) * scale, NEG)
        top = jnp.max(scores, axis=1, keepdims=True)
        weights = jnp.exp(scores - top)
        total = jnp.sum(weights, axis=1, keepdims=True)
        attended = matmul(weights.astype(bf16), values[:, part]) / total
        o_ref[:, part] = attended.astype(bf16)


def attend(x, wq, wk, wv, cosine, sine, kpos, qpos, rows):
    length, width = x.shape
    cols = 2 * DH
    once = pl.Buffered(1)
    fixed = lambda a: pl.BlockSpec(a.shape, lambda h: (0, 0), pipeline_mode=once)
    wide = lambda r: pl.BlockSpec((r, cols), lambda h: (0, h))
    shape = lambda r: jax.ShapeDtypeStruct((r, H * DH), bf16)
    return pl.pallas_call(
        attend_kernel,
        grid=(H * DH // cols,),
        in_specs=[fixed(x), wide(width), wide(width), wide(width)]
        + [fixed(cosine), fixed(sine), fixed(kpos), fixed(qpos)],
        out_specs=[wide(rows), wide(rows), wide(length), wide(length)],
        out_shape=[shape(rows), shape(rows), shape(length), shape(length)],
        compiler_params=pltpu.CompilerParams(vmem_limit_bytes=56 << 20),
        cost_estimate=pl.CostEstimate(
            flops=2 * width * H * DH * (2 * length + rows) + 4 * rows * length * H * DH,
            bytes_accessed=2 * (3 * width * H * DH + 3 * length * width),
            transcendentals=rows * length * H,
        ),
    )(x, wq, wk, wv, cosine, sine, kpos, qpos)


def attend_back_kernel(
    q_ref, k_ref, v_ref, do_ref, cos_ref, sin_ref, kpos_ref, qpos_ref, dq_ref, dk_ref, dv_ref
):
    rows = q_ref.shape[0]
    scale = DH ** (-0.5)
    allowed = kpos_ref[...] <= qpos_ref[...]
    q, k, v, do = q_ref[...], k_ref[...], v_ref[...], do_ref[...]
    scores = jnp.where(allowed, times_transposed(k, q) * scale, NEG)
    top = jnp.max(scores, axis=0, keepdims=True)
    weights = jnp.exp(scores - top)
    weights = weights * (1.0 / jnp.sum(weights, axis=0, keepdims=True))
    weight_grad = times_transposed(v, do)
    delta = jnp.sum(weights * weight_grad, axis=0, keepdims=True)
    score_grad = (weights * (weight_grad - delta)).astype(bf16)
    dv_ref[...] = matmul(weights.astype(bf16), do).astype(bf16)
    dk = matmul(score_grad, q) * scale
    dk_ref[...] = unspin(dk, cos_ref[...], sin_ref[...]).astype(bf16)
    dq = contract_rows(score_grad, k) * scale
    dq_ref[...] = unspin(dq, cos_ref[:rows], sin_ref[:rows]).astype(bf16)


def attend_back(q, k, v, do, cosine, sine, kpos, qpos):
    rows, length = q.shape[0], k.shape[0]
    once = pl.Buffered(1)
    fixed = lambda a: pl.BlockSpec(a.shape, lambda h: (0, 0), pipeline_mode=once)
    wide = lambda r: pl.BlockSpec((r, DH), lambda h: (0, h))
    shape = lambda r: jax.ShapeDtypeStruct((r, H * DH), bf16)
    return pl.pallas_call(
        attend_back_kernel,
        grid=(H,),
        in_specs=[wide(rows), wide(length), wide(length), wide(rows)]
        + [fixed(cosine), fixed(sine), fixed(kpos), fixed(qpos)],
        out_specs=[wide(rows), wide(length), wide(length)],
        out_shape=[shape(rows), shape(length), shape(length)],
        compiler_params=pltpu.CompilerParams(vmem_limit_bytes=56 << 20),
        cost_estimate=pl.CostEstimate(
            flops=10 * rows * length * H * DH,
            bytes_accessed=2 * 4 * length * H * DH,
            transcendentals=rows * length * H,
        ),
    )(q, k, v, do, cosine, sine, kpos, qpos)


def per_device(
    tokens,
    expert_index,
    cotangent,
    gains,
    w_qkv,
    w_attn_out,
    w_router,
    w_shared_in,
    w_shared_out,
    w_expert_in,
    w_expert_out,
):
    rows, width = tokens.shape
    ways, places = lax.axis_size("ep"), lax.axis_size("dp")
    here, place = lax.axis_index("ep"), lax.axis_index("dp")
    local = w_expert_in.shape[0]
    experts = local * ways

    token_blocks = earlier_blocks(tokens)
    small = jnp.concatenate(
        [w_router.astype(bf16), gains.astype(bf16), jnp.zeros((gains.shape[0], 128 - experts - 2), bf16)],
        axis=1,
    )
    small = gather_rows(small)
    qkv_low = w_qkv.astype(bf16)
    wk = gather_rows(qkv_low[:, width : 2 * width])
    wv = gather_rows(qkv_low[:, 2 * width :])
    wq = gather_rows(qkv_low[:, :width])
    attn_weight = gather_rows(w_attn_out.astype(bf16))
    shared_in_weight = gather_rows(w_shared_in.astype(bf16))
    shared_out_weight = gather_rows(w_shared_out.astype(bf16))
    expert_in_low, expert_out_low = w_expert_in.astype(bf16), w_expert_out.astype(bf16)
    expert_in_weight, expert_out_weight = [], []
    for e in range(local):
        expert_in_weight.append(lax.all_gather(expert_in_low[e], "dp", axis=0, tiled=True))
        expert_out_weight.append(lax.all_gather(expert_out_low[e], "dp", axis=0, tiled=True))
    choose = jnp.sum(
        (expert_index[:, :, None] == jnp.arange(experts, dtype=jnp.int32)).astype(f32), axis=1
    )
    order = (0, 2, 4, 6, 1, 3, 5, 7)

    def lay(blocks):
        return jnp.concatenate([piece for k in order for piece in blocks[k]], axis=0)

    upstream_all = lay(gather_ep(cotangent))
    choose_all = lay(gather_ep(choose.astype(bf16)))

    router_weight = small[:, :experts]
    gain_attn = small[:, experts].astype(f32)
    gain_ffn = small[:, experts + 1].astype(f32)

    inputs_all = jnp.concatenate(token_blocks, axis=0).astype(f32)
    inv_first = lax.rsqrt(jnp.mean(inputs_all * inputs_all, axis=-1, keepdims=True) + EPS)
    normed_first = inputs_all * inv_first
    attn_in = (normed_first * gain_attn).astype(bf16)
    inputs = tokens.astype(f32)
    lane = jnp.arange(rows, dtype=jnp.int32)
    steps = jnp.arange(places, dtype=jnp.int32)
    positions = ((place - steps)[:, None] * rows + lane[None, :]).reshape(-1)
    key_pos = jnp.where(positions >= 0, positions, FAR)
    query_pos = place * rows + lane
    frequency = 10000.0 ** (-2.0 * jnp.arange(DH // 2, dtype=f32) / DH)
    angles = positions.astype(f32)[:, None] * frequency[None, :]
    cosine, sine = jnp.cos(angles), jnp.sin(angles)
    cosine = jnp.concatenate([cosine, cosine], axis=1)
    sine = jnp.concatenate([-sine, sine], axis=1)
    attended_low, queries, keys, values = attend(
        attn_in, wq, wk, wv, cosine, sine, key_pos[None, :], query_pos[:, None], rows
    )
    hidden = inputs + matmul(attended_low, attn_weight)
    inv_second = lax.rsqrt(jnp.mean(hidden * hidden, axis=-1, keepdims=True) + EPS)
    normed_second = hidden * inv_second
    ffn_in = (normed_second * gain_ffn).astype(bf16)

    ffn_all = lay(gather_ep(ffn_in))

    def route(rows_in):
        logits = matmul(rows_in, router_weight)
        raised = jnp.exp(logits - jnp.max(logits, axis=-1, keepdims=True))
        return raised / jnp.sum(raised, axis=-1, keepdims=True)

    router_probs = route(ffn_in)

    shared_pre = matmul(ffn_in, shared_in_weight)
    shared_gate, shared_up = shared_pre[:, :EFF], shared_pre[:, EFF:]
    shared_act = (jax.nn.silu(shared_gate) * shared_up).astype(bf16)
    shared_out = matmul(shared_act, shared_out_weight)
    shared_act_grad = times_transposed(cotangent, shared_out_weight)
    shared_pre_grad = swiglu_back(shared_gate, shared_up, shared_act_grad).astype(bf16)
    shared_out_part = scatter_rows(contract_rows(shared_act, cotangent).astype(bf16))
    shared_in_part = scatter_rows(contract_rows(ffn_in, shared_pre_grad).astype(bf16))
    shared_back = times_transposed(shared_pre_grad, shared_in_weight)

    gates_all = route(ffn_all) * choose_all.astype(f32)
    upstream_wide = upstream_all.astype(f32)
    expert_ids = jnp.arange(experts, dtype=jnp.int32)
    routed = 0.0
    back = 0.0
    gate_grads, in_parts, out_parts = [], [], []
    for e in range(local):
        gate = jnp.sum(jnp.where(expert_ids == here * local + e, gates_all, 0.0), axis=1, keepdims=True)
        pre = matmul(ffn_all, expert_in_weight[e])
        pre_gate, pre_up = pre[:, :EFF], pre[:, EFF:]
        act = (jax.nn.silu(pre_gate) * pre_up).astype(bf16)
        result = matmul(act, expert_out_weight[e]).astype(bf16).astype(f32)
        routed = routed + gate * result
        gate_grads.append(jnp.sum(upstream_wide * result, axis=-1))
        copy_grad = (gate * upstream_wide).astype(bf16)
        act_grad = times_transposed(copy_grad, expert_out_weight[e])
        pre_grad = swiglu_back(pre_gate, pre_up, act_grad).astype(bf16)
        out_parts.append(
            lax.psum_scatter(
                contract_rows(act, copy_grad).astype(bf16), "dp", scatter_dimension=0, tiled=True
            ).astype(f32)
        )
        in_parts.append(
            lax.psum_scatter(
                contract_rows(ffn_all, pre_grad).astype(bf16), "dp", scatter_dimension=0, tiled=True
            ).astype(f32)
        )
        back = back + times_transposed(pre_grad, expert_in_weight[e])
    expert_in_part = jnp.stack(in_parts, axis=0)
    expert_out_part = jnp.stack(out_parts, axis=0)

    def home(total):
        total = total.astype(bf16)
        return scatter_ep(
            total[: ways // 2 * rows].reshape(ways // 2, rows, -1),
            total[ways // 2 * rows :].reshape(ways // 2, rows, -1),
        )

    routed_in_grad = home(back)
    layer_out = (hidden + shared_out + home(routed)).astype(bf16)

    gate_grads = jnp.stack(gate_grads, axis=0).reshape(local, ways, rows)
    prob_grad = 0.0
    for slot, k in enumerate(order):
        piece = gate_grads[:, slot]
        if k:
            piece = flip(piece, k)
        for e in range(local):
            prob_grad = prob_grad + jnp.where(
                expert_ids == (here ^ k) * local + e, piece[e][:, None], 0.0
            )
    prob_grad = prob_grad * choose
    logit_grad = (
        router_probs * (prob_grad - jnp.sum(router_probs * prob_grad, axis=-1, keepdims=True))
    ).astype(bf16)
    router_grad = contract_rows(ffn_in, logit_grad)

    upstream = cotangent.astype(f32)
    ffn_in_grad = routed_in_grad + times_transposed(logit_grad, router_weight) + shared_back
    gain_ffn_grad = jnp.sum(ffn_in_grad * normed_second, axis=0)
    scaled_second = ffn_in_grad * gain_ffn
    hidden_grad = upstream + inv_second * (
        scaled_second
        - normed_second * jnp.mean(scaled_second * normed_second, axis=-1, keepdims=True)
    )
    branch_grad = hidden_grad.astype(bf16)
    attended_grad = times_transposed(branch_grad, attn_weight).astype(bf16)
    attn_out_part = scatter_rows(contract_rows(attended_low, branch_grad).astype(bf16))

    query_grad, key_grad, value_grad = attend_back(
        queries, keys, values, attended_grad, cosine, sine, key_pos[:, None], query_pos[None, :]
    )
    query_part = scatter_rows(contract_rows(attn_in[:rows], query_grad).astype(bf16))
    key_part = scatter_rows(contract_rows(attn_in, key_grad).astype(bf16))
    value_part = scatter_rows(contract_rows(attn_in, value_grad).astype(bf16))
    attn_in_grads = times_transposed(key_grad, wk) + times_transposed(value_grad, wv)
    query_back = times_transposed(query_grad, wq)
    first = attn_in_grads[:rows] + query_back
    gain_attn_grad = jnp.sum(attn_in_grads * normed_first, axis=0) + jnp.sum(
        query_back * normed_first[:rows], axis=0
    )
    attn_in_grad = sum_to_owner(
        [first] + [attn_in_grads[k * rows : (k + 1) * rows] for k in range(1, places)]
    )
    small_grad = jnp.concatenate(
        [
            router_grad,
            gain_attn_grad[:, None],
            gain_ffn_grad[:, None],
            jnp.zeros((width, 256 - experts - 2), f32),
        ],
        axis=1,
    )
    small_part = scatter_rows(small_grad.astype(bf16))
    normed_own, inv_own = normed_first[:rows], inv_first[:rows]
    scaled_first = attn_in_grad * gain_attn
    input_grad = hidden_grad + inv_own * (
        scaled_first - normed_own * jnp.mean(scaled_first * normed_own, axis=-1, keepdims=True)
    )
    return (
        layer_out,
        input_grad.astype(bf16),
        small_part[:, experts : experts + 2],
        jnp.concatenate([query_part, key_part, value_part], axis=1),
        attn_out_part,
        small_part[:, :experts],
        shared_in_part,
        shared_out_part,
        expert_in_part,
        expert_out_part,
    )


def solution(mesh):
    both = P(("ep", "dp"), None)
    cut = P("ep", "dp", None)
    return jax.shard_map(
        per_device,
        mesh=mesh,
        in_specs=(both,) * 9 + (cut,) * 2,
        out_specs=(both,) * 8 + (cut,) * 2,
        check_vma=False,
    )
```

time: 2130 us -> 963 us (0.45)
  waiting for transfers between devices: 1060 us -> 249 us
  blocking collectives: 415 us -> 0 us
  starting transfers between devices: 27.2 us -> 242 us
  local copies, waits for them, and re-layouts: 292 us -> 129 us
  Pallas kernels: 0 us -> 38.2 us
  matrix products: 237 us -> 207 us
    reduce_scatter x7 -> x4, waiting for transfers between devices: 771 us -> 0.01 us  [the longest x2 0.01 us: per_device(): lax.psum_scatter(contract_rows(act, copy_grad).astype(bf16), 'dp', scatte...]
    ppermute x0 -> x203, waiting for transfers between devices: none -> 248 us  [the longest x142 183 us: flip(): return lax.ppermute(x, 'ep', [(i, i ^ bit) for i in range(count)])]
    ppermute x0 -> x203, starting transfers between devices: none -> 242 us  [the longest x55 140 us: turn(): lax.ppermute(x, 'dp', [(i, (i + step) % count) for i in range(count)])]
    unnamed x2 -> x0, blocking collectives: 170 us -> none
    all_to_all x3 -> x0, waiting for transfers between devices: 148 us -> none  [the longest x1 93.6 us: per_device(): lax.all_to_all(send_grad, 'ep', split_axis=0, concat_axis=1, tiled=True)]
    dot_general x23 -> x9, matrix products: 197 us -> 57.6 us  [matmul(): return jnp.dot(left_side, right_side, preferred_element_type=f32)]
    all_gather x2 -> x0, blocking collectives: 139 us -> none  [the longest x1 69.8 us: per_device(): lax.all_gather(gains.astype(bf16), ('ep', 'dp'), axis=0, tiled=True)]
    all_gather x8 -> x4, waiting for transfers between devices: 131 us -> 0.04 us  [the longest x2 0.04 us: per_device(): lax.all_gather(expert_in_low[e], 'dp', axis=0, tiled=True)]
  transfers between devices with their start and end apart: 23 -> 211, of which waited for: 14 -> 90; matrix products, arithmetic and copies ran while one was open for 24% -> 40% of each run, Pallas kernels for 0% -> 4%
where the time goes in v1:
time: 963 us; the launch traced here: 953 us
  waiting for transfers between devices  249 us (26%)
  starting transfers between devices  242 us (25%)
  matrix products  207 us (21%)
  local copies, waits for them, and re-layouts  129 us (13%)
  other arithmetic  69.1 us (7%)
  Pallas kernels  38.2 us (4%)
  between operations  18.5 us (2%)
    ppermute x142, waiting for transfers between devices, flip(): return lax.ppermute(x, 'ep', [(i, i ^ bit) for i in range(count)])  183 us
    ppermute x55, starting transfers between devices, turn(): lax.ppermute(x, 'dp', [(i, (i + step) % count) for i in range(count)])  140 us
    ppermute x142, starting transfers between devices, flip(): return lax.ppermute(x, 'ep', [(i, i ^ bit) for i in range(count)])  93.5 us
    dot_general x11, matrix products, times_transposed(): lax.dot_general(left_side, right_side, (((1,), (1,)), ((), ())), preferre...  85.5 us
    dot_general x11, matrix products, contract_rows(): lax.dot_general(left_side, right_side, (((0,), (0,)), ((), ())), preferre...  64.1 us
    dot_general x9, matrix products, matmul(): return jnp.dot(left_side, right_side, preferred_element_type=f32)  57.6 us
    ppermute x55, waiting for transfers between devices, turn(): lax.ppermute(x, 'dp', [(i, (i + step) % count) for i in range(count)])  46.5 us
    unnamed x354, local copies, waits for them, and re-layouts  31.9 us
  transfers between devices with their start and end apart: 211, of which 90 were waited for; matrix products, arithmetic and copies ran while one was open for 40% of the time, Pallas kernels for 4%

profile of v1, /device:TPU:0, one launch (start us, length us, event | category | flops | bytes accessed | tf_op | source)
XLA Modules:
  0.0 953.5 jit_solution(15339679015580034124)
XLA Ops:
  79.6 9.2 collective-permute-done.82
  92.8 5.7 collective-permute-done.15
  179.8 6.9 collective-permute-done.46
  194.9 6.8 collective-permute-done.20
  209.8 5.9 collective-permute-done.61
  220.5 8.7 collective-permute-done.117
  241.6 5.7 collective-permute-done.90
  330.6 19.8 %shard_map.186 = (bf16[256,1280]{1,0:T(8,128)(2,1)}, bf16[256,1280]{1,0:T(8,128)(2,1)}, bf16[1024,1280]{1,0:T(8,128)(2,1)}, bf16[1024,1280]{1,0:T(8,128)(2,1)}) custom-call(bf16[1024,1280]{1,0:T(8,128)(2,1)} %multiply_convert_fusion.6.x_ref, bf16[1280,1280]{1,0:T(8,128)(2,1)} %bitcast.653, bf16[1280,1280]{1,0:T(8,128)(2,1)} %bitcast.675, ...), custom_call_target="tpu_custom_call" | custom-call | flops 8891924480 | bytes 17694720 | tf_op jit(solution)/shard_map/pallas_call | solution.py:201
  395.8 6.1 collective-permute-done.197
  408.7 23.5 %collective-permute-start.199 = (bf16[28,640]{1,0:T(8,128)(2,1)S(1)}, bf16[28,640]{1,0:T(8,128)(2,1)S(1)}, u32[]{:S(2)}, u32[]{:S(2)}) collective-permute-start(bf16[28,640]{1,0:T(8,128)(2,1)S(1)} %get-tuple-element.153), channel_id=1, source_target_pairs={{0,1},{1,2},{2,3},{3,0},{4,5},{5,6},{6,7},{7,4},{8,9},{9,10},{10,1... | collective-permute-start | bytes 107528 | tf_op jit(solution)/shard_map/ppermute | solution.py:51
  432.3 17.7 %collective-permute-start.201 = (bf16[28,640]{1,0:T(8,128)(2,1)S(1)}, bf16[28,640]{1,0:T(8,128)(2,1)S(1)}, u32[]{:S(2)}, u32[]{:S(2)}) collective-permute-start(bf16[28,640]{1,0:T(8,128)(2,1)S(1)} %get-tuple-element.154), channel_id=1, source_target_pairs={{0,3},{1,0},{2,1},{3,2},{4,7},{5,4},{6,5},{7,6},{8,11},{9,8},{10,9... | collective-permute-start | bytes 107528 | tf_op jit(solution)/shard_map/ppermute | solution.py:51
  454.5 10.6 %collective-permute-done.188 = bf16[2,2,40,1792]{3,2,1,0:T(8,128)(2,1)S(1)} collective-permute-done((bf16[2,2,40,1792]{3,2,1,0:T(8,128)(2,1)S(1)}, bf16[2,2,40,1792]{3,2,1,0:T(8,128)(2,1)S(1)}, u32[]{:S(2)}, u32[]{:S(2)}) %collective-permute-start.188) | collective-permute-done | bytes 573472 | tf_op jit(solution)/shard_map/ppermute | solution.py:46
  472.2 16.2 %fusion.17 = f32[2048,1792]{0,1:T(8,128)} fusion(bf16[2048,1280]{1,0:T(8,128)(2,1)} %copy-done.2, bf16[1,1280,1792]{2,1,0:T(8,128)(2,1)} %all-gather.9.cloned.1.call-done), kind=kOutput, calls=%fused_computation.50 | convolution fusion | flops 9395240960 | bytes 24510464 | tf_op jit(solution)/shard_map/dot_general | solution.py:34
  488.4 15.1 %multiply_convert_fusion.3 = (bf16[2048,896]{0,1:T(8,128)(2,1)}, bf16[2048,896]{0,1:T(8,128)(2,1)}, bf16[2048,896]{0,1:T(8,128)(2,1)S(1)}) fusion(f32[2048,1792]{0,1:T(8,128)} %fusion.17, bf16[1,896,1280]{2,1,0:T(8,128)(2,1)} %all-gather.11.cloned.1.call-done, bf16[2048,1280]{1,0:T(8,128)(2,1)} %constant_dynamic-update-slice_fusion.20, ...), kind=kOutput, calls=%fused_computation.27 | convolution fusion | flops 4733009920 | bytes 33234944 | tf_op jit(solution)/shard_map/dot_general | solution.py:28
  505.2 8.9 convolution_convert_fusion.10
  514.2 16.5 %fusion.14 = f32[2048,1792]{0,1:T(8,128)} fusion(bf16[2048,1280]{1,0:T(8,128)(2,1)} %copy-done.2, bf16[1,1280,1792]{2,1,0:T(8,128)(2,1)} %all-gather.13.cloned.1.call-done), kind=kOutput, calls=%fused_computation.47 | convolution fusion | flops 9395240960 | bytes 24510464 | tf_op jit(solution)/shard_map/dot_general | solution.py:34
  530.7 15.1 %multiply_convert_fusion.1 = (bf16[2048,896]{0,1:T(8,128)(2,1)}, bf16[2048,896]{0,1:T(8,128)(2,1)}, bf16[2048,896]{0,1:T(8,128)(2,1)S(1)}) fusion(f32[2048,1792]{0,1:T(8,128)} %fusion.14, bf16[1,896,1280]{2,1,0:T(8,128)(2,1)} %all-gather.15.cloned.1.call-done, bf16[2048,1280]{1,0:T(8,128)(2,1)} %constant_dynamic-update-slice_fusion.20, ...), kind=kOutput, calls=%fused_computation.25 | convolution fusion | flops 4733009920 | bytes 33234944 | tf_op jit(solution)/shard_map/dot_general | solution.py:28
  547.6 8.9 convolution_convert_fusion.9
  572.9 14.4 %convolution_convert_fusion.8 = bf16[1280,1792]{1,0:T(8,128)(2,1)} fusion(bf16[2048,1280]{1,0:T(8,128)(2,1)} %copy-done.2, bf16[2048,896]{0,1:T(8,128)(2,1)} %get-tuple-element.91, bf16[2048,896]{0,1:T(8,128)(2,1)S(1)} %copy-done.144), kind=kOutput, calls=%fused_computation.21 | convolution fusion | flops 9412214784 | bytes 17170432 | tf_op jit(solution)/shard_map/dot_general | solution.py:22
  587.4 15.8 %fusion.11 = f32[2048,1280]{1,0:T(8,128)} fusion(bf16[2048,896]{0,1:T(8,128)(2,1)} %get-tuple-element.91, bf16[2048,896]{0,1:T(8,128)(2,1)} %get-tuple-element.90, bf16[1,1280,1792]{2,1,0:T(8,128)(2,1)} %all-gather.9.cloned.1.call-done), kind=kOutput, calls=%fused_computation.43 | convolution fusion | flops 9409921024 | bytes 22413312 | tf_op jit(solution)/shard_map/dot_general | solution.py:28
  603.2 16.2 %add_convert_fusion = bf16[2048,1280]{1,0:T(8,128)(2,1)} fusion(f32[2048,1280]{1,0:T(8,128)} %fusion.11, bf16[2048,896]{0,1:T(8,128)(2,1)} %get-tuple-element.89, bf16[2048,896]{0,1:T(8,128)(2,1)S(1)} %copy-done.145, bf16[1,1280,1792]{2,1,0:T(8,128)(2,1)} %all-gather.13.cloned.1.call-done), kind=kOutput, calls=%fused_computation.12 | convolution fusion | flops 9415163904 | bytes 27656192 | tf_op jit(solution)/shard_map/dot_general | solution.py:28
  625.3 6.4 convolution_convert_fusion.1
  631.7 10.2 %fusion.5 = (f32[2048]{0:T(1024)S(1)}, f32[2048]{0:T(1024)S(1)}, bf16[2048,1280]{1,0:T(8,128)(2,1)}) fusion(bf16[2048,1280]{1,0:T(8,128)(2,1)S(1)} %bitcast.688, bf16[2048,1280]{1,0:T(8,128)(2,1)S(1)} %convolution_convert_fusion.1, f32[2048]{0:T(1024)S(1)} %get-tuple-element.73, f32[2048]{0:T(1024)S(1)} %copy-done.114, ...), kind=kOutput, calls=%fused_computation.11 | convolution fusion | flops 4729073664 | bytes 21725184 | tf_op jit(solution)/shard_map/dot_general | solution.py:34
  643.1 15.4 %convolution_convert_fusion.7 = bf16[1280,1792]{1,0:T(8,128)(2,1)} fusion(bf16[2048,1280]{1,0:T(8,128)(2,1)} %copy-done.2, bf16[2048,896]{0,1:T(8,128)(2,1)} %get-tuple-element.89, bf16[2048,896]{0,1:T(8,128)(2,1)} %get-tuple-element.88), kind=kOutput, calls=%fused_computation.20 | convolution fusion | flops 9412214784 | bytes 17170432 | tf_op jit(solution)/shard_map/dot_general | solution.py:22
  685.5 10.5 %collective-permute-done.126 = bf16[2,128,1280]{2,1,0:T(8,128)(2,1)S(1)} collective-permute-done((bf16[2,128,1280]{2,1,0:T(8,128)(2,1)S(1)}, bf16[2,128,1280]{2,1,0:T(8,128)(2,1)S(1)}, u32[]{:S(2)}, u32[]{:S(2)}) %collective-permute-start.126) | collective-permute-done | bytes 655392 | tf_op jit(solution)/shard_map/ppermute | solution.py:46
  701.1 8.9 collective-permute-done.112
  728.1 18.4 %shard_map.187 = (bf16[256,1280]{1,0:T(8,128)(2,1)}, bf16[1024,1280]{1,0:T(8,128)(2,1)}, bf16[1024,1280]{1,0:T(8,128)(2,1)}) custom-call(bf16[256,1280]{1,0:T(8,128)(2,1)} %get-tuple-element.18.q_ref, bf16[1024,1280]{1,0:T(8,128)(2,1)} %get-tuple-element.19.k_ref, bf16[1024,1280]{1,0:T(8,128)(2,1)} %get-tuple-element.20.v_ref, ...), custom_call_target="tpu_custom_call" | custom-call | flops 3355443200 | bytes 10485760 | tf_op jit(solution)/shard_map/pallas_call | solution.py:244
  746.5 6.9 convolution_convert_fusion.3
  753.5 5.5 fusion.187
  772.6 8.4 multiply_reduce_fusion
  823.5 18.5 %collective-permute-done.139 = bf16[256,1280]{1,0:T(8,128)(2,1)S(1)} collective-permute-done((bf16[256,1280]{1,0:T(8,128)(2,1)S(1)}, bf16[256,1280]{1,0:T(8,128)(2,1)S(1)}, u32[]{:S(2)}, u32[]{:S(2)}) %collective-permute-start.139) | collective-permute-done | bytes 655392 | tf_op jit(solution)/shard_map/ppermute | solution.py:66
  864.3 6.7 collective-permute-done.168
  (1186 shorter events, 565.5 us)
Async XLA Ops:
  7.2 465.0 %all-gather.9.cloned.1.call-start = ((), (), s32[]{:S(2)}) async-start(), calls=%async_computation.8 | async-start | bytes 5734400 | tf_op jit(solution)/shard_map/all_gather | solution.py:295
  11.4 477.0 %all-gather.11.cloned.1.call-start = ((), (), s32[]{:S(2)}) async-start(), calls=%async_computation.9 | async-start | bytes 2867200 | tf_op jit(solution)/shard_map/all_gather | solution.py:296
  13.5 500.7 %all-gather.13.cloned.1.call-start = ((), (), s32[]{:S(2)}) async-start(), calls=%async_computation.10 | async-start | bytes 5734400 | tf_op jit(solution)/shard_map/all_gather | solution.py:295
  14.3 516.4 %all-gather.15.cloned.1.call-start = ((), (), s32[]{:S(2)}) async-start(), calls=%async_computation.11 | async-start | bytes 2867200 | tf_op jit(solution)/shard_map/all_gather | solution.py:296
  14.4 75.7 %collective-permute-start.41 = (bf16[40,1280]{1,0:T(8,128)(2,1)S(1)}, bf16[40,1280]{1,0:T(8,128)(2,1)S(1)}, u32[]{:S(2)}, u32[]{:S(2)}) collective-permute-start(bf16[40,1280]{1,0:T(8,128)(2,1)S(1)} %get-tuple-element.140), channel_id=1, source_target_pairs={{0,1},{1,2},{2,3},{3,0},{4,5},{5,6},{6,7},{7,4},{8,9},{9,10},{10,1... | collective-permute-start | bytes 307208 | tf_op jit(solution)/shard_map/ppermute | solution.py:51
  17.5 102.0 %collective-permute-start.43 = (bf16[40,1280]{1,0:T(8,128)(2,1)S(1)}, bf16[40,1280]{1,0:T(8,128)(2,1)S(1)}, u32[]{:S(2)}, u32[]{:S(2)}) collective-permute-start(bf16[40,1280]{1,0:T(8,128)(2,1)S(1)} %get-tuple-element.140), channel_id=1, source_target_pairs={{0,3},{1,0},{2,1},{3,2},{4,7},{5,4},{6,5},{7,6},{8,11},{9,8},{10,9... | collective-permute-start | bytes 307208 | tf_op jit(solution)/shard_map/ppermute | solution.py:51
  20.0 38.4 %collective-permute-start.4 = (bf16[40,128]{1,0:T(8,128)(2,1)S(1)}, bf16[40,128]{1,0:T(8,128)(2,1)S(1)}, u32[]{:S(2)}, u32[]{:S(2)}) collective-permute-start(bf16[40,128]{1,0:T(8,128)(2,1)S(1)} %get-tuple-element.87), channel_id=1, source_target_pairs={{0,3},{1,0},{2,1},{3,2},{4,7},{5,4},{6,5},{7,6},{8,11},{9,8},{10,9... | collective-permute-start | bytes 30728 | tf_op jit(solution)/shard_map/ppermute | solution.py:51
  25.6 773.1 %reduce-scatter.9.cloned.1.call-start = ((), (), s32[]{:S(2)}) async-start(), calls=%async_computation.6 | async-start | bytes 2867200 | tf_op jit(solution)/shard_map/reduce_scatter | solution.py:372
  73.9 50.1 %collective-permute-start.30 = (bf16[40,1280]{1,0:T(8,128)(2,1)S(1)}, bf16[40,1280]{1,0:T(8,128)(2,1)S(1)}, u32[]{:S(2)}, u32[]{:S(2)}) collective-permute-start(bf16[40,1280]{1,0:T(8,128)(2,1)S(1)} %get-tuple-element.141), channel_id=1, source_target_pairs={{0,3},{1,0},{2,1},{3,2},{4,7},{5,4},{6,5},{7,6},{8,11},{9,8},{10,9... | collective-permute-start | bytes 307208 | tf_op jit(solution)/shard_map/ppermute | solution.py:51
  123.9 94.3 %collective-permute-start.116 = (bf16[256,1280]{1,0:T(8,128)(2,1)}, bf16[256,1280]{1,0:T(8,128)(2,1)S(1)}, u32[]{:S(2)}, u32[]{:S(2)}) collective-permute-start(bf16[256,1280]{1,0:T(8,128)(2,1)} %param.13), channel_id=1, source_target_pairs={{0,8},{4,12},{8,0},{12,4},{16,24},{20,28},{24,16},{28,20},{1,9},{5... | collective-permute-start | bytes 1966088 | tf_op jit(solution)/shard_map/ppermute | solution.py:46
  209.1 100.8 %collective-permute-start.120 = (bf16[256,1280]{1,0:T(8,128)(2,1)}, bf16[256,1280]{1,0:T(8,128)(2,1)}, u32[]{:S(2)}, u32[]{:S(2)}) collective-permute-start(bf16[256,1280]{1,0:T(8,128)(2,1)} %param.13), channel_id=1, source_target_pairs={{0,4},{4,0},{8,12},{12,8},{16,20},{20,16},{24,28},{28,24},{1,5},{5... | collective-permute-start | bytes 1966088 | tf_op jit(solution)/shard_map/ppermute | solution.py:46
  215.8 46.2 %collective-permute-start.71 = (bf16[4,40,1792]{2,1,0:T(8,128)(2,1)}, bf16[4,40,1792]{2,1,0:T(8,128)(2,1)}, u32[]{:S(2)}, u32[]{:S(2)}) collective-permute-start(bf16[4,40,1792]{2,1,0:T(8,128)(2,1)} %bitcast_dynamic-update-slice_fusion.60), channel_id=1, source_target_pairs={{0,4},{4,0},{8,12},{12,8},{16,20},{20,16},{24,28},{28,24},{1,5},{5... | collective-permute-start | bytes 1720328 | tf_op jit(solution)/shard_map/ppermute | solution.py:46
  216.5 43.0 %collective-permute-start.72 = (bf16[4,40,1792]{2,1,0:T(8,128)(2,1)}, bf16[4,40,1792]{2,1,0:T(8,128)(2,1)}, u32[]{:S(2)}, u32[]{:S(2)}) collective-permute-start(bf16[4,40,1792]{2,1,0:T(8,128)(2,1)} %bitcast_dynamic-update-slice_fusion.60), channel_id=1, source_target_pairs={{0,8},{4,12},{8,0},{12,4},{16,24},{20,28},{24,16},{28,20},{1,9},{5... | collective-permute-start | bytes 1720328 | tf_op jit(solution)/shard_map/ppermute | solution.py:46
  250.0 53.9 %collective-permute-start = (bf16[256,1280]{1,0:T(8,128)(2,1)}, bf16[256,1280]{1,0:T(8,128)(2,1)}, u32[]{:S(2)}, u32[]{:S(2)}) collective-permute-start(bf16[256,1280]{1,0:T(8,128)(2,1)} %param.11), channel_id=1, source_target_pairs={{0,1},{1,2},{2,3},{4,5},{5,6},{6,7},{8,9},{9,10},{10,11},{12,13},{... | collective-permute-start | bytes 1966088 | tf_op jit(solution)/shard_map/ppermute | solution.py:58
  372.7 79.1 %collective-permute-start.185 = (bf16[2,2,4,40,1792]{4,3,2,1,0:T(8,128)(2,1)S(1)}, bf16[2,2,4,40,1792]{4,3,2,1,0:T(8,128)(2,1)S(1)}, u32[]{:S(2)}, u32[]{:S(2)}) collective-permute-start(bf16[2,2,4,40,1792]{4,3,2,1,0:T(8,128)(2,1)S(1)} %dynamic-slice_bitcast_fusion), channel_id=1, source_target_pairs={{0,4},{4,0},{8,12},{12,8},{16,20},{20,16},{24,28},{28,24},{1,5},{5... | collective-permute-start | bytes 6881288 | tf_op jit(solution)/shard_map/ppermute | solution.py:46
  408.7 43.1 %collective-permute-start.199 = (bf16[28,640]{1,0:T(8,128)(2,1)S(1)}, bf16[28,640]{1,0:T(8,128)(2,1)S(1)}, u32[]{:S(2)}, u32[]{:S(2)}) collective-permute-start(bf16[28,640]{1,0:T(8,128)(2,1)S(1)} %get-tuple-element.153), channel_id=1, source_target_pairs={{0,1},{1,2},{2,3},{3,0},{4,5},{5,6},{6,7},{7,4},{8,9},{9,10},{10,1... | collective-permute-start | bytes 107528 | tf_op jit(solution)/shard_map/ppermute | solution.py:51
  453.2 115.8 %collective-permute-start.200 = (bf16[28,1280]{1,0:T(8,128)(2,1)S(1)}, bf16[28,1280]{1,0:T(8,128)(2,1)S(1)}, u32[]{:S(2)}, u32[]{:S(2)}) collective-permute-start(bf16[28,1280]{1,0:T(8,128)(2,1)S(1)} %pad_maximum_fusion.23), channel_id=1, source_target_pairs={{0,1},{1,2},{2,3},{3,0},{4,5},{5,6},{6,7},{7,4},{8,9},{9,10},{10,1... | collective-permute-start | bytes 215048 | tf_op jit(solution)/shard_map/ppermute | solution.py:51
  466.7 89.8 %collective-permute-start.187 = (bf16[2,40,1792]{2,1,0:T(8,128)(2,1)S(1)}, bf16[2,40,1792]{2,1,0:T(8,128)(2,1)S(1)}, u32[]{:S(2)}, u32[]{:S(2)}) collective-permute-start(bf16[2,40,1792]{2,1,0:T(8,128)(2,1)S(1)} %dynamic-slice_bitcast_fusion.19), channel_id=1, source_target_pairs={{0,16},{4,20},{8,24},{12,28},{16,0},{20,4},{24,8},{28,12},{1,17},{... | collective-permute-start | bytes 860168 | tf_op jit(solution)/shard_map/ppermute | solution.py:46
  514.1 284.6 %reduce-scatter.11.cloned.1.call-start = ((), (), s32[]{:S(2)}) async-start(), calls=%async_computation.7 | async-start | bytes 2867200 | tf_op jit(solution)/shard_map/reduce_scatter | solution.py:372
  556.5 385.7 %reduce-scatter.5.cloned.1.call-start = ((), (), s32[]{:S(2)}) async-start(), calls=%async_computation.4 | async-start | bytes 5734400 | tf_op jit(solution)/shard_map/reduce_scatter | solution.py:377
  587.3 354.8 %reduce-scatter.7.cloned.1.call-start = ((), (), s32[]{:S(2)}) async-start(), calls=%async_computation.5 | async-start | bytes 5734400 | tf_op jit(solution)/shard_map/reduce_scatter | solution.py:377
  624.8 51.0 %collective-permute-start.125 = (bf16[4,256,1280]{2,1,0:T(8,128)(2,1)}, bf16[4,256,1280]{2,1,0:T(8,128)(2,1)}, u32[]{:S(2)}, u32[]{:S(2)}) collective-permute-start(bf16[4,256,1280]{2,1,0:T(8,128)(2,1)} %bitcast.115), channel_id=1, source_target_pairs={{0,4},{4,0},{8,12},{12,8},{16,20},{20,16},{24,28},{28,24},{1,5},{5... | collective-permute-start | bytes 7864328 | tf_op jit(solution)/shard_map/ppermute | solution.py:46
  711.0 73.3 %collective-permute-start.113 = (bf16[128,1280]{1,0:T(8,128)(2,1)}, bf16[128,1280]{1,0:T(8,128)(2,1)}, u32[]{:S(2)}, u32[]{:S(2)}) collective-permute-start(bf16[128,1280]{1,0:T(8,128)(2,1)} %slice_bitcast_fusion.6), channel_id=1, source_target_pairs={{0,16},{4,20},{8,24},{12,28},{16,0},{20,4},{24,8},{28,12},{1,17},{... | collective-permute-start | bytes 983048 | tf_op jit(solution)/shard_map/ppermute | solution.py:46
  715.2 76.6 %collective-permute-start.115 = (bf16[128,1280]{1,0:T(8,128)(2,1)}, bf16[128,1280]{1,0:T(8,128)(2,1)}, u32[]{:S(2)}, u32[]{:S(2)}) collective-permute-start(bf16[128,1280]{1,0:T(8,128)(2,1)} %slice_bitcast_fusion.4), channel_id=1, source_target_pairs={{0,8},{4,12},{8,0},{12,4},{16,24},{20,28},{24,16},{28,20},{1,9},{5... | collective-permute-start | bytes 983048 | tf_op jit(solution)/shard_map/ppermute | solution.py:46
  760.2 44.4 %collective-permute-start.176 = (bf16[2,2,4,40,1280]{4,3,2,1,0:T(8,128)(2,1)}, bf16[2,2,4,40,1280]{4,3,2,1,0:T(8,128)(2,1)}, u32[]{:S(2)}, u32[]{:S(2)}) collective-permute-start(bf16[2,2,4,40,1280]{4,3,2,1,0:T(8,128)(2,1)} %dynamic-slice_bitcast_fusion.1), channel_id=1, source_target_pairs={{0,4},{4,0},{8,12},{12,8},{16,20},{20,16},{24,28},{28,24},{1,5},{5... | collective-permute-start | bytes 4915208 | tf_op jit(solution)/shard_map/ppermute | solution.py:46
  764.4 45.4 %collective-permute-start.149 = (bf16[2,2,4,40,1280]{4,3,2,1,0:T(8,128)(2,1)}, bf16[2,2,4,40,1280]{4,3,2,1,0:T(8,128)(2,1)}, u32[]{:S(2)}, u32[]{:S(2)}) collective-permute-start(bf16[2,2,4,40,1280]{4,3,2,1,0:T(8,128)(2,1)} %dynamic-slice_bitcast_fusion.4), channel_id=1, source_target_pairs={{0,4},{4,0},{8,12},{12,8},{16,20},{20,16},{24,28},{28,24},{1,5},{5... | collective-permute-start | bytes 4915208 | tf_op jit(solution)/shard_map/ppermute | solution.py:46
  771.4 42.6 %collective-permute-start.158 = (bf16[2,2,4,40,1280]{4,3,2,1,0:T(8,128)(2,1)}, bf16[2,2,4,40,1280]{4,3,2,1,0:T(8,128)(2,1)}, u32[]{:S(2)}, u32[]{:S(2)}) collective-permute-start(bf16[2,2,4,40,1280]{4,3,2,1,0:T(8,128)(2,1)} %dynamic-slice_bitcast_fusion.3), channel_id=1, source_target_pairs={{0,4},{4,0},{8,12},{12,8},{16,20},{20,16},{24,28},{28,24},{1,5},{5... | collective-permute-start | bytes 4915208 | tf_op jit(solution)/shard_map/ppermute | solution.py:46
  803.1 39.0 %collective-permute-start.139 = (bf16[256,1280]{1,0:T(8,128)(2,1)S(1)}, bf16[256,1280]{1,0:T(8,128)(2,1)S(1)}, u32[]{:S(2)}, u32[]{:S(2)}) collective-permute-start(bf16[256,1280]{1,0:T(8,128)(2,1)S(1)} %fusion.38), channel_id=1, source_target_pairs={{1,0},{2,1},{3,2},{5,4},{6,5},{7,6},{9,8},{10,9},{11,10},{13,12},{... | collective-permute-start | bytes 1966088 | tf_op jit(solution)/shard_map/ppermute | solution.py:66
  807.4 42.1 %collective-permute-start.179 = (bf16[2,2,40,1280]{3,2,1,0:T(8,128)(2,1)}, bf16[2,2,40,1280]{3,2,1,0:T(8,128)(2,1)}, u32[]{:S(2)}, u32[]{:S(2)}) collective-permute-start(bf16[2,2,40,1280]{3,2,1,0:T(8,128)(2,1)} %dynamic-slice_bitcast_fusion.7), channel_id=1, source_target_pairs={{0,16},{4,20},{8,24},{12,28},{16,0},{20,4},{24,8},{28,12},{1,17},{... | collective-permute-start | bytes 1228808 | tf_op jit(solution)/shard_map/ppermute | solution.py:46
  809.8 42.7 %collective-permute-start.177 = (bf16[2,2,40,1280]{3,2,1,0:T(8,128)(2,1)}, bf16[2,2,40,1280]{3,2,1,0:T(8,128)(2,1)}, u32[]{:S(2)}, u32[]{:S(2)}) collective-permute-start(bf16[2,2,40,1280]{3,2,1,0:T(8,128)(2,1)} %dynamic-slice_bitcast_fusion.8), channel_id=1, source_target_pairs={{0,8},{4,12},{8,0},{12,4},{16,24},{20,28},{24,16},{28,20},{1,9},{5... | collective-permute-start | bytes 1228808 | tf_op jit(solution)/shard_map/ppermute | solution.py:46
  814.0 39.7 %collective-permute-start.152 = (bf16[2,2,40,1280]{3,2,1,0:T(8,128)(2,1)}, bf16[2,2,40,1280]{3,2,1,0:T(8,128)(2,1)}, u32[]{:S(2)}, u32[]{:S(2)}) collective-permute-start(bf16[2,2,40,1280]{3,2,1,0:T(8,128)(2,1)} %dynamic-slice_bitcast_fusion.13), channel_id=1, source_target_pairs={{0,16},{4,20},{8,24},{12,28},{16,0},{20,4},{24,8},{28,12},{1,17},{... | collective-permute-start | bytes 1228808 | tf_op jit(solution)/shard_map/ppermute | solution.py:46
  855.6 39.9 %collective-permute-start.140 = (bf16[2,2,4,40,256]{4,3,2,1,0:T(8,128)(2,1)S(1)}, bf16[2,2,4,40,256]{4,3,2,1,0:T(8,128)(2,1)S(1)}, u32[]{:S(2)}, u32[]{:S(2)}) collective-permute-start(bf16[2,2,4,40,256]{4,3,2,1,0:T(8,128)(2,1)S(1)} %dynamic-slice_bitcast_fusion.17), channel_id=1, source_target_pairs={{0,4},{4,0},{8,12},{12,8},{16,20},{20,16},{24,28},{28,24},{1,5},{5... | collective-permute-start | bytes 983048 | tf_op jit(solution)/shard_map/ppermute | solution.py:46
  (340 other events, 5040.5 us)
Sparse Core Ops, SparseCore 0:
  11.5 106.6 all-gather.8
  119.7 63.2 all-gather.10
  184.6 96.3 all-gather.12
  282.4 49.9 all-gather.14
  514.2 47.7 reduce-scatter.8
  564.3 48.4 reduce-scatter.10
  615.2 82.5 reduce-scatter.4
  700.7 83.6 reduce-scatter.6

commit v2 on v1

v2 whole, which is shorter than its diff:
```python
import functools

import jax
import jax.numpy as jnp
from jax import lax
from jax.experimental import pallas as pl
from jax.experimental.pallas import tpu as pltpu
from jax.sharding import PartitionSpec as P

H = 10
DH = 128
EFF = 896
EPS = 1e-06
NEG = -1e30
FAR = 1 << 30

bf16 = jnp.bfloat16
f32 = jnp.float32


def contract_rows(left_side, right_side):
    return lax.dot_general(
        left_side, right_side, (((0,), (0,)), ((), ())), preferred_element_type=f32
    )


def times_transposed(left_side, right_side):
    return lax.dot_general(
        left_side, right_side, (((1,), (1,)), ((), ())), preferred_element_type=f32
    )


def matmul(left_side, right_side):
    return jnp.dot(left_side, right_side, preferred_element_type=f32)


def swiglu_back(gate_part, up_part, act_grad):
    sigma_gate = jax.nn.sigmoid(gate_part)
    silu_gate = gate_part * sigma_gate
    slope = sigma_gate * (1.0 + gate_part * (1.0 - sigma_gate))
    return jnp.concatenate([act_grad * up_part * slope, act_grad * silu_gate], axis=-1)


def flip(x, bit):
    count = lax.axis_size("ep")
    return lax.ppermute(x, "ep", [(i, i ^ bit) for i in range(count)])


def flip_dp(x, bit):
    count = lax.axis_size("dp")
    return lax.ppermute(x, "dp", [(i, i ^ bit) for i in range(count)])


def add(a, b):
    return a.astype(f32) + b.astype(f32)


def after(*values):
    there = iter(lax.optimization_barrier(tuple(v for v in values if v is not None)))
    return tuple(None if v is None else next(there) for v in values)


def pick(x, index, axis):
    return lax.dynamic_index_in_dim(x, index, axis, keepdims=False)


def put(whole, part, index):
    return lax.dynamic_update_slice(whole, part, (index,) + (0,) * (whole.ndim - 1))


def earlier_blocks(x):
    count = lax.axis_size("dp")
    return [x] + [
        lax.ppermute(x, "dp", [(i, i + step) for i in range(count - step)]) for step in range(1, count)
    ]


def place_bits():
    here, place = lax.axis_index("ep"), lax.axis_index("dp")
    return here & 1, (here >> 1) & 1, (here >> 2) & 1, place & 1, place >> 1


def spread_near(x):
    return [flip(x, 2), flip(x, 4)]


def spread_far(side, down):
    half = side.shape[0] // 2
    return flip(down[:half], 2), flip(side[half:], 4)


def spread_chips(x, side, down, far):
    chip = lax.axis_index("ep") >> 1
    mine = jnp.zeros((4,) + x.shape, x.dtype)
    for k, block in enumerate((x, side, down, jnp.concatenate(far, axis=0))):
        mine = put(mine, block[None], chip ^ k)
    return mine


def line_near(x):
    if lax.axis_size("dp") != 4:
        return [lax.all_gather(x, "dp", axis=0, tiled=False)]
    return [flip_dp(x, bit) for bit in (1, 2, 3)]


def line_end(x, blocks):
    if len(blocks) == 1:
        return blocks[0]
    place = lax.axis_index("dp")
    whole = jnp.zeros((4,) + x.shape, x.dtype)
    for k, block in enumerate([x] + blocks):
        whole = put(whole, block[None], place ^ k)
    return whole


def rows_whole(mine):
    other = flip(mine, 1)
    core = lax.axis_index("ep") & 1
    both = jnp.zeros((4, 2) + mine.shape[1:], mine.dtype)
    both = lax.dynamic_update_slice(both, mine[:, None], (0, core, 0, 0, 0))
    both = lax.dynamic_update_slice(both, other[:, None], (0, 1 - core, 0, 0, 0))
    return both.reshape(-1, mine.shape[-1])


def split_near(one):
    _, side, down, _, _ = place_bits()
    left, right = one[:, :, 0], one[:, :, 1]
    return [
        pick(left, side, 1),
        pick(right, down, 0),
        flip(pick(left, 1 - side, 1), 2),
        flip(pick(right, 1 - down, 0), 4),
    ]


def split_far(left, right, from_side, from_down):
    _, side, down, _, _ = place_bits()
    left = add(left, from_side).astype(bf16)
    right = add(right, from_down).astype(bf16)
    return [
        pick(left, down, 0),
        pick(right, side, 0),
        flip(pick(left, 1 - down, 0), 4),
        flip(pick(right, 1 - side, 0), 2),
    ]


def collect_near(mine, arrived):
    one = add(mine, arrived).astype(bf16)
    return split_near(one.reshape(2, 2, 2, one.shape[1] // 2, one.shape[2]))


def collect_end(left, right, from_down, from_side):
    return jnp.concatenate([add(left, from_down), add(right, from_side)], axis=0)


def rows_core(parts):
    ways, places = lax.axis_size("ep"), lax.axis_size("dp")
    core, _, _, _, _ = place_bits()
    blocks = [
        x.reshape(2, 2, 2, places, x.shape[0] // (ways * places), x.shape[1]) for x in parts
    ]
    half = lambda which: jnp.concatenate([pick(x, which, 2) for x in blocks], axis=-1)
    return half(core), flip(half(1 - core), 1)


def rows_near(kept, arrived):
    one = add(kept, arrived).astype(bf16)
    places = one.shape[2]
    return split_near(one.reshape(one.shape[:2] + (2, places // 2) + one.shape[3:]))


def rows_line(left, right, from_down, from_side):
    left = add(left, from_down).astype(bf16)
    right = add(right, from_side).astype(bf16)
    line = jnp.concatenate([left, right], axis=0)
    _, _, _, odd, _ = place_bits()
    if line.shape[0] != 4:
        rows, width = line.shape[1:]
        total = lax.psum_scatter(
            line.reshape(-1, width), "dp", scatter_dimension=0, tiled=True
        )
        return total, total
    line = line.reshape((2, 2) + line.shape[1:])
    return pick(line, odd, 1), flip_dp(pick(line, 1 - odd, 1), 1)


def rows_last(kept, arrived):
    if kept.ndim == 2:
        return kept.astype(f32), None
    _, _, _, _, upper = place_bits()
    line = add(kept, arrived).astype(bf16)
    return pick(line, upper, 0), flip_dp(pick(line, 1 - upper, 0), 2)


def rows_end(kept, arrived):
    return kept if arrived is None else add(kept, arrived)


def spin(x, cosine, sine):
    return x * cosine + pltpu.roll(x, DH // 2, 1) * sine


def unspin(x, cosine, sine):
    return x * cosine - pltpu.roll(x, DH // 2, 1) * sine


def attend_kernel(
    x_ref, wq_ref, wk_ref, wv_ref, cos_ref, sin_ref, kpos_ref, qpos_ref, o_ref, q_ref, k_ref, v_ref
):
    rows = o_ref.shape[0]
    scale = DH ** (-0.5)
    keys = matmul(x_ref[...], wk_ref[...])
    values = matmul(x_ref[...], wv_ref[...]).astype(bf16)
    queries = matmul(x_ref[:rows], wq_ref[...])
    v_ref[...] = values
    allowed = kpos_ref[...] <= qpos_ref[...]
    for head in range(keys.shape[1] // DH):
        part = slice(head * DH, (head + 1) * DH)
        k = spin(keys[:, part], cos_ref[...], sin_ref[...]).astype(bf16)
        q = spin(queries[:, part], cos_ref[:rows], sin_ref[:rows]).astype(bf16)
        k_ref[:, part] = k
        q_ref[:, part] = q
        scores = jnp.where(allowed, times_transposed(q, k) * scale, NEG)
        top = jnp.max(scores, axis=1, keepdims=True)
        weights = jnp.exp(scores - top)
        total = jnp.sum(weights, axis=1, keepdims=True)
        attended = matmul(weights.astype(bf16), values[:, part]) / total
        o_ref[:, part] = attended.astype(bf16)


def attend(x, weights, cosine, sine, kpos, qpos, rows):
    length, width = x.shape
    cols = 2 * DH
    once = pl.Buffered(1)
    fixed = lambda a: pl.BlockSpec(a.shape, lambda h: (0, 0), pipeline_mode=once)
    wide = lambda r: pl.BlockSpec((r, cols), lambda h: (0, h))
    steps = H * DH // cols
    part = lambda n: pl.BlockSpec((width, cols), lambda h, n=n: (0, h + n * steps))
    shape = lambda r: jax.ShapeDtypeStruct((r, H * DH), bf16)
    return pl.pallas_call(
        attend_kernel,
        grid=(steps,),
        in_specs=[fixed(x), part(0), part(1), part(2)]
        + [fixed(cosine), fixed(sine), fixed(kpos), fixed(qpos)],
        out_specs=[wide(rows), wide(rows), wide(length), wide(length)],
        out_shape=[shape(rows), shape(rows), shape(length), shape(length)],
        compiler_params=pltpu.CompilerParams(vmem_limit_bytes=56 << 20),
        cost_estimate=pl.CostEstimate(
            flops=2 * width * H * DH * (2 * length + rows) + 4 * rows * length * H * DH,
            bytes_accessed=2 * (3 * width * H * DH + 3 * length * width),
            transcendentals=rows * length * H,
        ),
    )(x, weights, weights, weights, cosine, sine, kpos, qpos)


def attend_back_kernel(
    q_ref, k_ref, v_ref, do_ref, cos_ref, sin_ref, kpos_ref, qpos_ref, dq_ref, dk_ref, dv_ref
):
    rows = q_ref.shape[0]
    scale = DH ** (-0.5)
    allowed = kpos_ref[...] <= qpos_ref[...]
    q, k, v, do = q_ref[...], k_ref[...], v_ref[...], do_ref[...]
    scores = jnp.where(allowed, times_transposed(k, q) * scale, NEG)
    top = jnp.max(scores, axis=0, keepdims=True)
    weights = jnp.exp(scores - top)
    weights = weights * (1.0 / jnp.sum(weights, axis=0, keepdims=True))
    weight_grad = times_transposed(v, do)
    delta = jnp.sum(weights * weight_grad, axis=0, keepdims=True)
    score_grad = (weights * (weight_grad - delta)).astype(bf16)
    dv_ref[...] = matmul(weights.astype(bf16), do).astype(bf16)
    dk = matmul(score_grad, q) * scale
    dk_ref[...] = unspin(dk, cos_ref[...], sin_ref[...]).astype(bf16)
    dq = contract_rows(score_grad, k) * scale
    dq_ref[...] = unspin(dq, cos_ref[:rows], sin_ref[:rows]).astype(bf16)


def attend_back(q, k, v, do, cosine, sine, kpos, qpos):
    rows, length = q.shape[0], k.shape[0]
    once = pl.Buffered(1)
    fixed = lambda a: pl.BlockSpec(a.shape, lambda h: (0, 0), pipeline_mode=once)
    wide = lambda r: pl.BlockSpec((r, DH), lambda h: (0, h))
    shape = lambda r: jax.ShapeDtypeStruct((r, H * DH), bf16)
    return pl.pallas_call(
        attend_back_kernel,
        grid=(H,),
        in_specs=[wide(rows), wide(length), wide(length), wide(rows)]
        + [fixed(cosine), fixed(sine), fixed(kpos), fixed(qpos)],
        out_specs=[wide(rows), wide(length), wide(length)],
        out_shape=[shape(rows), shape(length), shape(length)],
        compiler_params=pltpu.CompilerParams(vmem_limit_bytes=56 << 20),
        cost_estimate=pl.CostEstimate(
            flops=10 * rows * length * H * DH,
            bytes_accessed=2 * 4 * length * H * DH,
            transcendentals=rows * length * H,
        ),
    )(q, k, v, do, cosine, sine, kpos, qpos)


def expert_kernel(x_ref, w_ref, pre_ref, act_ref):
    gate = matmul(x_ref[...], w_ref[:, :EFF])
    up = matmul(x_ref[...], w_ref[:, EFF:])
    pre_ref[:, :EFF] = gate.astype(bf16)
    pre_ref[:, EFF:] = up.astype(bf16)
    act_ref[...] = (gate * jax.nn.sigmoid(gate) * up).astype(bf16)


def expert_forward(x, weight):
    count, width = x.shape
    step = min(512, count)
    rows = lambda n: pl.BlockSpec((step, n), lambda i: (i, 0))
    return pl.pallas_call(
        expert_kernel,
        grid=(count // step,),
        in_specs=[
            rows(width),
            pl.BlockSpec(weight.shape, lambda i: (0, 0), pipeline_mode=pl.Buffered(1)),
        ],
        out_specs=[rows(2 * EFF), rows(EFF)],
        out_shape=[
            jax.ShapeDtypeStruct((count, 2 * EFF), bf16),
            jax.ShapeDtypeStruct((count, EFF), bf16),
        ],
        compiler_params=pltpu.CompilerParams(vmem_limit_bytes=48 << 20),
        cost_estimate=pl.CostEstimate(
            flops=4 * count * width * EFF, bytes_accessed=12 << 20, transcendentals=0
        ),
    )(x, weight)


def expert_back_kernel(grad_ref, w_ref, pre_ref, out_ref):
    act_grad = times_transposed(grad_ref[...], w_ref[...])
    gate = pre_ref[:, :EFF].astype(f32)
    up = pre_ref[:, EFF:].astype(f32)
    sigma = jax.nn.sigmoid(gate)
    out_ref[:, :EFF] = (act_grad * up * (sigma * (1.0 + gate * (1.0 - sigma)))).astype(bf16)
    out_ref[:, EFF:] = (act_grad * (gate * sigma)).astype(bf16)


def expert_back(grad, weight, pre):
    count, width = grad.shape
    step = min(512, count)
    rows = lambda n: pl.BlockSpec((step, n), lambda i: (i, 0))
    return pl.pallas_call(
        expert_back_kernel,
        grid=(count // step,),
        in_specs=[
            rows(width),
            pl.BlockSpec(weight.shape, lambda i: (0, 0), pipeline_mode=pl.Buffered(1)),
            rows(2 * EFF),
        ],
        out_specs=rows(2 * EFF),
        out_shape=jax.ShapeDtypeStruct((count, 2 * EFF), bf16),
        compiler_params=pltpu.CompilerParams(vmem_limit_bytes=48 << 20),
        cost_estimate=pl.CostEstimate(
            flops=2 * count * width * EFF, bytes_accessed=12 << 20, transcendentals=0
        ),
    )(grad, weight, pre)


def widen(x, count):
    groups, rows = count
    x = x.reshape(groups, x.shape[0] // groups, x.shape[1])
    return jnp.pad(x, ((0, 0), (0, rows - x.shape[1]), (0, 0))).reshape(groups * rows, x.shape[2])


def per_device(
    tokens,
    expert_index,
    cotangent,
    gains,
    w_qkv,
    w_attn_out,
    w_router,
    w_shared_in,
    w_shared_out,
    w_expert_in,
    w_expert_out,
):
    rows, width = tokens.shape
    ways, places = lax.axis_size("ep"), lax.axis_size("dp")
    here, place = lax.axis_index("ep"), lax.axis_index("dp")
    experts = w_expert_in.shape[0] * ways
    shard = gains.shape[0]
    down_shard = w_shared_out.shape[0]
    devices = ways * places
    expert_ids = jnp.arange(experts, dtype=jnp.int32)

    local = w_expert_in.shape[0]
    first_low = jnp.concatenate(
        [
            w_qkv.astype(bf16),
            w_router.astype(bf16),
            gains.astype(bf16),
            jnp.zeros((shard, 128 - experts - 2), bf16),
        ],
        axis=1,
    )
    second_low = jnp.concatenate(
        [
            w_attn_out.astype(bf16),
            w_shared_in.astype(bf16),
            widen(w_shared_out.astype(bf16), (1, shard)),
        ],
        axis=1,
    )
    first_line = line_near(first_low)
    expert_in_low, expert_out_low, token_rows, *first_line = after(
        w_expert_in.astype(bf16), w_expert_out.astype(bf16), tokens, *first_line
    )
    token_blocks = earlier_blocks(token_rows)
    expert_weights = [
        (
            lax.all_gather(expert_in_low[e], "dp", axis=0, tiled=True),
            lax.all_gather(expert_out_low[e], "dp", axis=0, tiled=True),
        )
        for e in range(local)
    ]
    first_line = line_end(first_low, first_line)
    second_low, first_line = after(second_low, first_line)
    second_line = line_near(second_low)
    first_near = spread_near(first_line)
    first_far = spread_far(*first_near)
    first_mine = spread_chips(first_line, *first_near, first_far)
    count = len(second_line)
    first_mine, *arrived = after(first_mine, *second_line, *token_blocks)
    second_line, token_blocks = arrived[:count], arrived[count:]
    first_weights = rows_whole(first_mine)
    second_line = line_end(second_low, second_line)
    second_near = spread_near(second_line)
    choose = jnp.sum((expert_index[:, :, None] == expert_ids).astype(f32), axis=1)
    choose_rows = choose.T.astype(bf16)
    choose_near = spread_near(choose_rows)
    choose_mine = spread_chips(choose_rows, *choose_near, spread_far(*choose_near))
    chosen = jnp.concatenate([choose_mine, flip(choose_mine, 1)], axis=0)
    chosen = chosen.transpose(1, 0, 2).reshape(experts, -1).astype(f32)
    up_packed = cotangent

    router_weight = first_weights[:, 3 * width : 3 * width + experts]
    gain_attn = first_weights[:, 3 * width + experts].astype(f32)
    gain_ffn = first_weights[:, 3 * width + experts + 1].astype(f32)

    inputs_all = jnp.concatenate(token_blocks, axis=0).astype(f32)
    inv_first = lax.rsqrt(jnp.mean(inputs_all * inputs_all, axis=-1, keepdims=True) + EPS)
    normed_first = inputs_all * inv_first
    attn_in = (normed_first * gain_attn).astype(bf16)
    inputs = tokens.astype(f32)
    lane = jnp.arange(rows, dtype=jnp.int32)
    steps = jnp.arange(places, dtype=jnp.int32)
    positions = ((place - steps)[:, None] * rows + lane[None, :]).reshape(-1)
    key_pos = jnp.where(positions >= 0, positions, FAR)
    query_pos = place * rows + lane
    frequency = 10000.0 ** (-2.0 * jnp.arange(DH // 2, dtype=f32) / DH)
    angles = positions.astype(f32)[:, None] * frequency[None, :]
    cosine, sine = jnp.cos(angles), jnp.sin(angles)
    cosine = jnp.concatenate([cosine, cosine], axis=1)
    sine = jnp.concatenate([-sine, sine], axis=1)
    attended_low, queries, keys, values = attend(
        attn_in, first_weights, cosine, sine, key_pos[None, :], query_pos[:, None], rows
    )
    *second_near, attended_low = after(*second_near, attended_low)
    second_far = spread_far(*second_near)
    second_weights = rows_whole(spread_chips(second_line, *second_near, second_far))
    attn_weight = second_weights[:, :width]
    shared_in_weight = second_weights[:, width : width + 2 * EFF]
    shared_out_weight = (
        second_weights[:, width + 2 * EFF :]
        .reshape(devices, shard, width)[:, :down_shard]
        .reshape(EFF, width)
    )
    hidden = inputs + matmul(attended_low, attn_weight)
    inv_second = lax.rsqrt(jnp.mean(hidden * hidden, axis=-1, keepdims=True) + EPS)
    normed_second = hidden * inv_second
    ffn_in = (normed_second * gain_ffn).astype(bf16)

    ffn_near = spread_near(ffn_in)

    def route(rows_in):
        logits = matmul(rows_in, router_weight)
        raised = jnp.exp(logits - jnp.max(logits, axis=-1, keepdims=True))
        return raised / jnp.sum(raised, axis=-1, keepdims=True)

    router_probs = route(ffn_in)

    shared_pre = matmul(ffn_in, shared_in_weight)
    *ffn_near, shared_pre = after(*ffn_near, shared_pre)
    ffn_far = spread_far(*ffn_near)
    shared_gate, shared_up = shared_pre[:, :EFF], shared_pre[:, EFF:]
    shared_act = (jax.nn.silu(shared_gate) * shared_up).astype(bf16)
    shared_out = matmul(shared_act, shared_out_weight)
    shared_act_grad = times_transposed(cotangent, shared_out_weight)
    shared_pre_grad = swiglu_back(shared_gate, shared_up, shared_act_grad).astype(bf16)
    *ffn_far, shared_out = after(*ffn_far, shared_out)
    ffn_mine = spread_chips(ffn_in, *ffn_near, ffn_far)
    ffn_other = flip(ffn_mine, 1)
    up_packed, ffn_mine = after(up_packed, ffn_mine)
    up_near = spread_near(up_packed)

    shared_grads = jnp.concatenate(
        [
            contract_rows(ffn_in, shared_pre_grad).astype(bf16),
            widen(contract_rows(shared_act, cotangent).astype(bf16), (devices, shard)),
        ],
        axis=1,
    )
    shared_back = times_transposed(shared_pre_grad, shared_in_weight)
    *up_near, shared_grads = after(*up_near, shared_grads)
    up_far = spread_far(*up_near)
    shared_kept, shared_core = rows_core([shared_grads])

    half = ways // 2 * rows
    ffn_all = jnp.concatenate([ffn_mine, ffn_other], axis=0).reshape(-1, width)
    logits = lax.dot_general(
        router_weight, ffn_all, (((0,), (1,)), ((), ())), preferred_element_type=f32
    )
    raised = jnp.exp(logits - jnp.max(logits, axis=0, keepdims=True))
    all_probs = raised / jnp.sum(raised, axis=0, keepdims=True)

    def reduce_places(grad):
        return lax.psum_scatter(grad.astype(bf16), "dp", scatter_dimension=0, tiled=True).astype(f32)

    out_parts, in_parts, back = [], [], 0.0
    results, gate_rows = [], []
    for e in range(local):
        pre, act = expert_forward(ffn_all, expert_weights[e][0])
        if e == 0:
            *up_far, shared_core, act = after(*up_far, shared_core, act)
            shared_state = rows_near(shared_kept, shared_core)
            up_mine = spread_chips(up_packed, *up_near, up_far)
            upstream_all = jnp.concatenate([up_mine, flip(up_mine, 1)], axis=0)
            upstream_all = upstream_all.reshape(-1, width).astype(f32)
        expert = here * local + e
        gate = jnp.sum(jnp.where(expert_ids[:, None] == expert, all_probs * chosen, 0.0), axis=0)
        gate = gate[:, None]
        result = matmul(act, expert_weights[e][1]).astype(bf16)
        result_wide = result.astype(f32)
        gate_grad = jnp.sum(upstream_all * result_wide, axis=-1).reshape(ways, 1, rows)
        gate_rows.append(jnp.where(expert_ids[:, None] == expert, gate_grad, 0.0))
        results.append((gate, result))
        copy_grad = (gate * upstream_all).astype(bf16)
        if e < local - 1:
            out_grad = contract_rows(act, copy_grad).astype(bf16)
            copy_grad, out_grad = after(copy_grad, out_grad)
            out_parts.append(reduce_places(out_grad))
            pre_grad = expert_back(copy_grad, expert_weights[e][1], pre)
            if e == 0:
                *shared_state, pre_grad = after(*shared_state, pre_grad)
                shared_state = split_far(*shared_state)
            in_grad = contract_rows(ffn_all, pre_grad).astype(bf16)
            pre_grad, in_grad = after(pre_grad, in_grad)
            in_parts.append(reduce_places(in_grad))
            if e == 0:
                *shared_state, in_grad = after(*shared_state, in_grad)
                shared_line = rows_line(*shared_state)
            back = (back + times_transposed(pre_grad, expert_weights[e][0])).astype(bf16)
            back, ffn_all = after(back, ffn_all)
            continue
        sides = (slice(half, 2 * half), slice(0, half))

        def pack(side):
            rows_out = sum(g[side] * r[side].astype(f32) for g, r in results)
            blocks = slice(side.start // rows, side.stop // rows)
            grads_out = sum(g[blocks] for g in gate_rows)
            return jnp.concatenate(
                [
                    rows_out.astype(bf16).reshape(ways // 2, rows, width),
                    jnp.pad(grads_out.astype(bf16), ((0, 0), (0, 0), (0, width - rows))),
                ],
                axis=1,
            )

        def back_of(grad, side):
            total = times_transposed(grad, expert_weights[e][0]) + back[side]
            return total.astype(bf16).reshape(ways // 2, rows, width)

        packs = [pack(side) for side in sides]
        res_core = flip(packs[0], 1)
        copy_grad, packs[1], out_parts[0] = after(copy_grad, packs[1], out_parts[0])
        pre_grad = expert_back(copy_grad, expert_weights[e][1], pre)
        res_core, pre_grad = after(res_core, pre_grad)
        res_state = collect_near(packs[1], res_core)
        back_other = back_of(pre_grad[half:], sides[0])
        back_core = flip(back_other, 1)
        *res_state, pre_grad, back_other = after(*res_state, pre_grad, back_other)
        res_state = split_far(*res_state)
        back_here = back_of(pre_grad[:half], sides[1])
        back_core, back_here, pre_grad, copy_grad, *res_state = after(
            back_core, back_here, pre_grad, copy_grad, *res_state
        )
        back_state = collect_near(back_here, back_core)
        routed = collect_end(*res_state)
        out_grad = contract_rows(act, copy_grad).astype(bf16)
        *back_state, out_grad, pre_grad = after(*back_state, out_grad, pre_grad)
        back_state = split_far(*back_state)
        in_grad = contract_rows(ffn_all, pre_grad).astype(bf16)
        *back_state, in_grad, in_parts[0] = after(*back_state, in_grad, in_parts[0])
        routed_in_grad = collect_end(*back_state)
        out_parts.append(reduce_places(out_grad))
        in_parts.append(reduce_places(in_grad))
    layer_out = (hidden + shared_out + routed[:rows]).astype(bf16)
    prob_grad = routed[rows:, :rows].T * choose
    logit_grad = (
        router_probs * (prob_grad - jnp.sum(router_probs * prob_grad, axis=-1, keepdims=True))
    ).astype(bf16)
    router_grad = contract_rows(ffn_in, logit_grad)

    upstream = cotangent.astype(f32)
    ffn_in_grad = routed_in_grad + times_transposed(logit_grad, router_weight) + shared_back
    gain_ffn_grad = jnp.sum(ffn_in_grad * normed_second, axis=0)
    scaled_second = ffn_in_grad * gain_ffn
    hidden_grad = upstream + inv_second * (
        scaled_second
        - normed_second * jnp.mean(scaled_second * normed_second, axis=-1, keepdims=True)
    )
    branch_grad = hidden_grad.astype(bf16)
    attended_grad = times_transposed(branch_grad, attn_weight).astype(bf16)
    attn_out_grad = contract_rows(attended_low, branch_grad).astype(bf16)
    attn_kept, attn_core = rows_core([attn_out_grad])
    attn_core, attended_grad = after(attn_core, attended_grad)
    attn_state = rows_near(attn_kept, attn_core)
    attended_grad, attn_state[0], out_parts[-1] = after(attended_grad, attn_state[0], out_parts[-1])
    query_grad, key_grad, value_grad = attend_back(
        queries, keys, values, attended_grad, cosine, sine, key_pos[:, None], query_pos[None, :]
    )
    *attn_state, query_grad, key_grad, value_grad = after(
        *attn_state, query_grad, key_grad, value_grad
    )
    attn_state = split_far(*attn_state)
    pair_kept, pair_core = rows_core(
        [
            contract_rows(attn_in, key_grad).astype(bf16),
            contract_rows(attn_in, value_grad).astype(bf16),
        ]
    )
    *attn_state, pair_kept = after(*attn_state, pair_kept)
    attn_line = rows_line(*attn_state)
    attn_in_grads = times_transposed(key_grad, first_weights[:, width : 2 * width]) + times_transposed(
        value_grad, first_weights[:, 2 * width : 3 * width]
    )
    query_back = times_transposed(query_grad, first_weights[:, :width])
    parts = [attn_in_grads[:rows] + query_back] + [
        attn_in_grads[k * rows : (k + 1) * rows] for k in range(1, places)
    ]
    gain_attn_grad = jnp.sum(attn_in_grads * normed_first, axis=0) + jnp.sum(
        query_back * normed_first[:rows], axis=0
    )

    arrived = [
        lax.ppermute(parts[k].astype(bf16), "dp", [(i, i - k) for i in range(k, places)])
        for k in range(1, places)
    ]
    pair_core, gain_attn_grad = after(pair_core, gain_attn_grad)
    pair_state = rows_near(pair_kept, pair_core)
    small_grad = jnp.concatenate(
        [
            router_grad.astype(bf16),
            gain_attn_grad[:, None].astype(bf16),
            gain_ffn_grad[:, None].astype(bf16),
            jnp.zeros((width, 128 - experts - 2), bf16),
        ],
        axis=1,
    )
    query_kept, query_core = rows_core(
        [contract_rows(attn_in[:rows], query_grad).astype(bf16), small_grad]
    )
    query_core, *pair_state = after(query_core, *pair_state)
    query_state = rows_near(query_kept, query_core)
    pair_state = split_far(*pair_state)
    *query_state, pair_state[0], shared_kept, shared_arrived = after(
        *query_state, pair_state[0], *shared_line
    )
    shared_line = rows_last(shared_kept, shared_arrived)
    query_state = split_far(*query_state)
    *pair_state, query_state[0] = after(*pair_state, query_state[0])
    pair_line = rows_line(*pair_state)
    attn_arrived, pair_kept = after(attn_line[1], pair_line[0])
    attn_line, pair_line = (attn_line[0], attn_arrived), (pair_kept, pair_line[1])
    attn_last = rows_last(*attn_line)
    *query_state, _ = after(*query_state, pair_line[0])
    query_line = rows_line(*query_state)
    *arrived, query_kept = after(*arrived, query_line[0])
    query_line = (query_kept, query_line[1])
    attn_in_grad = parts[0] + sum(x.astype(f32) for x in arrived)
    query_line = rows_last(*query_line)
    in_parts[-1], shared_arrived, query_kept = after(in_parts[-1], shared_line[1], query_line[0])
    query_line = (query_kept, query_line[1])
    shared_part = rows_end(shared_line[0], shared_arrived).astype(f32)
    value_key_part = rows_end(*rows_last(*pair_line))
    query_part = rows_end(*query_line)
    attn_out_part = rows_end(*attn_last).astype(f32)
    normed_own, inv_own = normed_first[:rows], inv_first[:rows]
    scaled_first = attn_in_grad * gain_attn
    input_grad = hidden_grad + inv_own * (
        scaled_first - normed_own * jnp.mean(scaled_first * normed_own, axis=-1, keepdims=True)
    )
    expert_in_part = jnp.stack(in_parts, axis=0)
    expert_out_part = jnp.stack(out_parts, axis=0)
    small_part = query_part[:, width:]
    return (
        layer_out,
        input_grad.astype(bf16),
        small_part[:, experts : experts + 2],
        jnp.concatenate(
            [
                query_part[:, :width],
                value_key_part,
            ],
            axis=1,
        ),
        attn_out_part,
        small_part[:, :experts],
        shared_part[:, : 2 * EFF],
        shared_part[:down_shard, 2 * EFF :],
        expert_in_part,
        expert_out_part,
    )


def solution(mesh):
    both = P(("ep", "dp"), None)
    cut = P("ep", "dp", None)
    return jax.shard_map(
        per_device,
        mesh=mesh,
        in_specs=(both,) * 9 + (cut,) * 2,
        out_specs=(both,) * 8 + (cut,) * 2,
        check_vma=False,
    )
```

time: 963 us -> 894 us (0.928)
  starting transfers between devices: 242 us -> 130 us
  Pallas kernels: 38.2 us -> 93.2 us
  matrix products: 207 us -> 155 us
  other arithmetic: 69.1 us -> 111 us
    ppermute x142 -> x55, waiting for transfers between devices: 183 us -> 108 us  [flip(): return lax.ppermute(x, 'ep', [(i, i ^ bit) for i in range(count)])]
    ppermute x61 -> x20, starting transfers between devices: 148 us -> 81.1 us  [the longest x14 67.9 us: flip_dp(): return lax.ppermute(x, 'dp', [(i, i ^ bit) for i in range(count)])]
    pallas_call x1 -> x5, Pallas kernels: 19.8 us -> 74.8 us  [the longest x2 31.8 us: expert_forward(): pl.pallas_call(expert_kernel, grid=(count // step,), in_specs=[rows(width...]
    ppermute x142 -> x55, starting transfers between devices: 93.5 us -> 48.5 us  [flip(): return lax.ppermute(x, 'ep', [(i, i ^ bit) for i in range(count)])]
    reduce_scatter x4, waiting for transfers between devices: 0.01 us -> 44 us  [reduce_places(): lax.psum_scatter(grad.astype(bf16), 'dp', scatter_dimension=0, tiled=True)]
    ppermute x61 -> x20, waiting for transfers between devices: 65.1 us -> 102 us  [the longest x14 102 us: flip_dp(): return lax.ppermute(x, 'dp', [(i, i ^ bit) for i in range(count)])]
    dot_general x9 -> x6, matrix products: 57.6 us -> 29.7 us  [matmul(): return jnp.dot(left_side, right_side, preferred_element_type=f32)]
    dot_general x11 -> x10, matrix products: 85.5 us -> 60.3 us  [times_transposed(): lax.dot_general(left_side, right_side, (((1,), (1,)), ((), ())), preferre...]
  transfers between devices with their start and end apart: 211 -> 83, of which waited for: 90 -> 34; matrix products, arithmetic and copies ran while one was open for 40% -> 41% of each run, Pallas kernels for 4% -> 11%
where the time goes in v2:
time: 894 us; the launch traced here: 887 us
  waiting for transfers between devices  255 us (29%)
  matrix products  155 us (17%)
  starting transfers between devices  130 us (15%)
  local copies, waits for them, and re-layouts  126 us (14%)
  other arithmetic  111 us (12%)
  Pallas kernels  93.2 us (10%)
  between operations  16.6 us (2%)
    ppermute x55, waiting for transfers between devices, flip(): return lax.ppermute(x, 'ep', [(i, i ^ bit) for i in range(count)])  108 us
    ppermute x14, waiting for transfers between devices, flip_dp(): return lax.ppermute(x, 'dp', [(i, i ^ bit) for i in range(count)])  102 us
    ppermute x14, starting transfers between devices, flip_dp(): return lax.ppermute(x, 'dp', [(i, i ^ bit) for i in range(count)])  67.9 us
    dot_general x11, matrix products, contract_rows(): lax.dot_general(left_side, right_side, (((0,), (0,)), ((), ())), preferre...  62.2 us
    dot_general x10, matrix products, times_transposed(): lax.dot_general(left_side, right_side, (((1,), (1,)), ((), ())), preferre...  60.3 us
    ppermute x55, starting transfers between devices, flip(): return lax.ppermute(x, 'ep', [(i, i ^ bit) for i in range(count)])  48.5 us
    reduce_scatter x4, waiting for transfers between devices, reduce_places(): lax.psum_scatter(grad.astype(bf16), 'dp', scatter_dimension=0, tiled=True)  44 us
    pallas_call x2, Pallas kernels, expert_forward(): pl.pallas_call(expert_kernel, grid=(count // step,), in_specs=[rows(width...  31.8 us
  transfers between devices with their start and end apart: 83, of which 34 were waited for; matrix products, arithmetic and copies ran while one was open for 41% of the time, Pallas kernels for 11%

profile of v2, /device:TPU:0, one launch (start us, length us, event | category | flops | bytes accessed | tf_op | source)
XLA Modules:
  0.0 887.1 jit_solution(830416178878190914)
XLA Ops:
  23.6 18.6 %collective-permute-done.1 = bf16[40,3968]{1,0:T(8,128)(2,1)S(1)} collective-permute-done((bf16[40,3968]{1,0:T(8,128)(2,1)S(1)}, bf16[40,3968]{1,0:T(8,128)(2,1)S(1)}, u32[]{:S(2)}, u32[]{:S(2)}) %collective-permute-start.1) | collective-permute-done | bytes 317472 | tf_op jit(solution)/shard_map/ppermute | solution.py:51
  70.1 20.9 %collective-permute-done.4 = bf16[4,40,3968]{2,1,0:T(8,128)(2,1)} collective-permute-done((bf16[4,40,3968]{2,1,0:T(8,128)(2,1)}, bf16[4,40,3968]{2,1,0:T(8,128)(2,1)}, u32[]{:S(2)}, u32[]{:S(2)}) %collective-permute-start.4) | collective-permute-done | bytes 1269792 | tf_op jit(solution)/shard_map/ppermute | solution.py:46
  98.1 30.9 %collective-permute-done.9 = bf16[40,4352]{1,0:T(8,128)(2,1)} collective-permute-done((bf16[40,4352]{1,0:T(8,128)(2,1)S(1)}, bf16[40,4352]{1,0:T(8,128)(2,1)}, u32[]{:S(2)}, u32[]{:S(2)}) %collective-permute-start.9) | collective-permute-done | bytes 348192 | tf_op jit(solution)/shard_map/ppermute | solution.py:51
  132.1 38.2 %collective-permute-start.8 = (bf16[40,4352]{1,0:T(8,128)(2,1)S(1)}, bf16[40,4352]{1,0:T(8,128)(2,1)S(1)}, u32[]{:S(2)}, u32[]{:S(2)}) collective-permute-start(bf16[40,4352]{1,0:T(8,128)(2,1)S(1)} %pad_maximum_fusion.20), channel_id=1, source_target_pairs={{0,2},{1,3},{2,0},{3,1},{4,6},{5,7},{6,4},{7,5},{8,10},{9,11},{10,... | collective-permute-start | bytes 1044488 | tf_op jit(solution)/shard_map/ppermute | solution.py:51
  170.2 9.1 %collective-permute-start.7 = (bf16[40,4352]{1,0:T(8,128)(2,1)S(1)}, bf16[40,4352]{1,0:T(8,128)(2,1)S(1)}, u32[]{:S(2)}, u32[]{:S(2)}) collective-permute-start(bf16[40,4352]{1,0:T(8,128)(2,1)S(1)} %pad_maximum_fusion.20), channel_id=1, source_target_pairs={{0,1},{1,0},{2,3},{3,2},{4,5},{5,4},{6,7},{7,6},{8,9},{9,8},{10,11... | collective-permute-start | bytes 1044488 | tf_op jit(solution)/shard_map/ppermute | solution.py:51
  179.5 7.9 collective-permute-done.8
  219.7 19.6 %shard_map.186 = (bf16[256,1280]{1,0:T(8,128)(2,1)}, bf16[256,1280]{1,0:T(8,128)(2,1)}, bf16[1024,1280]{1,0:T(8,128)(2,1)}, bf16[1024,1280]{1,0:T(8,128)(2,1)}) custom-call(bf16[1024,1280]{1,0:T(8,128)(2,1)} %multiply_convert_fusion.x_ref, bf16[1280,3968]{1,0:T(8,128)(2,1)} %bitcast.360, bf16[1280,3968]{1,0:T(8,128)(2,1)} %bitcast.361, ...), custom_call_target="tpu_custom_call" | custom-call | flops 8891924480 | bytes 17694720 | tf_op jit(solution)/shard_map/pallas_call | solution.py:241
  248.2 13.4 %collective-permute-done.16 = bf16[2,40,4352]{2,1,0:T(8,128)(2,1)S(1)} collective-permute-done((bf16[2,40,4352]{2,1,0:T(8,128)(2,1)S(1)}, bf16[2,40,4352]{2,1,0:T(8,128)(2,1)S(1)}, u32[]{:S(2)}, u32[]{:S(2)}) %collective-permute-start.16) | collective-permute-done | bytes 696352 | tf_op jit(solution)/shard_map/ppermute | solution.py:46
  340.4 7.1 collective-permute-done.30
  369.9 15.8 %shard_map.187 = (bf16[2048,1792]{1,0:T(8,128)(2,1)}, bf16[2048,896]{1,0:T(8,128)(2,1)S(1)}) custom-call(bf16[2048,1280]{1,0:T(8,128)(2,1)} %bitcast.379, bf16[1280,1792]{1,0:T(8,128)(2,1)} %bitcast.425), custom_call_target="tpu_custom_call" | custom-call | flops 9395240960 | bytes 12582912 | tf_op jit(solution)/shard_map/pallas_call | solution.py:312
  411.5 11.6 %shard_map.188 = bf16[2048,1792]{1,0:T(8,128)(2,1)} custom-call(bf16[2048,1280]{1,0:T(8,128)(2,1)} %copy-done.10, bf16[896,1280]{1,0:T(8,128)(2,1)S(1)} %bitcast.357, bf16[2048,1792]{1,0:T(8,128)(2,1)} %get-tuple-element.186.pre_ref), custom_call_target="tpu_custom_call" | custom-call | flops 4697620480 | bytes 12582912 | tf_op jit(solution)/shard_map/pallas_call | solution.py:344
  423.1 15.5 %convolution_convert_fusion.9 = bf16[1280,1792]{1,0:T(8,128)(2,1)} fusion(bf16[2048,1280]{1,0:T(8,128)(2,1)} %bitcast.380, bf16[2048,1792]{1,0:T(8,128)(2,1)} %shard_map.188), kind=kOutput, calls=%fused_computation.20 | convolution fusion | flops 9397534720 | bytes 17170432 | tf_op jit(solution)/shard_map/dot_general | solution.py:22
  438.6 14.8 %convolution_convert_fusion.8 = bf16[2048,1280]{1,0:T(8,128)(2,1)} fusion(bf16[2048,1792]{1,0:T(8,128)(2,1)} %shard_map.188, bf16[1,1280,1792]{2,1,0:T(8,128)(2,1)} %all-gather.9.cloned.1.call-done), kind=kOutput, calls=%fused_computation.19 | convolution fusion | flops 9397862400 | bytes 17170432 | tf_op jit(solution)/shard_map/dot_general | solution.py:28
  453.5 15.9 %shard_map.189 = (bf16[2048,1792]{1,0:T(8,128)(2,1)}, bf16[2048,896]{1,0:T(8,128)(2,1)S(1)}) custom-call(bf16[2048,1280]{1,0:T(8,128)(2,1)} %bitcast.381, bf16[1280,1792]{1,0:T(8,128)(2,1)} %bitcast.426), custom_call_target="tpu_custom_call" | custom-call | flops 9395240960 | bytes 12582912 | tf_op jit(solution)/shard_map/pallas_call | solution.py:312
  471.3 8.1 convolution_convert_fusion
  479.4 13.4 %fusion.1 = (f32[2048]{0:T(1024)S(1)}, f32[2048]{0:T(1024)S(1)}, bf16[2048,1280]{1,0:T(8,128)(2,1)}, bf16[2048,1280]{1,0:T(8,128)(2,1)}) fusion(bf16[8,256,1280]{2,1,0:T(8,128)(2,1)} %copy-done.9, bf16[2048,1280]{1,0:T(8,128)(2,1)S(1)} %convolution_convert_fusion, f32[2048]{0:T(1024)S(1)} %get-tuple-element.294, bf16[2048,896]{1,0:T(8,128)(2,1)S(1)} %copy-done.6, ...), kind=kOutput, calls=%fused_computation.5 | convolution fusion | flops 4723830784 | bytes 26959872 | tf_op jit(solution)/shard_map/dot_general | solution.py:34
  525.4 11.9 %shard_map.190 = bf16[2048,1792]{1,0:T(8,128)(2,1)} custom-call(bf16[2048,1280]{1,0:T(8,128)(2,1)} %get-tuple-element.209.grad_ref, bf16[896,1280]{1,0:T(8,128)(2,1)S(1)} %bitcast.358, bf16[2048,1792]{1,0:T(8,128)(2,1)} %get-tuple-element.193.pre_ref), custom_call_target="tpu_custom_call" | custom-call | flops 4697620480 | bytes 12582912 | tf_op jit(solution)/shard_map/pallas_call | solution.py:344
  543.5 7.6 add_convert_fusion.4
  561.6 6.8 add_convert_fusion.3
  593.2 15.3 %convolution_convert_fusion.7 = bf16[1280,1792]{1,0:T(8,128)(2,1)} fusion(bf16[2048,1280]{1,0:T(8,128)(2,1)} %bitcast.382, bf16[2048,1792]{1,0:T(8,128)(2,1)} %shard_map.190), kind=kOutput, calls=%fused_computation.18 | convolution fusion | flops 9397534720 | bytes 17170432 | tf_op jit(solution)/shard_map/dot_general | solution.py:22
  609.0 8.6 reduce-scatter.7.cloned.1.call-done
  630.9 10.1 %collective-permute-start.63 = (bf16[2,40,3072]{2,1,0:T(8,128)(2,1)}, bf16[2,40,3072]{2,1,0:T(8,128)(2,1)}, u32[]{:S(2)}, u32[]{:S(2)}) collective-permute-start(bf16[2,40,3072]{2,1,0:T(8,128)(2,1)} %get-tuple-element.352), channel_id=1, source_target_pairs={{0,1},{1,0},{2,3},{3,2},{4,5},{5,4},{6,7},{7,6},{8,9},{9,8},{10,11... | collective-permute-start | bytes 1474568 | tf_op jit(solution)/shard_map/ppermute | solution.py:51
  651.3 32.6 %reduce-scatter.9.cloned.1.call-done = bf16[224,1280]{1,0:T(8,128)(2,1)} async-done(((bf16[896,1280]{1,0:T(8,128)(2,1)}), bf16[224,1280]{1,0:T(8,128)(2,1)}) %reduce-scatter.9.cloned.1.call-update) | async-done | bytes 573456 | tf_op jit(solution)/shard_map/reduce_scatter | solution.py:520
  686.1 18.4 %shard_map.191 = (bf16[256,1280]{1,0:T(8,128)(2,1)}, bf16[1024,1280]{1,0:T(8,128)(2,1)}, bf16[1024,1280]{1,0:T(8,128)(2,1)}) custom-call(bf16[256,1280]{1,0:T(8,128)(2,1)} %get-tuple-element.225.q_ref, bf16[1024,1280]{1,0:T(8,128)(2,1)} %get-tuple-element.226.k_ref, bf16[1024,1280]{1,0:T(8,128)(2,1)} %get-tuple-element.227.v_ref, ...), custom_call_target="tpu_custom_call" | custom-call | flops 3355443200 | bytes 10485760 | tf_op jit(solution)/shard_map/pallas_call | solution.py:284
  730.8 9.6 %multiply_reduce_fusion = (f32[1280]{0:T(1024)S(1)}, bf16[1024,1280]{1,0:T(8,128)(2,1)S(1)}, f32[1024,1280]{1,0:T(8,128)}, f32[1024,1280]{1,0:T(8,128)}) fusion(f32[1024]{0:T(1024)S(1)} %copy-done.90, bf16[256,1280]{1,0:T(8,128)(2,1)} %collective-permute-done.12, bf16[256,1280]{1,0:T(8,128)(2,1)} %collective-permute-done.11, ...), kind=kOutput, calls=%fused_computation.33 | convolution fusion | flops 3372481280 | bytes 26878976 | tf_op jit(solution)/shard_map/dot_general | solution.py:28
  763.8 17.8 %collective-permute-done.58 = bf16[2,2,40,2560]{3,2,1,0:T(8,128)(2,1)S(1)} collective-permute-done((bf16[2,2,40,2560]{3,2,1,0:T(8,128)(2,1)S(1)}, bf16[2,2,40,2560]{3,2,1,0:T(8,128)(2,1)S(1)}, u32[]{:S(2)}, u32[]{:S(2)}) %collective-permute-start.58) | collective-permute-done | bytes 819232 | tf_op jit(solution)/shard_map/ppermute | solution.py:46
  787.6 7.6 collective-permute-done.60
  796.5 8.4 collective-permute-done.64
  807.8 11.6 %collective-permute-done.68 = bf16[2,40,1280]{2,1,0:T(8,128)(2,1)S(1)} collective-permute-done((bf16[2,40,1280]{2,1,0:T(8,128)(2,1)S(1)}, bf16[2,40,1280]{2,1,0:T(8,128)(2,1)S(1)}, u32[]{:S(2)}, u32[]{:S(2)}) %collective-permute-start.68) | collective-permute-done | bytes 204832 | tf_op jit(solution)/shard_map/ppermute | solution.py:51
  823.8 9.0 %collective-permute-done.74 = bf16[40,1280]{1,0:T(8,128)(2,1)S(1)} collective-permute-done((bf16[40,1280]{1,0:T(8,128)(2,1)S(1)}, bf16[40,1280]{1,0:T(8,128)(2,1)S(1)}, u32[]{:S(2)}, u32[]{:S(2)}) %collective-permute-start.74) | collective-permute-done | bytes 102432 | tf_op jit(solution)/shard_map/ppermute | solution.py:51
  846.1 7.0 collective-permute-done.72
  867.3 9.4 %collective-permute-done.71 = bf16[40,1408]{0,1:T(8,128)(2,1)S(1)} collective-permute-done((bf16[40,1408]{0,1:T(8,128)(2,1)}, bf16[40,1408]{0,1:T(8,128)(2,1)S(1)}, u32[]{:S(2)}, u32[]{:S(2)}) %collective-permute-start.71) | collective-permute-done | bytes 112672 | tf_op jit(solution)/shard_map/ppermute | solution.py:51
  (646 shorter events, 418.2 us)
Async XLA Ops:
  7.2 362.7 %all-gather.9.cloned.1.call-start = ((), (), s32[]{:S(2)}) async-start(), calls=%async_computation.8 | async-start | bytes 5734400 | tf_op jit(solution)/shard_map/all_gather | solution.py:414
  43.9 366.0 %all-gather.11.cloned.1.call-start = ((), (), s32[]{:S(2)}) async-start(), calls=%async_computation.9 | async-start | bytes 2867200 | tf_op jit(solution)/shard_map/all_gather | solution.py:415
  52.6 138.8 %collective-permute-start.12 = (bf16[256,1280]{1,0:T(8,128)(2,1)S(1)}, bf16[256,1280]{1,0:T(8,128)(2,1)}, u32[]{:S(2)}, u32[]{:S(2)}) collective-permute-start(bf16[256,1280]{1,0:T(8,128)(2,1)S(1)} %copy-done.32), channel_id=1, source_target_pairs={{0,3},{4,7},{8,11},{12,15},{16,19},{20,23},{24,27},{28,31}} | collective-permute-start | bytes 1966088 | tf_op jit(solution)/shard_map/ppermute | solution.py:74
  57.8 133.6 %collective-permute-start.11 = (bf16[256,1280]{1,0:T(8,128)(2,1)S(1)}, bf16[256,1280]{1,0:T(8,128)(2,1)}, u32[]{:S(2)}, u32[]{:S(2)}) collective-permute-start(bf16[256,1280]{1,0:T(8,128)(2,1)S(1)} %copy-done.32), channel_id=1, source_target_pairs={{0,2},{1,3},{4,6},{5,7},{8,10},{9,11},{12,14},{13,15},{16,18},{17,... | collective-permute-start | bytes 1966088 | tf_op jit(solution)/shard_map/ppermute | solution.py:74
  63.7 30.3 %collective-permute-start.3 = (bf16[4,40,3968]{2,1,0:T(8,128)(2,1)}, bf16[4,40,3968]{2,1,0:T(8,128)(2,1)}, u32[]{:S(2)}, u32[]{:S(2)}) collective-permute-start(bf16[4,40,3968]{2,1,0:T(8,128)(2,1)} %bitcast_dynamic-update-slice_fusion.20), channel_id=1, source_target_pairs={{0,8},{4,12},{8,0},{12,4},{16,24},{20,28},{24,16},{28,20},{1,9},{5... | collective-permute-start | bytes 3809288 | tf_op jit(solution)/shard_map/ppermute | solution.py:46
  65.2 63.9 %collective-permute-start.9 = (bf16[40,4352]{1,0:T(8,128)(2,1)S(1)}, bf16[40,4352]{1,0:T(8,128)(2,1)}, u32[]{:S(2)}, u32[]{:S(2)}) collective-permute-start(bf16[40,4352]{1,0:T(8,128)(2,1)S(1)} %pad_maximum_fusion.20), channel_id=1, source_target_pairs={{0,3},{1,2},{2,1},{3,0},{4,7},{5,6},{6,5},{7,4},{8,11},{9,10},{10,... | collective-permute-start | bytes 1044488 | tf_op jit(solution)/shard_map/ppermute | solution.py:51
  66.3 387.2 %all-gather.13.cloned.1.call-start = ((), (), s32[]{:S(2)}) async-start(), calls=%async_computation.10 | async-start | bytes 5734400 | tf_op jit(solution)/shard_map/all_gather | solution.py:414
  91.0 100.4 %collective-permute-start.10 = (bf16[256,1280]{1,0:T(8,128)(2,1)S(1)}, bf16[256,1280]{1,0:T(8,128)(2,1)S(1)}, u32[]{:S(2)}, u32[]{:S(2)}) collective-permute-start(bf16[256,1280]{1,0:T(8,128)(2,1)S(1)} %copy-done.32), channel_id=1, source_target_pairs={{0,1},{1,2},{2,3},{4,5},{5,6},{6,7},{8,9},{9,10},{10,11},{12,13},{... | collective-permute-start | bytes 1966088 | tf_op jit(solution)/shard_map/ppermute | solution.py:74
  94.0 38.1 %collective-permute-start.5 = (bf16[2,40,3968]{2,1,0:T(8,128)(2,1)S(1)}, bf16[2,40,3968]{2,1,0:T(8,128)(2,1)S(1)}, u32[]{:S(2)}, u32[]{:S(2)}) collective-permute-start(bf16[2,40,3968]{2,1,0:T(8,128)(2,1)S(1)} %slice.284), channel_id=1, source_target_pairs={{0,8},{4,12},{8,0},{12,4},{16,24},{20,28},{24,16},{28,20},{1,9},{5... | collective-permute-start | bytes 1904648 | tf_op jit(solution)/shard_map/ppermute | solution.py:46
  129.1 41.2 %collective-permute-start.6 = (bf16[2,40,3968]{2,1,0:T(8,128)(2,1)S(1)}, bf16[2,40,3968]{2,1,0:T(8,128)(2,1)S(1)}, u32[]{:S(2)}, u32[]{:S(2)}) collective-permute-start(bf16[2,40,3968]{2,1,0:T(8,128)(2,1)S(1)} %slice.285), channel_id=1, source_target_pairs={{0,16},{4,20},{8,24},{12,28},{16,0},{20,4},{24,8},{28,12},{1,17},{... | collective-permute-start | bytes 1904648 | tf_op jit(solution)/shard_map/ppermute | solution.py:46
  132.1 55.3 %collective-permute-start.8 = (bf16[40,4352]{1,0:T(8,128)(2,1)S(1)}, bf16[40,4352]{1,0:T(8,128)(2,1)S(1)}, u32[]{:S(2)}, u32[]{:S(2)}) collective-permute-start(bf16[40,4352]{1,0:T(8,128)(2,1)S(1)} %pad_maximum_fusion.20), channel_id=1, source_target_pairs={{0,2},{1,3},{2,0},{3,1},{4,6},{5,7},{6,4},{7,5},{8,10},{9,11},{10,... | collective-permute-start | bytes 1044488 | tf_op jit(solution)/shard_map/ppermute | solution.py:51
  194.8 44.5 %collective-permute-start.14 = (bf16[4,40,4352]{2,1,0:T(8,128)(2,1)}, bf16[4,40,4352]{2,1,0:T(8,128)(2,1)}, u32[]{:S(2)}, u32[]{:S(2)}) collective-permute-start(bf16[4,40,4352]{2,1,0:T(8,128)(2,1)} %bitcast_dynamic-update-slice_fusion.16), channel_id=1, source_target_pairs={{0,16},{4,20},{8,24},{12,28},{16,0},{20,4},{24,8},{28,12},{1,17},{... | collective-permute-start | bytes 4177928 | tf_op jit(solution)/shard_map/ppermute | solution.py:46
  196.6 42.8 %collective-permute-start.13 = (bf16[4,40,4352]{2,1,0:T(8,128)(2,1)}, bf16[4,40,4352]{2,1,0:T(8,128)(2,1)}, u32[]{:S(2)}, u32[]{:S(2)}) collective-permute-start(bf16[4,40,4352]{2,1,0:T(8,128)(2,1)} %bitcast_dynamic-update-slice_fusion.16), channel_id=1, source_target_pairs={{0,8},{4,12},{8,0},{12,4},{16,24},{20,28},{24,16},{28,20},{1,9},{5... | collective-permute-start | bytes 4177928 | tf_op jit(solution)/shard_map/ppermute | solution.py:46
  263.3 207.9 %all-gather.15.cloned.1.call-start = ((), (), s32[]{:S(2)}) async-start(), calls=%async_computation.11 | async-start | bytes 2867200 | tf_op jit(solution)/shard_map/all_gather | solution.py:415
  291.0 232.3 %reduce-scatter.5.cloned.1.call-start = ((), (), s32[]{:S(2)}) async-start(), calls=%async_computation.4 | async-start | bytes 2867200 | tf_op jit(solution)/shard_map/reduce_scatter | solution.py:520
  333.8 30.2 %collective-permute-start.23 = (bf16[4,256,1280]{2,1,0:T(8,128)(2,1)}, bf16[4,256,1280]{2,1,0:T(8,128)(2,1)}, u32[]{:S(2)}, u32[]{:S(2)}) collective-permute-start(bf16[4,256,1280]{2,1,0:T(8,128)(2,1)} %fusion.41), channel_id=1, source_target_pairs={{0,4},{4,0},{8,12},{12,8},{16,20},{20,16},{24,28},{28,24},{1,5},{5... | collective-permute-start | bytes 7864328 | tf_op jit(solution)/shard_map/ppermute | solution.py:46
  353.0 32.8 %collective-permute-start.33 = (bf16[2,2,4,40,3072]{4,3,2,1,0:T(8,128)(2,1)}, bf16[2,2,4,40,3072]{4,3,2,1,0:T(8,128)(2,1)}, u32[]{:S(2)}, u32[]{:S(2)}) collective-permute-start(bf16[2,2,4,40,3072]{4,3,2,1,0:T(8,128)(2,1)} %dynamic-slice_bitcast_fusion), channel_id=1, source_target_pairs={{0,4},{4,0},{8,12},{12,8},{16,20},{20,16},{24,28},{28,24},{1,5},{5... | collective-permute-start | bytes 11796488 | tf_op jit(solution)/shard_map/ppermute | solution.py:46
  393.2 29.9 %collective-permute-start.35 = (bf16[2,2,40,3072]{3,2,1,0:T(8,128)(2,1)}, bf16[2,2,40,3072]{3,2,1,0:T(8,128)(2,1)}, u32[]{:S(2)}, u32[]{:S(2)}) collective-permute-start(bf16[2,2,40,3072]{3,2,1,0:T(8,128)(2,1)} %get-tuple-element.327), channel_id=1, source_target_pairs={{0,16},{4,20},{8,24},{12,28},{16,0},{20,4},{24,8},{28,12},{1,17},{... | collective-permute-start | bytes 2949128 | tf_op jit(solution)/shard_map/ppermute | solution.py:46
  453.4 164.2 %reduce-scatter.7.cloned.1.call-start = ((), (), s32[]{:S(2)}) async-start(), calls=%async_computation.5 | async-start | bytes 5734400 | tf_op jit(solution)/shard_map/reduce_scatter | solution.py:520
  499.9 37.4 %collective-permute-start.37 = (bf16[4,272,1280]{2,1,0:T(8,128)(2,1)}, bf16[4,272,1280]{2,1,0:T(8,128)(2,1)}, u32[]{:S(2)}, u32[]{:S(2)}) collective-permute-start(bf16[4,272,1280]{2,1,0:T(8,128)(2,1)} %fusion.28), channel_id=1, source_target_pairs={{0,4},{4,0},{8,12},{12,8},{16,20},{20,16},{24,28},{28,24},{1,5},{5... | collective-permute-start | bytes 8355848 | tf_op jit(solution)/shard_map/ppermute | solution.py:46
  511.6 172.3 %reduce-scatter.9.cloned.1.call-start = ((), (), s32[]{:S(2)}) async-start(), calls=%async_computation.6 | async-start | bytes 2867200 | tf_op jit(solution)/shard_map/reduce_scatter | solution.py:520
  589.5 31.1 %collective-permute-start.45 = (bf16[128,1280]{1,0:T(8,128)(2,1)}, bf16[128,1280]{1,0:T(8,128)(2,1)}, u32[]{:S(2)}, u32[]{:S(2)}) collective-permute-start(bf16[128,1280]{1,0:T(8,128)(2,1)} %get-tuple-element.378), channel_id=1, source_target_pairs={{0,16},{4,20},{8,24},{12,28},{16,0},{20,4},{24,8},{28,12},{1,17},{... | collective-permute-start | bytes 983048 | tf_op jit(solution)/shard_map/ppermute | solution.py:46
  608.5 234.8 %reduce-scatter.11.cloned.1.call-start = ((), (), s32[]{:S(2)}) async-start(), calls=%async_computation.7 | async-start | bytes 5734400 | tf_op jit(solution)/shard_map/reduce_scatter | solution.py:520
  630.9 154.6 %collective-permute-start.63 = (bf16[2,40,3072]{2,1,0:T(8,128)(2,1)}, bf16[2,40,3072]{2,1,0:T(8,128)(2,1)}, u32[]{:S(2)}, u32[]{:S(2)}) collective-permute-start(bf16[2,40,3072]{2,1,0:T(8,128)(2,1)} %get-tuple-element.352), channel_id=1, source_target_pairs={{0,1},{1,0},{2,3},{3,2},{4,5},{5,4},{6,7},{7,6},{8,9},{9,8},{10,11... | collective-permute-start | bytes 1474568 | tf_op jit(solution)/shard_map/ppermute | solution.py:51
  645.5 58.9 %collective-permute-start.49 = (bf16[2,2,40,1280]{3,2,1,0:T(8,128)(2,1)S(1)}, bf16[2,2,40,1280]{3,2,1,0:T(8,128)(2,1)S(1)}, u32[]{:S(2)}, u32[]{:S(2)}) collective-permute-start(bf16[2,2,40,1280]{3,2,1,0:T(8,128)(2,1)S(1)} %get-tuple-element.368), channel_id=1, source_target_pairs={{0,16},{4,20},{8,24},{12,28},{16,0},{20,4},{24,8},{28,12},{1,17},{... | collective-permute-start | bytes 1228808 | tf_op jit(solution)/shard_map/ppermute | solution.py:46
  647.7 56.7 %collective-permute-start.48 = (bf16[2,2,40,1280]{3,2,1,0:T(8,128)(2,1)S(1)}, bf16[2,2,40,1280]{3,2,1,0:T(8,128)(2,1)S(1)}, u32[]{:S(2)}, u32[]{:S(2)}) collective-permute-start(bf16[2,2,40,1280]{3,2,1,0:T(8,128)(2,1)S(1)} %get-tuple-element.370), channel_id=1, source_target_pairs={{0,8},{4,12},{8,0},{12,4},{16,24},{20,28},{24,16},{28,20},{1,9},{5... | collective-permute-start | bytes 1228808 | tf_op jit(solution)/shard_map/ppermute | solution.py:46
  717.6 35.3 %collective-permute-start.56 = (bf16[2,40,1280]{2,1,0:T(8,128)(2,1)}, bf16[2,40,1280]{2,1,0:T(8,128)(2,1)}, u32[]{:S(2)}, u32[]{:S(2)}) collective-permute-start(bf16[2,40,1280]{2,1,0:T(8,128)(2,1)} %get-tuple-element.386), channel_id=1, source_target_pairs={{0,8},{4,12},{8,0},{12,4},{16,24},{20,28},{24,16},{28,20},{1,9},{5... | collective-permute-start | bytes 614408 | tf_op jit(solution)/shard_map/ppermute | solution.py:46
  719.8 33.1 %collective-permute-start.55 = (bf16[2,40,1280]{2,1,0:T(8,128)(2,1)}, bf16[2,40,1280]{2,1,0:T(8,128)(2,1)}, u32[]{:S(2)}, u32[]{:S(2)}) collective-permute-start(bf16[2,40,1280]{2,1,0:T(8,128)(2,1)} %get-tuple-element.388), channel_id=1, source_target_pairs={{0,16},{4,20},{8,24},{12,28},{16,0},{20,4},{24,8},{28,12},{1,17},{... | collective-permute-start | bytes 614408 | tf_op jit(solution)/shard_map/ppermute | solution.py:46
  741.7 98.0 %collective-permute-start.52 = (bf16[256,1280]{1,0:T(8,128)(2,1)}, bf16[256,1280]{1,0:T(8,128)(2,1)}, u32[]{:S(2)}, u32[]{:S(2)}) collective-permute-start(bf16[256,1280]{1,0:T(8,128)(2,1)} %get-tuple-element.320), channel_id=1, source_target_pairs={{3,0},{7,4},{11,8},{15,12},{19,16},{23,20},{27,24},{31,28}} | collective-permute-start | bytes 1966088 | tf_op jit(solution)/shard_map/ppermute | solution.py:649
  781.6 58.1 %collective-permute-start.51 = (bf16[256,1280]{1,0:T(8,128)(2,1)S(1)}, bf16[256,1280]{1,0:T(8,128)(2,1)S(1)}, u32[]{:S(2)}, u32[]{:S(2)}) collective-permute-start(bf16[256,1280]{1,0:T(8,128)(2,1)S(1)} %copy-done.53), channel_id=1, source_target_pairs={{2,0},{3,1},{6,4},{7,5},{10,8},{11,9},{14,12},{15,13},{18,16},{19,... | collective-permute-start | bytes 1966088 | tf_op jit(solution)/shard_map/ppermute | solution.py:649
  786.3 53.4 %collective-permute-start.50 = (bf16[256,1280]{1,0:T(8,128)(2,1)S(1)}, bf16[256,1280]{1,0:T(8,128)(2,1)S(1)}, u32[]{:S(2)}, u32[]{:S(2)}) collective-permute-start(bf16[256,1280]{1,0:T(8,128)(2,1)S(1)} %copy-done.52), channel_id=1, source_target_pairs={{1,0},{2,1},{3,2},{5,4},{6,5},{7,6},{9,8},{10,9},{11,10},{13,12},{... | collective-permute-start | bytes 1966088 | tf_op jit(solution)/shard_map/ppermute | solution.py:649
  805.4 28.8 %collective-permute-start.66 = (bf16[2,40,1408]{2,1,0:T(8,128)(2,1)S(1)}, bf16[2,40,1408]{2,1,0:T(8,128)(2,1)S(1)}, u32[]{:S(2)}, u32[]{:S(2)}) collective-permute-start(bf16[2,40,1408]{2,1,0:T(8,128)(2,1)S(1)} %get-tuple-element.384), channel_id=1, source_target_pairs={{0,16},{4,20},{8,24},{12,28},{16,0},{20,4},{24,8},{28,12},{1,17},{... | collective-permute-start | bytes 675848 | tf_op jit(solution)/shard_map/ppermute | solution.py:46
  (165 other events, 1894.2 us)
Sparse Core Ops, SparseCore 0:
  43.9 139.5 all-gather.8
  185.7 74.3 all-gather.10
  263.4 109.6 all-gather.12
  375.2 47.8 all-gather.14
  453.5 69.6 reduce-scatter.4
  525.5 92.0 reduce-scatter.6
  620.6 63.2 reduce-scatter.8
  686.8 96.6 reduce-scatter.10

commit v3 on v2

--- a/solution.py
+++ b/solution.py
@@ -405,17 +405,8 @@
         axis=1,
     )
     first_line = line_near(first_low)
-    expert_in_low, expert_out_low, token_rows, *first_line = after(
-        w_expert_in.astype(bf16), w_expert_out.astype(bf16), tokens, *first_line
-    )
+    token_rows, *first_line = after(tokens, *first_line)
     token_blocks = earlier_blocks(token_rows)
-    expert_weights = [
-        (
-            lax.all_gather(expert_in_low[e], "dp", axis=0, tiled=True),
-            lax.all_gather(expert_out_low[e], "dp", axis=0, tiled=True),
-        )
-        for e in range(local)
-    ]
     first_line = line_end(first_low, first_line)
     second_low, first_line = after(second_low, first_line)
     second_line = line_near(second_low)
@@ -423,8 +414,17 @@
     first_far = spread_far(*first_near)
     first_mine = spread_chips(first_line, *first_near, first_far)
     count = len(second_line)
-    first_mine, *arrived = after(first_mine, *second_line, *token_blocks)
+    first_mine, expert_in_low, expert_out_low, *arrived = after(
+        first_mine, w_expert_in.astype(bf16), w_expert_out.astype(bf16), *second_line, *token_blocks
+    )
     second_line, token_blocks = arrived[:count], arrived[count:]
+    expert_weights = [
+        [
+            lax.all_gather(expert_in_low[e], "dp", axis=0, tiled=True),
+            lax.all_gather(expert_out_low[e], "dp", axis=0, tiled=True),
+        ]
+        for e in range(local)
+    ]
     first_weights = rows_whole(first_mine)
     second_line = line_end(second_low, second_line)
     second_near = spread_near(second_line)
@@ -473,6 +473,7 @@
     normed_second = hidden * inv_second
     ffn_in = (normed_second * gain_ffn).astype(bf16)
 
+    ffn_in, expert_weights[0][0] = after(ffn_in, expert_weights[0][0])
     ffn_near = spread_near(ffn_in)
 
     def route(rows_in):
@@ -493,7 +494,7 @@
     *ffn_far, shared_out = after(*ffn_far, shared_out)
     ffn_mine = spread_chips(ffn_in, *ffn_near, ffn_far)
     ffn_other = flip(ffn_mine, 1)
-    up_packed, ffn_mine = after(up_packed, ffn_mine)
+    up_packed, ffn_mine, expert_weights[0][1] = after(up_packed, ffn_mine, expert_weights[0][1])
     up_near = spread_near(up_packed)
 
     shared_grads = jnp.concatenate(
@@ -544,7 +545,9 @@
             out_parts.append(reduce_places(out_grad))
             pre_grad = expert_back(copy_grad, expert_weights[e][1], pre)
             if e == 0:
-                *shared_state, pre_grad = after(*shared_state, pre_grad)
+                *shared_state, pre_grad, expert_weights[1][0] = after(
+                    *shared_state, pre_grad, expert_weights[1][0]
+                )
                 shared_state = split_far(*shared_state)
             in_grad = contract_rows(ffn_all, pre_grad).astype(bf16)
             pre_grad, in_grad = after(pre_grad, in_grad)
@@ -553,7 +556,7 @@
                 *shared_state, in_grad = after(*shared_state, in_grad)
                 shared_line = rows_line(*shared_state)
             back = (back + times_transposed(pre_grad, expert_weights[e][0])).astype(bf16)
-            back, ffn_all = after(back, ffn_all)
+            back, ffn_all, expert_weights[e + 1][1] = after(back, ffn_all, expert_weights[e + 1][1])
             continue
         sides = (slice(half, 2 * half), slice(0, half))
 
@@ -618,7 +621,7 @@
     attn_kept, attn_core = rows_core([attn_out_grad])
     attn_core, attended_grad = after(attn_core, attended_grad)
     attn_state = rows_near(attn_kept, attn_core)
-    attended_grad, attn_state[0], out_parts[-1] = after(attended_grad, attn_state[0], out_parts[-1])
+    attended_grad, attn_state[0] = after(attended_grad, attn_state[0])
     query_grad, key_grad, value_grad = attend_back(
         queries, keys, values, attended_grad, cosine, sine, key_pos[:, None], query_pos[None, :]
     )
@@ -649,7 +652,7 @@
         lax.ppermute(parts[k].astype(bf16), "dp", [(i, i - k) for i in range(k, places)])
         for k in range(1, places)
     ]
-    pair_core, gain_attn_grad = after(pair_core, gain_attn_grad)
+    pair_core, gain_attn_grad, out_parts[-1] = after(pair_core, gain_attn_grad, out_parts[-1])
     pair_state = rows_near(pair_kept, pair_core)
     small_grad = jnp.concatenate(
         [

time: 894 us -> 848 us (0.949)
  waiting for transfers between devices: 255 us -> 235 us
  starting transfers between devices: 130 us -> 111 us
    reduce_scatter x4, waiting for transfers between devices: 44 us -> 0.02 us  [reduce_places(): lax.psum_scatter(grad.astype(bf16), 'dp', scatter_dimension=0, tiled=True)]
    ppermute x14, waiting for transfers between devices: 102 us -> 130 us  [flip_dp(): return lax.ppermute(x, 'dp', [(i, i ^ bit) for i in range(count)])]
    ppermute x55, waiting for transfers between devices: 108 us -> 87.4 us  [flip(): return lax.ppermute(x, 'ep', [(i, i ^ bit) for i in range(count)])]
    ppermute x14, starting transfers between devices: 67.9 us -> 49.4 us  [flip_dp(): return lax.ppermute(x, 'dp', [(i, i ^ bit) for i in range(count)])]
    all_gather x2, waiting for transfers between devices: 0.01 us -> 17.8 us  [per_device(): lax.all_gather(expert_out_low[e], 'dp', axis=0, tiled=True)]
    unnamed x230 -> x240, local copies, waits for them, and re-layouts: 21.3 us -> 17.8 us
    dynamic_update_slice x23 -> x24, local copies, waits for them, and re-layouts: 27.3 us -> 24.7 us  [put(): lax.dynamic_update_slice(whole, part, (index,) + (0,) * (whole.ndim - 1))]
where the time goes in v3:
time: 848 us; the launch traced here: 841 us
  waiting for transfers between devices  235 us (28%)
  matrix products  153 us (18%)
  local copies, waits for them, and re-layouts  120 us (14%)
  starting transfers between devices  111 us (13%)
  other arithmetic  111 us (13%)
  Pallas kernels  93.7 us (11%)
  between operations  16.8 us (2%)
    ppermute x14, waiting for transfers between devices, flip_dp(): return lax.ppermute(x, 'dp', [(i, i ^ bit) for i in range(count)])  130 us
    ppermute x55, waiting for transfers between devices, flip(): return lax.ppermute(x, 'ep', [(i, i ^ bit) for i in range(count)])  87.4 us
    dot_general x11, matrix products, contract_rows(): lax.dot_general(left_side, right_side, (((0,), (0,)), ((), ())), preferre...  62.7 us
    dot_general x10, matrix products, times_transposed(): lax.dot_general(left_side, right_side, (((1,), (1,)), ((), ())), preferre...  59.8 us
    ppermute x14, starting transfers between devices, flip_dp(): return lax.ppermute(x, 'dp', [(i, i ^ bit) for i in range(count)])  49.4 us
    ppermute x55, starting transfers between devices, flip(): return lax.ppermute(x, 'ep', [(i, i ^ bit) for i in range(count)])  47.8 us
    pallas_call x2, Pallas kernels, expert_forward(): pl.pallas_call(expert_kernel, grid=(count // step,), in_specs=[rows(width...  31.9 us
    dot_general x6, matrix products, matmul(): return jnp.dot(left_side, right_side, preferred_element_type=f32)  28.2 us
  transfers between devices with their start and end apart: 83, of which 34 were waited for; matrix products, arithmetic and copies ran while one was open for 41% of the time, Pallas kernels for 11%

profile of v3, /device:TPU:0, one launch (start us, length us, event | category | flops | bytes accessed | tf_op | source)
XLA Modules:
  0.0 840.7 jit_solution(4895502082957965822)
XLA Ops:
  23.6 18.7 %collective-permute-done.1 = bf16[40,3968]{1,0:T(8,128)(2,1)} collective-permute-done((bf16[40,3968]{1,0:T(8,128)(2,1)S(1)}, bf16[40,3968]{1,0:T(8,128)(2,1)}, u32[]{:S(2)}, u32[]{:S(2)}) %collective-permute-start.1) | collective-permute-done | bytes 317472 | tf_op jit(solution)/shard_map/ppermute | solution.py:51
  65.6 10.2 %collective-permute-done.4 = bf16[4,40,3968]{2,1,0:T(8,128)(2,1)} collective-permute-done((bf16[4,40,3968]{2,1,0:T(8,128)(2,1)}, bf16[4,40,3968]{2,1,0:T(8,128)(2,1)}, u32[]{:S(2)}, u32[]{:S(2)}) %collective-permute-start.4) | collective-permute-done | bytes 1269792 | tf_op jit(solution)/shard_map/ppermute | solution.py:46
  84.3 20.8 %collective-permute-done.9 = bf16[40,4352]{1,0:T(8,128)(2,1)} collective-permute-done((bf16[40,4352]{1,0:T(8,128)(2,1)S(1)}, bf16[40,4352]{1,0:T(8,128)(2,1)}, u32[]{:S(2)}, u32[]{:S(2)}) %collective-permute-start.9) | collective-permute-done | bytes 348192 | tf_op jit(solution)/shard_map/ppermute | solution.py:51
  108.1 24.9 %collective-permute-start.8 = (bf16[40,4352]{1,0:T(8,128)(2,1)S(1)}, bf16[40,4352]{1,0:T(8,128)(2,1)S(1)}, u32[]{:S(2)}, u32[]{:S(2)}) collective-permute-start(bf16[40,4352]{1,0:T(8,128)(2,1)S(1)} %copy-done.56), channel_id=1, source_target_pairs={{0,2},{1,3},{2,0},{3,1},{4,6},{5,7},{6,4},{7,5},{8,10},{9,11},{10,... | collective-permute-start | bytes 1044488 | tf_op jit(solution)/shard_map/ppermute | solution.py:51
  133.0 11.2 %collective-permute-start.7 = (bf16[40,4352]{1,0:T(8,128)(2,1)S(1)}, bf16[40,4352]{1,0:T(8,128)(2,1)S(1)}, u32[]{:S(2)}, u32[]{:S(2)}) collective-permute-start(bf16[40,4352]{1,0:T(8,128)(2,1)S(1)} %copy-done.56), channel_id=1, source_target_pairs={{0,1},{1,0},{2,3},{3,2},{4,5},{5,4},{6,7},{7,6},{8,9},{9,8},{10,11... | collective-permute-start | bytes 1044488 | tf_op jit(solution)/shard_map/ppermute | solution.py:51
  148.6 7.4 collective-permute-done.7
  187.0 6.0 multiply_convert_fusion.x_ref
  193.0 19.6 %shard_map.186 = (bf16[256,1280]{1,0:T(8,128)(2,1)}, bf16[256,1280]{1,0:T(8,128)(2,1)}, bf16[1024,1280]{1,0:T(8,128)(2,1)}, bf16[1024,1280]{1,0:T(8,128)(2,1)}) custom-call(bf16[1024,1280]{1,0:T(8,128)(2,1)} %multiply_convert_fusion.x_ref, bf16[1280,3968]{1,0:T(8,128)(2,1)} %bitcast.355, bf16[1280,3968]{1,0:T(8,128)(2,1)} %bitcast.356, ...), custom_call_target="tpu_custom_call" | custom-call | flops 8891924480 | bytes 17694720 | tf_op jit(solution)/shard_map/pallas_call | solution.py:241
  219.7 11.6 %collective-permute-done.16 = bf16[2,40,4352]{2,1,0:T(8,128)(2,1)S(1)} collective-permute-done((bf16[2,40,4352]{2,1,0:T(8,128)(2,1)S(1)}, bf16[2,40,4352]{2,1,0:T(8,128)(2,1)S(1)}, u32[]{:S(2)}, u32[]{:S(2)}) %collective-permute-start.16) | collective-permute-done | bytes 696352 | tf_op jit(solution)/shard_map/ppermute | solution.py:46
  301.8 7.8 pad_maximum_fusion
  330.7 16.1 %shard_map.187 = (bf16[2048,1792]{1,0:T(8,128)(2,1)}, bf16[2048,896]{1,0:T(8,128)(2,1)S(1)}) custom-call(bf16[2048,1280]{1,0:T(8,128)(2,1)} %bitcast.374, bf16[1280,1792]{1,0:T(8,128)(2,1)} %bitcast.425), custom_call_target="tpu_custom_call" | custom-call | flops 9395240960 | bytes 12582912 | tf_op jit(solution)/shard_map/pallas_call | solution.py:312
  364.5 6.5 convolution_convert_fusion.11
  371.0 11.6 %shard_map.188 = bf16[2048,1792]{1,0:T(8,128)(2,1)} custom-call(bf16[2048,1280]{1,0:T(8,128)(2,1)} %copy-done.10, bf16[896,1280]{1,0:T(8,128)(2,1)S(1)} %bitcast.350, bf16[2048,1792]{1,0:T(8,128)(2,1)} %get-tuple-element.194.pre_ref), custom_call_target="tpu_custom_call" | custom-call | flops 4697620480 | bytes 12582912 | tf_op jit(solution)/shard_map/pallas_call | solution.py:344
  382.6 15.6 %convolution_convert_fusion.9 = bf16[1280,1792]{1,0:T(8,128)(2,1)} fusion(bf16[2048,1280]{1,0:T(8,128)(2,1)} %bitcast.375, bf16[2048,1792]{1,0:T(8,128)(2,1)} %shard_map.188), kind=kOutput, calls=%fused_computation.20 | convolution fusion | flops 9397534720 | bytes 17170432 | tf_op jit(solution)/shard_map/dot_general | solution.py:22
  398.2 14.8 %convolution_convert_fusion.8 = bf16[2048,1280]{1,0:T(8,128)(2,1)} fusion(bf16[2048,1792]{1,0:T(8,128)(2,1)} %shard_map.188, bf16[1280,1792]{1,0:T(8,128)(2,1)} %bitcast.426), kind=kOutput, calls=%fused_computation.19 | convolution fusion | flops 9397862400 | bytes 17170432 | tf_op jit(solution)/shard_map/dot_general | solution.py:28
  413.1 17.8 %all-gather.15.cloned.1.call-done = bf16[1,896,1280]{2,1,0:T(8,128)(2,1)} async-done(((bf16[1,224,1280]{2,1,0:T(8,128)(2,1)}), bf16[1,896,1280]{2,1,0:T(8,128)(2,1)}) %all-gather.15.cloned.1.call-update) | async-done | bytes 2293776 | tf_op jit(solution)/shard_map/all_gather | solution.py:424
  430.9 15.8 %shard_map.189 = (bf16[2048,1792]{1,0:T(8,128)(2,1)}, bf16[2048,896]{1,0:T(8,128)(2,1)S(1)}) custom-call(bf16[2048,1280]{1,0:T(8,128)(2,1)} %bitcast.376, bf16[1280,1792]{1,0:T(8,128)(2,1)} %bitcast.420), custom_call_target="tpu_custom_call" | custom-call | flops 9395240960 | bytes 12582912 | tf_op jit(solution)/shard_map/pallas_call | solution.py:312
  452.5 13.2 %fusion.1 = (f32[2048]{0:T(1024)S(1)}, f32[2048]{0:T(1024)S(1)}, bf16[2048,1280]{1,0:T(8,128)(2,1)}, bf16[2048,1280]{1,0:T(8,128)(2,1)}) fusion(bf16[8,256,1280]{2,1,0:T(8,128)(2,1)} %copy-done.9, bf16[2048,1280]{1,0:T(8,128)(2,1)S(1)} %convolution_convert_fusion, f32[2048]{0:T(1024)S(1)} %get-tuple-element.304, bf16[2048,896]{1,0:T(8,128)(2,1)S(1)} %copy-done.6, ...), kind=kOutput, calls=%fused_computation.5 | convolution fusion | flops 4723830784 | bytes 26959872 | tf_op jit(solution)/shard_map/dot_general | solution.py:34
  496.2 12.3 %shard_map.190 = bf16[2048,1792]{1,0:T(8,128)(2,1)} custom-call(bf16[2048,1280]{1,0:T(8,128)(2,1)} %get-tuple-element.219.grad_ref, bf16[896,1280]{1,0:T(8,128)(2,1)S(1)} %bitcast.353, bf16[2048,1792]{1,0:T(8,128)(2,1)} %get-tuple-element.203.pre_ref), custom_call_target="tpu_custom_call" | custom-call | flops 4697620480 | bytes 12582912 | tf_op jit(solution)/shard_map/pallas_call | solution.py:344
  514.0 7.6 add_convert_fusion.4
  530.7 7.1 add_convert_fusion.3
  543.2 6.4 convolution_convert_fusion.10
  561.7 15.3 %convolution_convert_fusion.7 = bf16[1280,1792]{1,0:T(8,128)(2,1)} fusion(bf16[2048,1280]{1,0:T(8,128)(2,1)} %bitcast.377, bf16[2048,1792]{1,0:T(8,128)(2,1)} %shard_map.190), kind=kOutput, calls=%fused_computation.18 | convolution fusion | flops 9397534720 | bytes 17170432 | tf_op jit(solution)/shard_map/dot_general | solution.py:22
  600.0 18.4 %shard_map.191 = (bf16[256,1280]{1,0:T(8,128)(2,1)}, bf16[1024,1280]{1,0:T(8,128)(2,1)}, bf16[1024,1280]{1,0:T(8,128)(2,1)}) custom-call(bf16[256,1280]{1,0:T(8,128)(2,1)} %get-tuple-element.234.q_ref, bf16[1024,1280]{1,0:T(8,128)(2,1)} %get-tuple-element.235.k_ref, bf16[1024,1280]{1,0:T(8,128)(2,1)} %get-tuple-element.236.v_ref, ...), custom_call_target="tpu_custom_call" | custom-call | flops 3355443200 | bytes 10485760 | tf_op jit(solution)/shard_map/pallas_call | solution.py:284
  644.5 9.9 %multiply_reduce_fusion = (f32[1280]{0:T(1024)S(1)}, bf16[1024,1280]{1,0:T(8,128)(2,1)}, f32[1024,1280]{1,0:T(8,128)}, f32[1024,1280]{1,0:T(8,128)}) fusion(f32[1024]{0:T(1024)S(1)} %copy-done.94, bf16[256,1280]{1,0:T(8,128)(2,1)S(1)} %copy-done.40, bf16[256,1280]{1,0:T(8,128)(2,1)S(1)} %copy-done.43, bf16[256,1280]{1,0:T(8,128)(2,1)S(1)} %copy-done.46, ...), kind=kOutput, calls=%fused_computation.33 | convolution fusion | flops 3372481280 | bytes 26878976 | tf_op jit(solution)/shard_map/dot_general | solution.py:28
  681.9 15.5 %collective-permute-done.58 = bf16[2,2,40,2560]{3,2,1,0:T(8,128)(2,1)S(1)} collective-permute-done((bf16[2,2,40,2560]{3,2,1,0:T(8,128)(2,1)S(1)}, bf16[2,2,40,2560]{3,2,1,0:T(8,128)(2,1)S(1)}, u32[]{:S(2)}, u32[]{:S(2)}) %collective-permute-start.58) | collective-permute-done | bytes 819232 | tf_op jit(solution)/shard_map/ppermute | solution.py:46
  704.5 7.0 collective-permute-done.60
  714.0 7.8 collective-permute-done.64
  726.1 37.7 %collective-permute-done.68 = bf16[2,40,1280]{2,1,0:T(8,128)(2,1)S(1)} collective-permute-done((bf16[2,40,1280]{2,1,0:T(8,128)(2,1)S(1)}, bf16[2,40,1280]{2,1,0:T(8,128)(2,1)S(1)}, u32[]{:S(2)}, u32[]{:S(2)}) %collective-permute-start.68) | collective-permute-done | bytes 204832 | tf_op jit(solution)/shard_map/ppermute | solution.py:51
  767.9 10.8 %collective-permute-done.74 = bf16[40,1280]{1,0:T(8,128)(2,1)S(1)} collective-permute-done((bf16[40,1280]{1,0:T(8,128)(2,1)S(1)}, bf16[40,1280]{1,0:T(8,128)(2,1)S(1)}, u32[]{:S(2)}, u32[]{:S(2)}) %collective-permute-start.74) | collective-permute-done | bytes 102432 | tf_op jit(solution)/shard_map/ppermute | solution.py:51
  795.8 7.7 collective-permute-done.70
  804.3 13.0 %collective-permute-done.73 = bf16[40,2560]{1,0:T(8,128)(2,1)S(1)} collective-permute-done((bf16[40,2560]{1,0:T(8,128)(2,1)S(1)}, bf16[40,2560]{1,0:T(8,128)(2,1)S(1)}, u32[]{:S(2)}, u32[]{:S(2)}) %collective-permute-start.73) | collective-permute-done | bytes 204832 | tf_op jit(solution)/shard_map/ppermute | solution.py:51
  (657 shorter events, 398.0 us)
Async XLA Ops:
  7.2 248.7 %all-gather.9.cloned.1.call-start = ((), (), s32[]{:S(2)}) async-start(), calls=%async_computation.8 | async-start | bytes 5734400 | tf_op jit(solution)/shard_map/all_gather | solution.py:423
  15.1 27.2 %collective-permute-start.1 = (bf16[40,3968]{1,0:T(8,128)(2,1)S(1)}, bf16[40,3968]{1,0:T(8,128)(2,1)}, u32[]{:S(2)}, u32[]{:S(2)}) collective-permute-start(bf16[40,3968]{1,0:T(8,128)(2,1)S(1)} %concatenate.94), channel_id=1, source_target_pairs={{0,2},{1,3},{2,0},{3,1},{4,6},{5,7},{6,4},{7,5},{8,10},{9,11},{10,... | collective-permute-start | bytes 952328 | tf_op jit(solution)/shard_map/ppermute | solution.py:51
  46.5 29.3 %collective-permute-start.4 = (bf16[4,40,3968]{2,1,0:T(8,128)(2,1)}, bf16[4,40,3968]{2,1,0:T(8,128)(2,1)}, u32[]{:S(2)}, u32[]{:S(2)}) collective-permute-start(bf16[4,40,3968]{2,1,0:T(8,128)(2,1)} %bitcast_dynamic-update-slice_fusion.20), channel_id=1, source_target_pairs={{0,16},{4,20},{8,24},{12,28},{16,0},{20,4},{24,8},{28,12},{1,17},{... | collective-permute-start | bytes 3809288 | tf_op jit(solution)/shard_map/ppermute | solution.py:46
  48.0 31.2 %collective-permute-start.3 = (bf16[4,40,3968]{2,1,0:T(8,128)(2,1)}, bf16[4,40,3968]{2,1,0:T(8,128)(2,1)}, u32[]{:S(2)}, u32[]{:S(2)}) collective-permute-start(bf16[4,40,3968]{2,1,0:T(8,128)(2,1)} %bitcast_dynamic-update-slice_fusion.20), channel_id=1, source_target_pairs={{0,8},{4,12},{8,0},{12,4},{16,24},{20,28},{24,16},{28,20},{1,9},{5... | collective-permute-start | bytes 3809288 | tf_op jit(solution)/shard_map/ppermute | solution.py:46
  52.2 103.8 %collective-permute-start.12 = (bf16[256,1280]{1,0:T(8,128)(2,1)}, bf16[256,1280]{1,0:T(8,128)(2,1)S(1)}, u32[]{:S(2)}, u32[]{:S(2)}) collective-permute-start(bf16[256,1280]{1,0:T(8,128)(2,1)} %param.11), channel_id=1, source_target_pairs={{0,3},{4,7},{8,11},{12,15},{16,19},{20,23},{24,27},{28,31}} | collective-permute-start | bytes 1966088 | tf_op jit(solution)/shard_map/ppermute | solution.py:74
  56.7 99.2 %collective-permute-start.11 = (bf16[256,1280]{1,0:T(8,128)(2,1)}, bf16[256,1280]{1,0:T(8,128)(2,1)S(1)}, u32[]{:S(2)}, u32[]{:S(2)}) collective-permute-start(bf16[256,1280]{1,0:T(8,128)(2,1)} %param.11), channel_id=1, source_target_pairs={{0,2},{1,3},{4,6},{5,7},{8,10},{9,11},{12,14},{13,15},{16,18},{17,... | collective-permute-start | bytes 1966088 | tf_op jit(solution)/shard_map/ppermute | solution.py:74
  58.1 98.6 %collective-permute-start.10 = (bf16[256,1280]{1,0:T(8,128)(2,1)}, bf16[256,1280]{1,0:T(8,128)(2,1)S(1)}, u32[]{:S(2)}, u32[]{:S(2)}) collective-permute-start(bf16[256,1280]{1,0:T(8,128)(2,1)} %param.11), channel_id=1, source_target_pairs={{0,1},{1,2},{2,3},{4,5},{5,6},{6,7},{8,9},{9,10},{10,11},{12,13},{... | collective-permute-start | bytes 1966088 | tf_op jit(solution)/shard_map/ppermute | solution.py:74
  75.7 29.4 %collective-permute-start.9 = (bf16[40,4352]{1,0:T(8,128)(2,1)S(1)}, bf16[40,4352]{1,0:T(8,128)(2,1)}, u32[]{:S(2)}, u32[]{:S(2)}) collective-permute-start(bf16[40,4352]{1,0:T(8,128)(2,1)S(1)} %copy-done.56), channel_id=1, source_target_pairs={{0,3},{1,2},{2,1},{3,0},{4,7},{5,6},{6,5},{7,4},{8,11},{9,10},{10,... | collective-permute-start | bytes 1044488 | tf_op jit(solution)/shard_map/ppermute | solution.py:51
  79.2 28.9 %collective-permute-start.5 = (bf16[2,40,3968]{2,1,0:T(8,128)(2,1)S(1)}, bf16[2,40,3968]{2,1,0:T(8,128)(2,1)S(1)}, u32[]{:S(2)}, u32[]{:S(2)}) collective-permute-start(bf16[2,40,3968]{2,1,0:T(8,128)(2,1)S(1)} %slice.284), channel_id=1, source_target_pairs={{0,8},{4,12},{8,0},{12,4},{16,24},{20,28},{24,16},{28,20},{1,9},{5... | collective-permute-start | bytes 1904648 | tf_op jit(solution)/shard_map/ppermute | solution.py:46
  105.1 27.9 %collective-permute-start.6 = (bf16[2,40,3968]{2,1,0:T(8,128)(2,1)S(1)}, bf16[2,40,3968]{2,1,0:T(8,128)(2,1)S(1)}, u32[]{:S(2)}, u32[]{:S(2)}) collective-permute-start(bf16[2,40,3968]{2,1,0:T(8,128)(2,1)S(1)} %slice.285), channel_id=1, source_target_pairs={{0,16},{4,20},{8,24},{12,28},{16,0},{20,4},{24,8},{28,12},{1,17},{... | collective-permute-start | bytes 1904648 | tf_op jit(solution)/shard_map/ppermute | solution.py:46
  108.1 40.5 %collective-permute-start.8 = (bf16[40,4352]{1,0:T(8,128)(2,1)S(1)}, bf16[40,4352]{1,0:T(8,128)(2,1)S(1)}, u32[]{:S(2)}, u32[]{:S(2)}) collective-permute-start(bf16[40,4352]{1,0:T(8,128)(2,1)S(1)} %copy-done.56), channel_id=1, source_target_pairs={{0,2},{1,3},{2,0},{3,1},{4,6},{5,7},{6,4},{7,5},{8,10},{9,11},{10,... | collective-permute-start | bytes 1044488 | tf_op jit(solution)/shard_map/ppermute | solution.py:51
  158.5 141.3 %all-gather.11.cloned.1.call-start = ((), (), s32[]{:S(2)}) async-start(), calls=%async_computation.9 | async-start | bytes 2867200 | tf_op jit(solution)/shard_map/all_gather | solution.py:424
  165.0 217.5 %all-gather.13.cloned.1.call-start = ((), (), s32[]{:S(2)}) async-start(), calls=%async_computation.10 | async-start | bytes 5734400 | tf_op jit(solution)/shard_map/all_gather | solution.py:423
  167.4 45.2 %collective-permute-start.14 = (bf16[4,40,4352]{2,1,0:T(8,128)(2,1)S(1)}, bf16[4,40,4352]{2,1,0:T(8,128)(2,1)S(1)}, u32[]{:S(2)}, u32[]{:S(2)}) collective-permute-start(bf16[4,40,4352]{2,1,0:T(8,128)(2,1)S(1)} %bitcast_dynamic-update-slice_fusion.16), channel_id=1, source_target_pairs={{0,16},{4,20},{8,24},{12,28},{16,0},{20,4},{24,8},{28,12},{1,17},{... | collective-permute-start | bytes 4177928 | tf_op jit(solution)/shard_map/ppermute | solution.py:46
  169.1 43.6 %collective-permute-start.13 = (bf16[4,40,4352]{2,1,0:T(8,128)(2,1)S(1)}, bf16[4,40,4352]{2,1,0:T(8,128)(2,1)}, u32[]{:S(2)}, u32[]{:S(2)}) collective-permute-start(bf16[4,40,4352]{2,1,0:T(8,128)(2,1)S(1)} %bitcast_dynamic-update-slice_fusion.16), channel_id=1, source_target_pairs={{0,8},{4,12},{8,0},{12,4},{16,24},{20,28},{24,16},{28,20},{1,9},{5... | collective-permute-start | bytes 4177928 | tf_op jit(solution)/shard_map/ppermute | solution.py:46
  169.6 261.3 %all-gather.15.cloned.1.call-start = ((), (), s32[]{:S(2)}) async-start(), calls=%async_computation.11 | async-start | bytes 2867200 | tf_op jit(solution)/shard_map/all_gather | solution.py:424
  243.3 250.7 %reduce-scatter.5.cloned.1.call-start = ((), (), s32[]{:S(2)}) async-start(), calls=%async_computation.4 | async-start | bytes 2867200 | tf_op jit(solution)/shard_map/reduce_scatter | solution.py:521
  319.7 27.2 %collective-permute-start.33 = (bf16[2,2,4,40,3072]{4,3,2,1,0:T(8,128)(2,1)}, bf16[2,2,4,40,3072]{4,3,2,1,0:T(8,128)(2,1)}, u32[]{:S(2)}, u32[]{:S(2)}) collective-permute-start(bf16[2,2,4,40,3072]{4,3,2,1,0:T(8,128)(2,1)} %dynamic-slice_bitcast_fusion), channel_id=1, source_target_pairs={{0,4},{4,0},{8,12},{12,8},{16,20},{20,16},{24,28},{28,24},{1,5},{5... | collective-permute-start | bytes 11796488 | tf_op jit(solution)/shard_map/ppermute | solution.py:46
  354.3 28.3 %collective-permute-start.35 = (bf16[2,2,40,3072]{3,2,1,0:T(8,128)(2,1)}, bf16[2,2,40,3072]{3,2,1,0:T(8,128)(2,1)S(1)}, u32[]{:S(2)}, u32[]{:S(2)}) collective-permute-start(bf16[2,2,40,3072]{3,2,1,0:T(8,128)(2,1)} %get-tuple-element.335), channel_id=1, source_target_pairs={{0,16},{4,20},{8,24},{12,28},{16,0},{20,4},{24,8},{28,12},{1,17},{... | collective-permute-start | bytes 2949128 | tf_op jit(solution)/shard_map/ppermute | solution.py:46
  413.0 164.5 %reduce-scatter.7.cloned.1.call-start = ((), (), s32[]{:S(2)}) async-start(), calls=%async_computation.5 | async-start | bytes 5734400 | tf_op jit(solution)/shard_map/reduce_scatter | solution.py:521
  472.8 35.7 %collective-permute-start.37 = (bf16[4,272,1280]{2,1,0:T(8,128)(2,1)}, bf16[4,272,1280]{2,1,0:T(8,128)(2,1)}, u32[]{:S(2)}, u32[]{:S(2)}) collective-permute-start(bf16[4,272,1280]{2,1,0:T(8,128)(2,1)} %fusion.28), channel_id=1, source_target_pairs={{0,4},{4,0},{8,12},{12,8},{16,20},{20,16},{24,28},{28,24},{1,5},{5... | collective-permute-start | bytes 8355848 | tf_op jit(solution)/shard_map/ppermute | solution.py:46
  485.4 181.8 %reduce-scatter.9.cloned.1.call-start = ((), (), s32[]{:S(2)}) async-start(), calls=%async_computation.6 | async-start | bytes 2867200 | tf_op jit(solution)/shard_map/reduce_scatter | solution.py:521
  577.1 241.0 %reduce-scatter.11.cloned.1.call-start = ((), (), s32[]{:S(2)}) async-start(), calls=%async_computation.7 | async-start | bytes 5734400 | tf_op jit(solution)/shard_map/reduce_scatter | solution.py:521
  589.8 112.7 %collective-permute-start.63 = (bf16[2,40,3072]{2,1,0:T(8,128)(2,1)}, bf16[2,40,3072]{2,1,0:T(8,128)(2,1)}, u32[]{:S(2)}, u32[]{:S(2)}) collective-permute-start(bf16[2,40,3072]{2,1,0:T(8,128)(2,1)} %get-tuple-element.360), channel_id=1, source_target_pairs={{0,1},{1,0},{2,3},{3,2},{4,5},{5,4},{6,7},{7,6},{8,9},{9,8},{10,11... | collective-permute-start | bytes 1474568 | tf_op jit(solution)/shard_map/ppermute | solution.py:51
  631.4 34.1 %collective-permute-start.56 = (bf16[2,40,1280]{2,1,0:T(8,128)(2,1)}, bf16[2,40,1280]{2,1,0:T(8,128)(2,1)}, u32[]{:S(2)}, u32[]{:S(2)}) collective-permute-start(bf16[2,40,1280]{2,1,0:T(8,128)(2,1)} %get-tuple-element.394), channel_id=1, source_target_pairs={{0,8},{4,12},{8,0},{12,4},{16,24},{20,28},{24,16},{28,20},{1,9},{5... | collective-permute-start | bytes 614408 | tf_op jit(solution)/shard_map/ppermute | solution.py:46
  633.4 32.1 %collective-permute-start.55 = (bf16[2,40,1280]{2,1,0:T(8,128)(2,1)}, bf16[2,40,1280]{2,1,0:T(8,128)(2,1)}, u32[]{:S(2)}, u32[]{:S(2)}) collective-permute-start(bf16[2,40,1280]{2,1,0:T(8,128)(2,1)} %get-tuple-element.396), channel_id=1, source_target_pairs={{0,16},{4,20},{8,24},{12,28},{16,0},{20,4},{24,8},{28,12},{1,17},{... | collective-permute-start | bytes 614408 | tf_op jit(solution)/shard_map/ppermute | solution.py:46
  657.2 129.3 %collective-permute-start.52 = (bf16[256,1280]{1,0:T(8,128)(2,1)}, bf16[256,1280]{1,0:T(8,128)(2,1)}, u32[]{:S(2)}, u32[]{:S(2)}) collective-permute-start(bf16[256,1280]{1,0:T(8,128)(2,1)} %get-tuple-element.328), channel_id=1, source_target_pairs={{3,0},{7,4},{11,8},{15,12},{19,16},{23,20},{27,24},{31,28}} | collective-permute-start | bytes 1966088 | tf_op jit(solution)/shard_map/ppermute | solution.py:652
  697.4 89.1 %collective-permute-start.51 = (bf16[256,1280]{1,0:T(8,128)(2,1)S(1)}, bf16[256,1280]{1,0:T(8,128)(2,1)S(1)}, u32[]{:S(2)}, u32[]{:S(2)}) collective-permute-start(bf16[256,1280]{1,0:T(8,128)(2,1)S(1)} %copy-done.65), channel_id=1, source_target_pairs={{2,0},{3,1},{6,4},{7,5},{10,8},{11,9},{14,12},{15,13},{18,16},{19,... | collective-permute-start | bytes 1966088 | tf_op jit(solution)/shard_map/ppermute | solution.py:652
  703.2 83.3 %collective-permute-start.50 = (bf16[256,1280]{1,0:T(8,128)(2,1)S(1)}, bf16[256,1280]{1,0:T(8,128)(2,1)S(1)}, u32[]{:S(2)}, u32[]{:S(2)}) collective-permute-start(bf16[256,1280]{1,0:T(8,128)(2,1)S(1)} %copy-done.64), channel_id=1, source_target_pairs={{1,0},{2,1},{3,2},{5,4},{6,5},{7,6},{9,8},{10,9},{11,10},{13,12},{... | collective-permute-start | bytes 1966088 | tf_op jit(solution)/shard_map/ppermute | solution.py:652
  721.8 42.0 %collective-permute-start.68 = (bf16[2,40,1280]{2,1,0:T(8,128)(2,1)S(1)}, bf16[2,40,1280]{2,1,0:T(8,128)(2,1)S(1)}, u32[]{:S(2)}, u32[]{:S(2)}) collective-permute-start(bf16[2,40,1280]{2,1,0:T(8,128)(2,1)S(1)} %dynamic-slice_bitcast_fusion.60), channel_id=1, source_target_pairs={{0,1},{1,0},{2,3},{3,2},{4,5},{5,4},{6,7},{7,6},{8,9},{9,8},{10,11... | collective-permute-start | bytes 614408 | tf_op jit(solution)/shard_map/ppermute | solution.py:51
  724.1 56.8 %collective-permute-start.66 = (bf16[2,40,1408]{2,1,0:T(8,128)(2,1)S(1)}, bf16[2,40,1408]{2,1,0:T(8,128)(2,1)S(1)}, u32[]{:S(2)}, u32[]{:S(2)}) collective-permute-start(bf16[2,40,1408]{2,1,0:T(8,128)(2,1)S(1)} %get-tuple-element.392), channel_id=1, source_target_pairs={{0,16},{4,20},{8,24},{12,28},{16,0},{20,4},{24,8},{28,12},{1,17},{... | collective-permute-start | bytes 675848 | tf_op jit(solution)/shard_map/ppermute | solution.py:46
  786.3 34.6 %collective-permute-start.69 = (bf16[40,3072]{1,0:T(8,128)(2,1)S(1)}, bf16[40,3072]{1,0:T(8,128)(2,1)}, u32[]{:S(2)}, u32[]{:S(2)}) collective-permute-start(bf16[40,3072]{1,0:T(8,128)(2,1)S(1)} %dynamic-slice_bitcast_fusion.52), channel_id=1, source_target_pairs={{0,2},{1,3},{2,0},{3,1},{4,6},{5,7},{6,4},{7,5},{8,10},{9,11},{10,... | collective-permute-start | bytes 737288 | tf_op jit(solution)/shard_map/ppermute | solution.py:51
  (170 other events, 1875.2 us)
Sparse Core Ops, SparseCore 0:
  158.6 84.5 all-gather.8
  245.4 47.8 all-gather.10
  294.9 86.0 all-gather.12
  383.0 47.8 all-gather.14
  433.6 45.8 reduce-scatter.4
  485.5 80.1 reduce-scatter.6
  577.2 55.9 reduce-scatter.8
  636.0 121.3 reduce-scatter.10

commit v4 on v3

--- a/solution.py
+++ b/solution.py
@@ -524,6 +524,8 @@
     results, gate_rows = [], []
     for e in range(local):
         pre, act = expert_forward(ffn_all, expert_weights[e][0])
+        if e:
+            act, expert_weights[e][1] = after(act, expert_weights[e][1])
         if e == 0:
             *up_far, shared_core, act = after(*up_far, shared_core, act)
             shared_state = rows_near(shared_kept, shared_core)
@@ -556,7 +558,7 @@
                 *shared_state, in_grad = after(*shared_state, in_grad)
                 shared_line = rows_line(*shared_state)
             back = (back + times_transposed(pre_grad, expert_weights[e][0])).astype(bf16)
-            back, ffn_all, expert_weights[e + 1][1] = after(back, ffn_all, expert_weights[e + 1][1])
+            back, ffn_all = after(back, ffn_all)
             continue
         sides = (slice(half, 2 * half), slice(0, half))
 
@@ -676,15 +678,15 @@
     query_state = split_far(*query_state)
     *pair_state, query_state[0] = after(*pair_state, query_state[0])
     pair_line = rows_line(*pair_state)
-    attn_arrived, pair_kept = after(attn_line[1], pair_line[0])
-    attn_line, pair_line = (attn_line[0], attn_arrived), (pair_kept, pair_line[1])
-    attn_last = rows_last(*attn_line)
     *query_state, _ = after(*query_state, pair_line[0])
     query_line = rows_line(*query_state)
     *arrived, query_kept = after(*arrived, query_line[0])
     query_line = (query_kept, query_line[1])
     attn_in_grad = parts[0] + sum(x.astype(f32) for x in arrived)
     query_line = rows_last(*query_line)
+    attn_arrived, query_kept = after(attn_line[1], query_line[0])
+    query_line = (query_kept, query_line[1])
+    attn_last = rows_last(attn_line[0], attn_arrived)
     in_parts[-1], shared_arrived, query_kept = after(in_parts[-1], shared_line[1], query_line[0])
     query_line = (query_kept, query_line[1])
     shared_part = rows_end(shared_line[0], shared_arrived).astype(f32)

time: 848 us -> 834 us (0.983)
  waiting for transfers between devices: 235 us -> 209 us
    all_gather x2, waiting for transfers between devices: 17.8 us -> 0.13 us  [per_device(): lax.all_gather(expert_out_low[e], 'dp', axis=0, tiled=True)]
    ppermute x14, waiting for transfers between devices: 130 us -> 120 us  [flip_dp(): return lax.ppermute(x, 'dp', [(i, i ^ bit) for i in range(count)])]
    unnamed x240 -> x238, local copies, waits for them, and re-layouts: 17.8 us -> 19 us
  transfers between devices with their start and end apart: 83 -> 83, of which waited for: 34 -> 34; matrix products, arithmetic and copies ran while one was open for 41% -> 43% of each run, Pallas kernels for 11% -> 11%
where the time goes in v4:
time: 834 us; the launch traced here: 826 us
  waiting for transfers between devices  209 us (25%)
  matrix products  157 us (19%)
  local copies, waits for them, and re-layouts  123 us (15%)
  starting transfers between devices  114 us (14%)
  other arithmetic  113 us (14%)
  Pallas kernels  93.7 us (11%)
  between operations  16.7 us (2%)
    ppermute x14, waiting for transfers between devices, flip_dp(): return lax.ppermute(x, 'dp', [(i, i ^ bit) for i in range(count)])  120 us
    ppermute x55, waiting for transfers between devices, flip(): return lax.ppermute(x, 'ep', [(i, i ^ bit) for i in range(count)])  88.3 us
    dot_general x11, matrix products, contract_rows(): lax.dot_general(left_side, right_side, (((0,), (0,)), ((), ())), preferre...  62.8 us
    dot_general x10, matrix products, times_transposed(): lax.dot_general(left_side, right_side, (((1,), (1,)), ((), ())), preferre...  60.3 us
    ppermute x14, starting transfers between devices, flip_dp(): return lax.ppermute(x, 'dp', [(i, i ^ bit) for i in range(count)])  51.5 us
    ppermute x55, starting transfers between devices, flip(): return lax.ppermute(x, 'ep', [(i, i ^ bit) for i in range(count)])  49.3 us
    pallas_call x2, Pallas kernels, expert_forward(): pl.pallas_call(expert_kernel, grid=(count // step,), in_specs=[rows(width...  31.8 us
    dot_general x6, matrix products, matmul(): return jnp.dot(left_side, right_side, preferred_element_type=f32)  30.7 us
  transfers between devices with their start and end apart: 83, of which 34 were waited for; matrix products, arithmetic and copies ran while one was open for 43% of the time, Pallas kernels for 11%

profile of v4, /device:TPU:0, one launch (start us, length us, event | category | flops | bytes accessed | tf_op | source)
XLA Modules:
  0.0 826.1 jit_solution(7275924002241037257)
XLA Ops:
  23.6 18.7 %collective-permute-done.1 = bf16[40,3968]{1,0:T(8,128)(2,1)} collective-permute-done((bf16[40,3968]{1,0:T(8,128)(2,1)S(1)}, bf16[40,3968]{1,0:T(8,128)(2,1)}, u32[]{:S(2)}, u32[]{:S(2)}) %collective-permute-start.1) | collective-permute-done | bytes 317472 | tf_op jit(solution)/shard_map/ppermute | solution.py:51
  65.6 10.2 %collective-permute-done.4 = bf16[4,40,3968]{2,1,0:T(8,128)(2,1)} collective-permute-done((bf16[4,40,3968]{2,1,0:T(8,128)(2,1)}, bf16[4,40,3968]{2,1,0:T(8,128)(2,1)}, u32[]{:S(2)}, u32[]{:S(2)}) %collective-permute-start.4) | collective-permute-done | bytes 1269792 | tf_op jit(solution)/shard_map/ppermute | solution.py:46
  84.3 20.8 %collective-permute-done.9 = bf16[40,4352]{1,0:T(8,128)(2,1)} collective-permute-done((bf16[40,4352]{1,0:T(8,128)(2,1)S(1)}, bf16[40,4352]{1,0:T(8,128)(2,1)}, u32[]{:S(2)}, u32[]{:S(2)}) %collective-permute-start.9) | collective-permute-done | bytes 348192 | tf_op jit(solution)/shard_map/ppermute | solution.py:51
  108.1 24.9 %collective-permute-start.8 = (bf16[40,4352]{1,0:T(8,128)(2,1)S(1)}, bf16[40,4352]{1,0:T(8,128)(2,1)S(1)}, u32[]{:S(2)}, u32[]{:S(2)}) collective-permute-start(bf16[40,4352]{1,0:T(8,128)(2,1)S(1)} %copy-done.55), channel_id=1, source_target_pairs={{0,2},{1,3},{2,0},{3,1},{4,6},{5,7},{6,4},{7,5},{8,10},{9,11},{10,... | collective-permute-start | bytes 1044488 | tf_op jit(solution)/shard_map/ppermute | solution.py:51
  133.0 11.2 %collective-permute-start.7 = (bf16[40,4352]{1,0:T(8,128)(2,1)S(1)}, bf16[40,4352]{1,0:T(8,128)(2,1)S(1)}, u32[]{:S(2)}, u32[]{:S(2)}) collective-permute-start(bf16[40,4352]{1,0:T(8,128)(2,1)S(1)} %copy-done.55), channel_id=1, source_target_pairs={{0,1},{1,0},{2,3},{3,2},{4,5},{5,4},{6,7},{7,6},{8,9},{9,8},{10,11... | collective-permute-start | bytes 1044488 | tf_op jit(solution)/shard_map/ppermute | solution.py:51
  148.6 7.4 collective-permute-done.7
  187.1 6.0 multiply_convert_fusion.x_ref
  193.0 19.6 %shard_map.186 = (bf16[256,1280]{1,0:T(8,128)(2,1)}, bf16[256,1280]{1,0:T(8,128)(2,1)}, bf16[1024,1280]{1,0:T(8,128)(2,1)}, bf16[1024,1280]{1,0:T(8,128)(2,1)}) custom-call(bf16[1024,1280]{1,0:T(8,128)(2,1)} %multiply_convert_fusion.x_ref, bf16[1280,3968]{1,0:T(8,128)(2,1)} %bitcast.356, bf16[1280,3968]{1,0:T(8,128)(2,1)} %bitcast.357, ...), custom_call_target="tpu_custom_call" | custom-call | flops 8891924480 | bytes 17694720 | tf_op jit(solution)/shard_map/pallas_call | solution.py:241
  219.8 11.6 %collective-permute-done.16 = bf16[2,40,4352]{2,1,0:T(8,128)(2,1)S(1)} collective-permute-done((bf16[2,40,4352]{2,1,0:T(8,128)(2,1)S(1)}, bf16[2,40,4352]{2,1,0:T(8,128)(2,1)S(1)}, u32[]{:S(2)}, u32[]{:S(2)}) %collective-permute-start.16) | collective-permute-done | bytes 696352 | tf_op jit(solution)/shard_map/ppermute | solution.py:46
  301.9 7.8 pad_maximum_fusion
  330.7 16.1 %shard_map.187 = (bf16[2048,1792]{1,0:T(8,128)(2,1)}, bf16[2048,896]{1,0:T(8,128)(2,1)S(1)}) custom-call(bf16[2048,1280]{1,0:T(8,128)(2,1)} %bitcast.375, bf16[1280,1792]{1,0:T(8,128)(2,1)} %bitcast.427), custom_call_target="tpu_custom_call" | custom-call | flops 9395240960 | bytes 12582912 | tf_op jit(solution)/shard_map/pallas_call | solution.py:312
  364.6 6.5 convolution_convert_fusion.11
  371.1 11.6 %shard_map.188 = bf16[2048,1792]{1,0:T(8,128)(2,1)} custom-call(bf16[2048,1280]{1,0:T(8,128)(2,1)} %copy-done.9, bf16[896,1280]{1,0:T(8,128)(2,1)S(1)} %bitcast.351, bf16[2048,1792]{1,0:T(8,128)(2,1)} %get-tuple-element.195.pre_ref), custom_call_target="tpu_custom_call" | custom-call | flops 4697620480 | bytes 12582912 | tf_op jit(solution)/shard_map/pallas_call | solution.py:344
  382.7 15.6 %convolution_convert_fusion.9 = bf16[1280,1792]{1,0:T(8,128)(2,1)} fusion(bf16[2048,1280]{1,0:T(8,128)(2,1)} %bitcast.376, bf16[2048,1792]{1,0:T(8,128)(2,1)} %shard_map.188), kind=kOutput, calls=%fused_computation.20 | convolution fusion | flops 9397534720 | bytes 17170432 | tf_op jit(solution)/shard_map/dot_general | solution.py:22
  398.3 14.8 %convolution_convert_fusion.8 = bf16[2048,1280]{1,0:T(8,128)(2,1)} fusion(bf16[2048,1792]{1,0:T(8,128)(2,1)} %shard_map.188, bf16[1280,1792]{1,0:T(8,128)(2,1)} %bitcast.428), kind=kOutput, calls=%fused_computation.19 | convolution fusion | flops 9397862400 | bytes 17170432 | tf_op jit(solution)/shard_map/dot_general | solution.py:28
  413.2 15.7 %shard_map.189 = (bf16[2048,1792]{1,0:T(8,128)(2,1)}, bf16[2048,896]{1,0:T(8,128)(2,1)S(1)}) custom-call(bf16[2048,1280]{1,0:T(8,128)(2,1)} %bitcast.377, bf16[1280,1792]{1,0:T(8,128)(2,1)} %bitcast.422), custom_call_target="tpu_custom_call" | custom-call | flops 9395240960 | bytes 12582912 | tf_op jit(solution)/shard_map/pallas_call | solution.py:312
  430.9 8.1 convolution_convert_fusion
  439.0 13.3 %fusion.1 = (f32[2048]{0:T(1024)S(1)}, f32[2048]{0:T(1024)S(1)}, bf16[2048,1280]{1,0:T(8,128)(2,1)}, bf16[2048,1280]{1,0:T(8,128)(2,1)}) fusion(bf16[8,256,1280]{2,1,0:T(8,128)(2,1)} %copy-done.8, bf16[2048,1280]{1,0:T(8,128)(2,1)S(1)} %convolution_convert_fusion, f32[2048]{0:T(1024)S(1)} %get-tuple-element.306, bf16[2048,896]{1,0:T(8,128)(2,1)S(1)} %copy-done.5, ...), kind=kOutput, calls=%fused_computation.5 | convolution fusion | flops 4723830784 | bytes 26959872 | tf_op jit(solution)/shard_map/dot_general | solution.py:34
  482.9 12.2 %shard_map.190 = bf16[2048,1792]{1,0:T(8,128)(2,1)} custom-call(bf16[2048,1280]{1,0:T(8,128)(2,1)} %get-tuple-element.221.grad_ref, bf16[896,1280]{1,0:T(8,128)(2,1)S(1)} %bitcast.354, bf16[2048,1792]{1,0:T(8,128)(2,1)} %get-tuple-element.205.pre_ref), custom_call_target="tpu_custom_call" | custom-call | flops 4697620480 | bytes 12582912 | tf_op jit(solution)/shard_map/pallas_call | solution.py:344
  501.0 7.6 add_convert_fusion.4
  508.6 6.5 collective-permute-done.40
  518.7 7.0 add_convert_fusion.3
  531.2 6.4 convolution_convert_fusion.10
  550.4 15.4 %convolution_convert_fusion.7 = bf16[1280,1792]{1,0:T(8,128)(2,1)} fusion(bf16[2048,1280]{1,0:T(8,128)(2,1)} %bitcast.378, bf16[2048,1792]{1,0:T(8,128)(2,1)} %shard_map.190), kind=kOutput, calls=%fused_computation.18 | convolution fusion | flops 9397534720 | bytes 17170432 | tf_op jit(solution)/shard_map/dot_general | solution.py:22
  589.0 18.5 %shard_map.191 = (bf16[256,1280]{1,0:T(8,128)(2,1)}, bf16[1024,1280]{1,0:T(8,128)(2,1)}, bf16[1024,1280]{1,0:T(8,128)(2,1)}) custom-call(bf16[256,1280]{1,0:T(8,128)(2,1)} %get-tuple-element.236.q_ref, bf16[1024,1280]{1,0:T(8,128)(2,1)} %get-tuple-element.237.k_ref, bf16[1024,1280]{1,0:T(8,128)(2,1)} %get-tuple-element.238.v_ref, ...), custom_call_target="tpu_custom_call" | custom-call | flops 3355443200 | bytes 10485760 | tf_op jit(solution)/shard_map/pallas_call | solution.py:284
  633.0 10.5 %multiply_reduce_fusion = (f32[1280]{0:T(1024)S(1)}, bf16[1024,1280]{1,0:T(8,128)(2,1)}, f32[1024,1280]{1,0:T(8,128)}, f32[1024,1280]{1,0:T(8,128)}) fusion(f32[1024]{0:T(1024)S(1)} %copy-done.93, bf16[256,1280]{1,0:T(8,128)(2,1)S(1)} %copy-done.39, bf16[256,1280]{1,0:T(8,128)(2,1)S(1)} %copy-done.42, bf16[256,1280]{1,0:T(8,128)(2,1)S(1)} %copy-done.45, ...), kind=kOutput, calls=%fused_computation.33 | convolution fusion | flops 3372481280 | bytes 26878976 | tf_op jit(solution)/shard_map/dot_general | solution.py:28
  672.4 14.3 %collective-permute-done.58 = bf16[2,2,40,2560]{3,2,1,0:T(8,128)(2,1)S(1)} collective-permute-done((bf16[2,2,40,2560]{3,2,1,0:T(8,128)(2,1)S(1)}, bf16[2,2,40,2560]{3,2,1,0:T(8,128)(2,1)S(1)}, u32[]{:S(2)}, u32[]{:S(2)}) %collective-permute-start.58) | collective-permute-done | bytes 819232 | tf_op jit(solution)/shard_map/ppermute | solution.py:46
  694.3 6.5 collective-permute-done.60
  703.8 7.3 collective-permute-done.64
  717.8 42.5 %collective-permute-done.72 = bf16[2,40,2560]{2,1,0:T(8,128)(2,1)S(1)} collective-permute-done((bf16[2,40,2560]{2,1,0:T(8,128)(2,1)S(1)}, bf16[2,40,2560]{2,1,0:T(8,128)(2,1)S(1)}, u32[]{:S(2)}, u32[]{:S(2)}) %collective-permute-start.72) | collective-permute-done | bytes 409632 | tf_op jit(solution)/shard_map/ppermute | solution.py:51
  775.0 9.1 %collective-permute-done.70 = bf16[2,40,1408]{2,1,0:T(8,128)(2,1)S(1)} collective-permute-done((bf16[2,40,1408]{2,1,0:T(8,128)(2,1)S(1)}, bf16[2,40,1408]{2,1,0:T(8,128)(2,1)S(1)}, u32[]{:S(2)}, u32[]{:S(2)}) %collective-permute-start.70) | collective-permute-done | bytes 225312 | tf_op jit(solution)/shard_map/ppermute | solution.py:51
  801.6 7.6 collective-permute-done.71
  (655 shorter events, 398.1 us)
Async XLA Ops:
  7.2 248.7 %all-gather.9.cloned.1.call-start = ((), (), s32[]{:S(2)}) async-start(), calls=%async_computation.8 | async-start | bytes 5734400 | tf_op jit(solution)/shard_map/all_gather | solution.py:423
  15.1 27.2 %collective-permute-start = (bf16[40,3968]{1,0:T(8,128)(2,1)S(1)}, bf16[40,3968]{1,0:T(8,128)(2,1)}, u32[]{:S(2)}, u32[]{:S(2)}) collective-permute-start(bf16[40,3968]{1,0:T(8,128)(2,1)S(1)} %concatenate.94), channel_id=1, source_target_pairs={{0,1},{1,0},{2,3},{3,2},{4,5},{5,4},{6,7},{7,6},{8,9},{9,8},{10,11... | collective-permute-start | bytes 952328 | tf_op jit(solution)/shard_map/ppermute | solution.py:51
  46.5 29.3 %collective-permute-start.4 = (bf16[4,40,3968]{2,1,0:T(8,128)(2,1)}, bf16[4,40,3968]{2,1,0:T(8,128)(2,1)}, u32[]{:S(2)}, u32[]{:S(2)}) collective-permute-start(bf16[4,40,3968]{2,1,0:T(8,128)(2,1)} %bitcast_dynamic-update-slice_fusion.20), channel_id=1, source_target_pairs={{0,16},{4,20},{8,24},{12,28},{16,0},{20,4},{24,8},{28,12},{1,17},{... | collective-permute-start | bytes 3809288 | tf_op jit(solution)/shard_map/ppermute | solution.py:46
  48.0 31.2 %collective-permute-start.3 = (bf16[4,40,3968]{2,1,0:T(8,128)(2,1)}, bf16[4,40,3968]{2,1,0:T(8,128)(2,1)}, u32[]{:S(2)}, u32[]{:S(2)}) collective-permute-start(bf16[4,40,3968]{2,1,0:T(8,128)(2,1)} %bitcast_dynamic-update-slice_fusion.20), channel_id=1, source_target_pairs={{0,8},{4,12},{8,0},{12,4},{16,24},{20,28},{24,16},{28,20},{1,9},{5... | collective-permute-start | bytes 3809288 | tf_op jit(solution)/shard_map/ppermute | solution.py:46
  52.2 103.8 %collective-permute-start.12 = (bf16[256,1280]{1,0:T(8,128)(2,1)}, bf16[256,1280]{1,0:T(8,128)(2,1)S(1)}, u32[]{:S(2)}, u32[]{:S(2)}) collective-permute-start(bf16[256,1280]{1,0:T(8,128)(2,1)} %param.11), channel_id=1, source_target_pairs={{0,3},{4,7},{8,11},{12,15},{16,19},{20,23},{24,27},{28,31}} | collective-permute-start | bytes 1966088 | tf_op jit(solution)/shard_map/ppermute | solution.py:74
  56.7 99.2 %collective-permute-start.11 = (bf16[256,1280]{1,0:T(8,128)(2,1)}, bf16[256,1280]{1,0:T(8,128)(2,1)S(1)}, u32[]{:S(2)}, u32[]{:S(2)}) collective-permute-start(bf16[256,1280]{1,0:T(8,128)(2,1)} %param.11), channel_id=1, source_target_pairs={{0,2},{1,3},{4,6},{5,7},{8,10},{9,11},{12,14},{13,15},{16,18},{17,... | collective-permute-start | bytes 1966088 | tf_op jit(solution)/shard_map/ppermute | solution.py:74
  58.1 98.6 %collective-permute-start.10 = (bf16[256,1280]{1,0:T(8,128)(2,1)}, bf16[256,1280]{1,0:T(8,128)(2,1)S(1)}, u32[]{:S(2)}, u32[]{:S(2)}) collective-permute-start(bf16[256,1280]{1,0:T(8,128)(2,1)} %param.11), channel_id=1, source_target_pairs={{0,1},{1,2},{2,3},{4,5},{5,6},{6,7},{8,9},{9,10},{10,11},{12,13},{... | collective-permute-start | bytes 1966088 | tf_op jit(solution)/shard_map/ppermute | solution.py:74
  75.7 29.4 %collective-permute-start.9 = (bf16[40,4352]{1,0:T(8,128)(2,1)S(1)}, bf16[40,4352]{1,0:T(8,128)(2,1)}, u32[]{:S(2)}, u32[]{:S(2)}) collective-permute-start(bf16[40,4352]{1,0:T(8,128)(2,1)S(1)} %copy-done.55), channel_id=1, source_target_pairs={{0,3},{1,2},{2,1},{3,0},{4,7},{5,6},{6,5},{7,4},{8,11},{9,10},{10,... | collective-permute-start | bytes 1044488 | tf_op jit(solution)/shard_map/ppermute | solution.py:51
  79.2 28.9 %collective-permute-start.5 = (bf16[2,40,3968]{2,1,0:T(8,128)(2,1)S(1)}, bf16[2,40,3968]{2,1,0:T(8,128)(2,1)S(1)}, u32[]{:S(2)}, u32[]{:S(2)}) collective-permute-start(bf16[2,40,3968]{2,1,0:T(8,128)(2,1)S(1)} %slice.284), channel_id=1, source_target_pairs={{0,8},{4,12},{8,0},{12,4},{16,24},{20,28},{24,16},{28,20},{1,9},{5... | collective-permute-start | bytes 1904648 | tf_op jit(solution)/shard_map/ppermute | solution.py:46
  105.1 27.9 %collective-permute-start.6 = (bf16[2,40,3968]{2,1,0:T(8,128)(2,1)S(1)}, bf16[2,40,3968]{2,1,0:T(8,128)(2,1)S(1)}, u32[]{:S(2)}, u32[]{:S(2)}) collective-permute-start(bf16[2,40,3968]{2,1,0:T(8,128)(2,1)S(1)} %slice.285), channel_id=1, source_target_pairs={{0,16},{4,20},{8,24},{12,28},{16,0},{20,4},{24,8},{28,12},{1,17},{... | collective-permute-start | bytes 1904648 | tf_op jit(solution)/shard_map/ppermute | solution.py:46
  108.1 40.5 %collective-permute-start.8 = (bf16[40,4352]{1,0:T(8,128)(2,1)S(1)}, bf16[40,4352]{1,0:T(8,128)(2,1)S(1)}, u32[]{:S(2)}, u32[]{:S(2)}) collective-permute-start(bf16[40,4352]{1,0:T(8,128)(2,1)S(1)} %copy-done.55), channel_id=1, source_target_pairs={{0,2},{1,3},{2,0},{3,1},{4,6},{5,7},{6,4},{7,5},{8,10},{9,11},{10,... | collective-permute-start | bytes 1044488 | tf_op jit(solution)/shard_map/ppermute | solution.py:51
  158.5 141.3 %all-gather.11.cloned.1.call-start = ((), (), s32[]{:S(2)}) async-start(), calls=%async_computation.9 | async-start | bytes 2867200 | tf_op jit(solution)/shard_map/all_gather | solution.py:424
  165.1 217.6 %all-gather.13.cloned.1.call-start = ((), (), s32[]{:S(2)}) async-start(), calls=%async_computation.10 | async-start | bytes 5734400 | tf_op jit(solution)/shard_map/all_gather | solution.py:423
  167.4 45.2 %collective-permute-start.14 = (bf16[4,40,4352]{2,1,0:T(8,128)(2,1)S(1)}, bf16[4,40,4352]{2,1,0:T(8,128)(2,1)S(1)}, u32[]{:S(2)}, u32[]{:S(2)}) collective-permute-start(bf16[4,40,4352]{2,1,0:T(8,128)(2,1)S(1)} %bitcast_dynamic-update-slice_fusion.16), channel_id=1, source_target_pairs={{0,16},{4,20},{8,24},{12,28},{16,0},{20,4},{24,8},{28,12},{1,17},{... | collective-permute-start | bytes 4177928 | tf_op jit(solution)/shard_map/ppermute | solution.py:46
  169.1 43.6 %collective-permute-start.13 = (bf16[4,40,4352]{2,1,0:T(8,128)(2,1)S(1)}, bf16[4,40,4352]{2,1,0:T(8,128)(2,1)}, u32[]{:S(2)}, u32[]{:S(2)}) collective-permute-start(bf16[4,40,4352]{2,1,0:T(8,128)(2,1)S(1)} %bitcast_dynamic-update-slice_fusion.16), channel_id=1, source_target_pairs={{0,8},{4,12},{8,0},{12,4},{16,24},{20,28},{24,16},{28,20},{1,9},{5... | collective-permute-start | bytes 4177928 | tf_op jit(solution)/shard_map/ppermute | solution.py:46
  169.6 261.3 %all-gather.15.cloned.1.call-start = ((), (), s32[]{:S(2)}) async-start(), calls=%async_computation.11 | async-start | bytes 2867200 | tf_op jit(solution)/shard_map/all_gather | solution.py:424
  243.3 237.4 %reduce-scatter.5.cloned.1.call-start = ((), (), s32[]{:S(2)}) async-start(), calls=%async_computation.4 | async-start | bytes 2867200 | tf_op jit(solution)/shard_map/reduce_scatter | solution.py:521
  319.7 27.3 %collective-permute-start.33 = (bf16[2,2,4,40,3072]{4,3,2,1,0:T(8,128)(2,1)}, bf16[2,2,4,40,3072]{4,3,2,1,0:T(8,128)(2,1)}, u32[]{:S(2)}, u32[]{:S(2)}) collective-permute-start(bf16[2,2,4,40,3072]{4,3,2,1,0:T(8,128)(2,1)} %dynamic-slice_bitcast_fusion), channel_id=1, source_target_pairs={{0,4},{4,0},{8,12},{12,8},{16,20},{20,16},{24,28},{28,24},{1,5},{5... | collective-permute-start | bytes 11796488 | tf_op jit(solution)/shard_map/ppermute | solution.py:46
  354.3 28.4 %collective-permute-start.35 = (bf16[2,2,40,3072]{3,2,1,0:T(8,128)(2,1)}, bf16[2,2,40,3072]{3,2,1,0:T(8,128)(2,1)S(1)}, u32[]{:S(2)}, u32[]{:S(2)}) collective-permute-start(bf16[2,2,40,3072]{3,2,1,0:T(8,128)(2,1)} %get-tuple-element.339), channel_id=1, source_target_pairs={{0,16},{4,20},{8,24},{12,28},{16,0},{20,4},{24,8},{28,12},{1,17},{... | collective-permute-start | bytes 2949128 | tf_op jit(solution)/shard_map/ppermute | solution.py:46
  413.1 153.2 %reduce-scatter.7.cloned.1.call-start = ((), (), s32[]{:S(2)}) async-start(), calls=%async_computation.5 | async-start | bytes 5734400 | tf_op jit(solution)/shard_map/reduce_scatter | solution.py:521
  459.5 35.6 %collective-permute-start.37 = (bf16[4,272,1280]{2,1,0:T(8,128)(2,1)}, bf16[4,272,1280]{2,1,0:T(8,128)(2,1)}, u32[]{:S(2)}, u32[]{:S(2)}) collective-permute-start(bf16[4,272,1280]{2,1,0:T(8,128)(2,1)} %fusion.28), channel_id=1, source_target_pairs={{0,4},{4,0},{8,12},{12,8},{16,20},{20,16},{24,28},{28,24},{1,5},{5... | collective-permute-start | bytes 8355848 | tf_op jit(solution)/shard_map/ppermute | solution.py:46
  472.1 184.4 %reduce-scatter.9.cloned.1.call-start = ((), (), s32[]{:S(2)}) async-start(), calls=%async_computation.6 | async-start | bytes 2867200 | tf_op jit(solution)/shard_map/reduce_scatter | solution.py:521
  565.8 232.9 %reduce-scatter.11.cloned.1.call-start = ((), (), s32[]{:S(2)}) async-start(), calls=%async_computation.7 | async-start | bytes 5734400 | tf_op jit(solution)/shard_map/reduce_scatter | solution.py:521
  578.5 113.8 %collective-permute-start.63 = (bf16[2,40,3072]{2,1,0:T(8,128)(2,1)}, bf16[2,40,3072]{2,1,0:T(8,128)(2,1)}, u32[]{:S(2)}, u32[]{:S(2)}) collective-permute-start(bf16[2,40,3072]{2,1,0:T(8,128)(2,1)} %get-tuple-element.364), channel_id=1, source_target_pairs={{0,1},{1,0},{2,3},{3,2},{4,5},{5,4},{6,7},{7,6},{8,9},{9,8},{10,11... | collective-permute-start | bytes 1474568 | tf_op jit(solution)/shard_map/ppermute | solution.py:51
  620.6 34.1 %collective-permute-start.56 = (bf16[2,40,1280]{2,1,0:T(8,128)(2,1)}, bf16[2,40,1280]{2,1,0:T(8,128)(2,1)}, u32[]{:S(2)}, u32[]{:S(2)}) collective-permute-start(bf16[2,40,1280]{2,1,0:T(8,128)(2,1)} %get-tuple-element.396), channel_id=1, source_target_pairs={{0,8},{4,12},{8,0},{12,4},{16,24},{20,28},{24,16},{28,20},{1,9},{5... | collective-permute-start | bytes 614408 | tf_op jit(solution)/shard_map/ppermute | solution.py:46
  622.1 32.7 %collective-permute-start.55 = (bf16[2,40,1280]{2,1,0:T(8,128)(2,1)}, bf16[2,40,1280]{2,1,0:T(8,128)(2,1)}, u32[]{:S(2)}, u32[]{:S(2)}) collective-permute-start(bf16[2,40,1280]{2,1,0:T(8,128)(2,1)} %get-tuple-element.398), channel_id=1, source_target_pairs={{0,16},{4,20},{8,24},{12,28},{16,0},{20,4},{24,8},{28,12},{1,17},{... | collective-permute-start | bytes 614408 | tf_op jit(solution)/shard_map/ppermute | solution.py:46
  646.5 124.7 %collective-permute-start.52 = (bf16[256,1280]{1,0:T(8,128)(2,1)}, bf16[256,1280]{1,0:T(8,128)(2,1)}, u32[]{:S(2)}, u32[]{:S(2)}) collective-permute-start(bf16[256,1280]{1,0:T(8,128)(2,1)} %get-tuple-element.332), channel_id=1, source_target_pairs={{3,0},{7,4},{11,8},{15,12},{19,16},{23,20},{27,24},{31,28}} | collective-permute-start | bytes 1966088 | tf_op jit(solution)/shard_map/ppermute | solution.py:654
  686.7 84.8 %collective-permute-start.51 = (bf16[256,1280]{1,0:T(8,128)(2,1)S(1)}, bf16[256,1280]{1,0:T(8,128)(2,1)S(1)}, u32[]{:S(2)}, u32[]{:S(2)}) collective-permute-start(bf16[256,1280]{1,0:T(8,128)(2,1)S(1)} %copy-done.64), channel_id=1, source_target_pairs={{2,0},{3,1},{6,4},{7,5},{10,8},{11,9},{14,12},{15,13},{18,16},{19,... | collective-permute-start | bytes 1966088 | tf_op jit(solution)/shard_map/ppermute | solution.py:654
  693.0 78.5 %collective-permute-start.50 = (bf16[256,1280]{1,0:T(8,128)(2,1)S(1)}, bf16[256,1280]{1,0:T(8,128)(2,1)S(1)}, u32[]{:S(2)}, u32[]{:S(2)}) collective-permute-start(bf16[256,1280]{1,0:T(8,128)(2,1)S(1)} %copy-done.63), channel_id=1, source_target_pairs={{1,0},{2,1},{3,2},{5,4},{6,5},{7,6},{9,8},{10,9},{11,10},{13,12},{... | collective-permute-start | bytes 1966088 | tf_op jit(solution)/shard_map/ppermute | solution.py:654
  712.4 49.4 %collective-permute-start.66 = (bf16[2,40,1408]{2,1,0:T(8,128)(2,1)S(1)}, bf16[2,40,1408]{2,1,0:T(8,128)(2,1)S(1)}, u32[]{:S(2)}, u32[]{:S(2)}) collective-permute-start(bf16[2,40,1408]{2,1,0:T(8,128)(2,1)S(1)} %get-tuple-element.394), channel_id=1, source_target_pairs={{0,16},{4,20},{8,24},{12,28},{16,0},{20,4},{24,8},{28,12},{1,17},{... | collective-permute-start | bytes 675848 | tf_op jit(solution)/shard_map/ppermute | solution.py:46
  713.2 47.1 %collective-permute-start.72 = (bf16[2,40,2560]{2,1,0:T(8,128)(2,1)S(1)}, bf16[2,40,2560]{2,1,0:T(8,128)(2,1)S(1)}, u32[]{:S(2)}, u32[]{:S(2)}) collective-permute-start(bf16[2,40,2560]{2,1,0:T(8,128)(2,1)S(1)} %dynamic-slice_bitcast_fusion.34), channel_id=1, source_target_pairs={{0,1},{1,0},{2,3},{3,2},{4,5},{5,4},{6,7},{7,6},{8,9},{9,8},{10,11... | collective-permute-start | bytes 1228808 | tf_op jit(solution)/shard_map/ppermute | solution.py:51
  767.6 34.0 %collective-permute-start.68 = (bf16[40,3072]{1,0:T(8,128)(2,1)}, bf16[40,3072]{1,0:T(8,128)(2,1)}, u32[]{:S(2)}, u32[]{:S(2)}) collective-permute-start(bf16[40,3072]{1,0:T(8,128)(2,1)} %dynamic-slice_bitcast_fusion.52), channel_id=1, source_target_pairs={{0,2},{1,3},{2,0},{3,1},{4,6},{5,7},{6,4},{7,5},{8,10},{9,11},{10,... | collective-permute-start | bytes 737288 | tf_op jit(solution)/shard_map/ppermute | solution.py:51
  (169 other events, 1927.7 us)
Sparse Core Ops, SparseCore 0:
  158.7 84.5 all-gather.8
  245.4 47.8 all-gather.10
  294.9 86.0 all-gather.12
  383.0 47.8 all-gather.14
  433.6 45.8 reduce-scatter.4
  481.8 82.5 reduce-scatter.6
  567.4 57.8 reduce-scatter.8
  628.1 124.1 reduce-scatter.10

commit v5 on v4

--- a/solution.py
+++ b/solution.py
@@ -627,8 +627,8 @@
     query_grad, key_grad, value_grad = attend_back(
         queries, keys, values, attended_grad, cosine, sine, key_pos[:, None], query_pos[None, :]
     )
-    *attn_state, query_grad, key_grad, value_grad = after(
-        *attn_state, query_grad, key_grad, value_grad
+    *attn_state, query_grad, key_grad, value_grad, out_parts[-1] = after(
+        *attn_state, query_grad, key_grad, value_grad, out_parts[-1]
     )
     attn_state = split_far(*attn_state)
     pair_kept, pair_core = rows_core(
@@ -654,7 +654,7 @@
         lax.ppermute(parts[k].astype(bf16), "dp", [(i, i - k) for i in range(k, places)])
         for k in range(1, places)
     ]
-    pair_core, gain_attn_grad, out_parts[-1] = after(pair_core, gain_attn_grad, out_parts[-1])
+    pair_core, gain_attn_grad = after(pair_core, gain_attn_grad)
     pair_state = rows_near(pair_kept, pair_core)
     small_grad = jnp.concatenate(
         [

time: 834 us -> 833 us (level)
    ppermute x14, waiting for transfers between devices: 120 us -> 93.8 us  [flip_dp(): return lax.ppermute(x, 'dp', [(i, i ^ bit) for i in range(count)])]
    reduce_scatter x4, waiting for transfers between devices: 0.02 us -> 17.3 us  [reduce_places(): lax.psum_scatter(grad.astype(bf16), 'dp', scatter_dimension=0, tiled=True)]
    unnamed x238 -> x226, local copies, waits for them, and re-layouts: 19 us -> 18.6 us
  transfers between devices with their start and end apart: 83 -> 83, of which waited for: 34 -> 33; matrix products, arithmetic and copies ran while one was open for 43% -> 45% of each run, Pallas kernels for 11% -> 11%
where the time goes in v5:
time: 833 us; the launch traced here: 826 us
  waiting for transfers between devices  203 us (24%)
  matrix products  158 us (19%)
  local copies, waits for them, and re-layouts  126 us (15%)
  other arithmetic  117 us (14%)
  starting transfers between devices  111 us (13%)
  Pallas kernels  93.6 us (11%)
  between operations  16.6 us (2%)
    ppermute x14, waiting for transfers between devices, flip_dp(): return lax.ppermute(x, 'dp', [(i, i ^ bit) for i in range(count)])  93.8 us
    ppermute x55, waiting for transfers between devices, flip(): return lax.ppermute(x, 'ep', [(i, i ^ bit) for i in range(count)])  91.6 us
    dot_general x11, matrix products, contract_rows(): lax.dot_general(left_side, right_side, (((0,), (0,)), ((), ())), preferre...  62.8 us
    dot_general x10, matrix products, times_transposed(): lax.dot_general(left_side, right_side, (((1,), (1,)), ((), ())), preferre...  61.8 us
    ppermute x14, starting transfers between devices, flip_dp(): return lax.ppermute(x, 'dp', [(i, i ^ bit) for i in range(count)])  50.2 us
    ppermute x55, starting transfers between devices, flip(): return lax.ppermute(x, 'ep', [(i, i ^ bit) for i in range(count)])  47.2 us
    pallas_call x2, Pallas kernels, expert_forward(): pl.pallas_call(expert_kernel, grid=(count // step,), in_specs=[rows(width...  31.8 us
    dot_general x6, matrix products, matmul(): return jnp.dot(left_side, right_side, preferred_element_type=f32)  30.7 us
  transfers between devices with their start and end apart: 83, of which 33 were waited for; matrix products, arithmetic and copies ran while one was open for 45% of the time, Pallas kernels for 11%

profile of v5, /device:TPU:0, one launch (start us, length us, event | category | flops | bytes accessed | tf_op | source)
XLA Modules:
  0.0 825.5 jit_solution(10084590873589842902)
XLA Ops:
  23.6 18.7 %collective-permute-done.1 = bf16[40,3968]{1,0:T(8,128)(2,1)} collective-permute-done((bf16[40,3968]{1,0:T(8,128)(2,1)S(1)}, bf16[40,3968]{1,0:T(8,128)(2,1)}, u32[]{:S(2)}, u32[]{:S(2)}) %collective-permute-start.1) | collective-permute-done | bytes 317472 | tf_op jit(solution)/shard_map/ppermute | solution.py:51
  65.6 10.2 %collective-permute-done.4 = bf16[4,40,3968]{2,1,0:T(8,128)(2,1)} collective-permute-done((bf16[4,40,3968]{2,1,0:T(8,128)(2,1)}, bf16[4,40,3968]{2,1,0:T(8,128)(2,1)}, u32[]{:S(2)}, u32[]{:S(2)}) %collective-permute-start.4) | collective-permute-done | bytes 1269792 | tf_op jit(solution)/shard_map/ppermute | solution.py:46
  84.3 20.8 %collective-permute-done.9 = bf16[40,4352]{1,0:T(8,128)(2,1)} collective-permute-done((bf16[40,4352]{1,0:T(8,128)(2,1)S(1)}, bf16[40,4352]{1,0:T(8,128)(2,1)}, u32[]{:S(2)}, u32[]{:S(2)}) %collective-permute-start.9) | collective-permute-done | bytes 348192 | tf_op jit(solution)/shard_map/ppermute | solution.py:51
  108.1 24.9 %collective-permute-start.8 = (bf16[40,4352]{1,0:T(8,128)(2,1)S(1)}, bf16[40,4352]{1,0:T(8,128)(2,1)S(1)}, u32[]{:S(2)}, u32[]{:S(2)}) collective-permute-start(bf16[40,4352]{1,0:T(8,128)(2,1)S(1)} %copy-done.52), channel_id=1, source_target_pairs={{0,2},{1,3},{2,0},{3,1},{4,6},{5,7},{6,4},{7,5},{8,10},{9,11},{10,... | collective-permute-start | bytes 1044488 | tf_op jit(solution)/shard_map/ppermute | solution.py:51
  133.0 11.2 %collective-permute-start.7 = (bf16[40,4352]{1,0:T(8,128)(2,1)S(1)}, bf16[40,4352]{1,0:T(8,128)(2,1)S(1)}, u32[]{:S(2)}, u32[]{:S(2)}) collective-permute-start(bf16[40,4352]{1,0:T(8,128)(2,1)S(1)} %copy-done.52), channel_id=1, source_target_pairs={{0,1},{1,0},{2,3},{3,2},{4,5},{5,4},{6,7},{7,6},{8,9},{9,8},{10,11... | collective-permute-start | bytes 1044488 | tf_op jit(solution)/shard_map/ppermute | solution.py:51
  148.6 7.4 collective-permute-done.7
  193.0 19.6 %shard_map.186 = (bf16[256,1280]{1,0:T(8,128)(2,1)}, bf16[256,1280]{1,0:T(8,128)(2,1)}, bf16[1024,1280]{1,0:T(8,128)(2,1)}, bf16[1024,1280]{1,0:T(8,128)(2,1)}) custom-call(bf16[1024,1280]{1,0:T(8,128)(2,1)} %multiply_convert_fusion.x_ref, bf16[1280,3968]{1,0:T(8,128)(2,1)} %bitcast.356, bf16[1280,3968]{1,0:T(8,128)(2,1)} %bitcast.357, ...), custom_call_target="tpu_custom_call" | custom-call | flops 8891924480 | bytes 17694720 | tf_op jit(solution)/shard_map/pallas_call | solution.py:241
  219.7 11.7 %collective-permute-done.16 = bf16[2,40,4352]{2,1,0:T(8,128)(2,1)S(1)} collective-permute-done((bf16[2,40,4352]{2,1,0:T(8,128)(2,1)S(1)}, bf16[2,40,4352]{2,1,0:T(8,128)(2,1)S(1)}, u32[]{:S(2)}, u32[]{:S(2)}) %collective-permute-start.16) | collective-permute-done | bytes 696352 | tf_op jit(solution)/shard_map/ppermute | solution.py:46
  301.8 7.9 pad_maximum_fusion
  330.7 16.1 %shard_map.187 = (bf16[2048,1792]{1,0:T(8,128)(2,1)}, bf16[2048,896]{1,0:T(8,128)(2,1)S(1)}) custom-call(bf16[2048,1280]{1,0:T(8,128)(2,1)} %bitcast.375, bf16[1280,1792]{1,0:T(8,128)(2,1)} %bitcast.425), custom_call_target="tpu_custom_call" | custom-call | flops 9395240960 | bytes 12582912 | tf_op jit(solution)/shard_map/pallas_call | solution.py:312
  364.6 6.5 convolution_convert_fusion.11
  371.1 11.6 %shard_map.188 = bf16[2048,1792]{1,0:T(8,128)(2,1)} custom-call(bf16[2048,1280]{1,0:T(8,128)(2,1)} %copy-done.9, bf16[896,1280]{1,0:T(8,128)(2,1)S(1)} %bitcast.351, bf16[2048,1792]{1,0:T(8,128)(2,1)} %get-tuple-element.195.pre_ref), custom_call_target="tpu_custom_call" | custom-call | flops 4697620480 | bytes 12582912 | tf_op jit(solution)/shard_map/pallas_call | solution.py:344
  382.6 15.6 %convolution_convert_fusion.9 = bf16[1280,1792]{1,0:T(8,128)(2,1)} fusion(bf16[2048,1280]{1,0:T(8,128)(2,1)} %bitcast.376, bf16[2048,1792]{1,0:T(8,128)(2,1)} %shard_map.188), kind=kOutput, calls=%fused_computation.20 | convolution fusion | flops 9397534720 | bytes 17170432 | tf_op jit(solution)/shard_map/dot_general | solution.py:22
  398.2 14.8 %convolution_convert_fusion.8 = bf16[2048,1280]{1,0:T(8,128)(2,1)} fusion(bf16[2048,1792]{1,0:T(8,128)(2,1)} %shard_map.188, bf16[1280,1792]{1,0:T(8,128)(2,1)} %bitcast.426), kind=kOutput, calls=%fused_computation.19 | convolution fusion | flops 9397862400 | bytes 17170432 | tf_op jit(solution)/shard_map/dot_general | solution.py:28
  413.1 15.7 %shard_map.189 = (bf16[2048,1792]{1,0:T(8,128)(2,1)}, bf16[2048,896]{1,0:T(8,128)(2,1)S(1)}) custom-call(bf16[2048,1280]{1,0:T(8,128)(2,1)} %bitcast.377, bf16[1280,1792]{1,0:T(8,128)(2,1)} %bitcast.420), custom_call_target="tpu_custom_call" | custom-call | flops 9395240960 | bytes 12582912 | tf_op jit(solution)/shard_map/pallas_call | solution.py:312
  430.8 8.1 convolution_convert_fusion
  439.0 13.4 %fusion.1 = (f32[2048]{0:T(1024)S(1)}, f32[2048]{0:T(1024)S(1)}, bf16[2048,1280]{1,0:T(8,128)(2,1)}, bf16[2048,1280]{1,0:T(8,128)(2,1)}) fusion(bf16[8,256,1280]{2,1,0:T(8,128)(2,1)} %copy-done.8, bf16[2048,1280]{1,0:T(8,128)(2,1)S(1)} %convolution_convert_fusion, f32[2048]{0:T(1024)S(1)} %get-tuple-element.306, bf16[2048,896]{1,0:T(8,128)(2,1)S(1)} %copy-done.5, ...), kind=kOutput, calls=%fused_computation.5 | convolution fusion | flops 4723830784 | bytes 26959872 | tf_op jit(solution)/shard_map/dot_general | solution.py:34
  482.8 12.2 %shard_map.190 = bf16[2048,1792]{1,0:T(8,128)(2,1)} custom-call(bf16[2048,1280]{1,0:T(8,128)(2,1)} %get-tuple-element.221.grad_ref, bf16[896,1280]{1,0:T(8,128)(2,1)S(1)} %bitcast.354, bf16[2048,1792]{1,0:T(8,128)(2,1)} %get-tuple-element.205.pre_ref), custom_call_target="tpu_custom_call" | custom-call | flops 4697620480 | bytes 12582912 | tf_op jit(solution)/shard_map/pallas_call | solution.py:344
  501.0 7.6 add_convert_fusion.4
  508.6 6.5 collective-permute-done.40
  518.7 7.0 add_convert_fusion.3
  531.1 6.4 convolution_convert_fusion.10
  550.3 15.4 %convolution_convert_fusion.7 = bf16[1280,1792]{1,0:T(8,128)(2,1)} fusion(bf16[2048,1280]{1,0:T(8,128)(2,1)} %bitcast.378, bf16[2048,1792]{1,0:T(8,128)(2,1)} %shard_map.190), kind=kOutput, calls=%fused_computation.18 | convolution fusion | flops 9397534720 | bytes 17170432 | tf_op jit(solution)/shard_map/dot_general | solution.py:22
  589.6 18.4 %shard_map.191 = (bf16[256,1280]{1,0:T(8,128)(2,1)}, bf16[1024,1280]{1,0:T(8,128)(2,1)}, bf16[1024,1280]{1,0:T(8,128)(2,1)}) custom-call(bf16[256,1280]{1,0:T(8,128)(2,1)} %get-tuple-element.236.q_ref, bf16[1024,1280]{1,0:T(8,128)(2,1)} %get-tuple-element.237.k_ref, bf16[1024,1280]{1,0:T(8,128)(2,1)} %get-tuple-element.238.v_ref, ...), custom_call_target="tpu_custom_call" | custom-call | flops 3355443200 | bytes 10485760 | tf_op jit(solution)/shard_map/pallas_call | solution.py:284
  608.0 17.3 %reduce-scatter.9.cloned.1.call-done = bf16[224,1280]{1,0:T(8,128)(2,1)} async-done(((bf16[896,1280]{1,0:T(8,128)(2,1)}), bf16[224,1280]{1,0:T(8,128)(2,1)}) %reduce-scatter.9.cloned.1.call-update) | async-done | bytes 573456 | tf_op jit(solution)/shard_map/reduce_scatter | solution.py:521
  633.1 7.9 fusion.16
  657.0 9.6 %multiply_reduce_fusion = (f32[1280]{0:T(1024)S(1)}, bf16[1024,1280]{1,0:T(8,128)(2,1)S(1)}, f32[1024,1280]{1,0:T(8,128)}, f32[1024,1280]{1,0:T(8,128)}) fusion(f32[1024]{0:T(1024)S(1)} %copy-done.89, bf16[256,1280]{1,0:T(8,128)(2,1)S(1)} %copy-done.38, bf16[256,1280]{1,0:T(8,128)(2,1)} %copy-done.39, bf16[256,1280]{1,0:T(8,128)(2,1)} %copy-done.41, ...), kind=kOutput, calls=%fused_computation.33 | convolution fusion | flops 3372481280 | bytes 26878976 | tf_op jit(solution)/shard_map/dot_general | solution.py:28
  690.3 17.3 %collective-permute-done.58 = bf16[2,2,40,2560]{3,2,1,0:T(8,128)(2,1)S(1)} collective-permute-done((bf16[2,2,40,2560]{3,2,1,0:T(8,128)(2,1)S(1)}, bf16[2,2,40,2560]{3,2,1,0:T(8,128)(2,1)S(1)}, u32[]{:S(2)}, u32[]{:S(2)}) %collective-permute-start.58) | collective-permute-done | bytes 819232 | tf_op jit(solution)/shard_map/ppermute | solution.py:46
  712.9 8.4 %collective-permute-done.60 = bf16[2,2,40,1408]{3,2,1,0:T(8,128)(2,1)S(1)} collective-permute-done((bf16[2,2,40,1408]{3,2,1,0:T(8,128)(2,1)S(1)}, bf16[2,2,40,1408]{3,2,1,0:T(8,128)(2,1)S(1)}, u32[]{:S(2)}, u32[]{:S(2)}) %collective-permute-start.60) | collective-permute-done | bytes 450592 | tf_op jit(solution)/shard_map/ppermute | solution.py:46
  723.1 8.0 collective-permute-done.64
  739.6 20.7 %collective-permute-done.72 = bf16[2,40,2560]{2,1,0:T(8,128)(2,1)} collective-permute-done((bf16[2,40,2560]{2,1,0:T(8,128)(2,1)}, bf16[2,40,2560]{2,1,0:T(8,128)(2,1)}, u32[]{:S(2)}, u32[]{:S(2)}) %collective-permute-start.72) | collective-permute-done | bytes 409632 | tf_op jit(solution)/shard_map/ppermute | solution.py:51
  777.4 12.2 %collective-permute-done.73 = bf16[40,2560]{1,0:T(8,128)(2,1)S(1)} collective-permute-done((bf16[40,2560]{1,0:T(8,128)(2,1)S(1)}, bf16[40,2560]{1,0:T(8,128)(2,1)S(1)}, u32[]{:S(2)}, u32[]{:S(2)}) %collective-permute-start.73) | collective-permute-done | bytes 204832 | tf_op jit(solution)/shard_map/ppermute | solution.py:51
  (642 shorter events, 400.2 us)
Async XLA Ops:
  7.2 248.8 %all-gather.9.cloned.1.call-start = ((), (), s32[]{:S(2)}) async-start(), calls=%async_computation.8 | async-start | bytes 5734400 | tf_op jit(solution)/shard_map/all_gather | solution.py:423
  46.5 29.3 %collective-permute-start.4 = (bf16[4,40,3968]{2,1,0:T(8,128)(2,1)}, bf16[4,40,3968]{2,1,0:T(8,128)(2,1)}, u32[]{:S(2)}, u32[]{:S(2)}) collective-permute-start(bf16[4,40,3968]{2,1,0:T(8,128)(2,1)} %bitcast_dynamic-update-slice_fusion.20), channel_id=1, source_target_pairs={{0,16},{4,20},{8,24},{12,28},{16,0},{20,4},{24,8},{28,12},{1,17},{... | collective-permute-start | bytes 3809288 | tf_op jit(solution)/shard_map/ppermute | solution.py:46
  48.0 31.2 %collective-permute-start.3 = (bf16[4,40,3968]{2,1,0:T(8,128)(2,1)}, bf16[4,40,3968]{2,1,0:T(8,128)(2,1)}, u32[]{:S(2)}, u32[]{:S(2)}) collective-permute-start(bf16[4,40,3968]{2,1,0:T(8,128)(2,1)} %bitcast_dynamic-update-slice_fusion.20), channel_id=1, source_target_pairs={{0,8},{4,12},{8,0},{12,4},{16,24},{20,28},{24,16},{28,20},{1,9},{5... | collective-permute-start | bytes 3809288 | tf_op jit(solution)/shard_map/ppermute | solution.py:46
  52.2 103.8 %collective-permute-start.12 = (bf16[256,1280]{1,0:T(8,128)(2,1)}, bf16[256,1280]{1,0:T(8,128)(2,1)S(1)}, u32[]{:S(2)}, u32[]{:S(2)}) collective-permute-start(bf16[256,1280]{1,0:T(8,128)(2,1)} %param.11), channel_id=1, source_target_pairs={{0,3},{4,7},{8,11},{12,15},{16,19},{20,23},{24,27},{28,31}} | collective-permute-start | bytes 1966088 | tf_op jit(solution)/shard_map/ppermute | solution.py:74
  56.7 99.2 %collective-permute-start.11 = (bf16[256,1280]{1,0:T(8,128)(2,1)}, bf16[256,1280]{1,0:T(8,128)(2,1)S(1)}, u32[]{:S(2)}, u32[]{:S(2)}) collective-permute-start(bf16[256,1280]{1,0:T(8,128)(2,1)} %param.11), channel_id=1, source_target_pairs={{0,2},{1,3},{4,6},{5,7},{8,10},{9,11},{12,14},{13,15},{16,18},{17,... | collective-permute-start | bytes 1966088 | tf_op jit(solution)/shard_map/ppermute | solution.py:74
  58.1 98.6 %collective-permute-start.10 = (bf16[256,1280]{1,0:T(8,128)(2,1)}, bf16[256,1280]{1,0:T(8,128)(2,1)S(1)}, u32[]{:S(2)}, u32[]{:S(2)}) collective-permute-start(bf16[256,1280]{1,0:T(8,128)(2,1)} %param.11), channel_id=1, source_target_pairs={{0,1},{1,2},{2,3},{4,5},{5,6},{6,7},{8,9},{9,10},{10,11},{12,13},{... | collective-permute-start | bytes 1966088 | tf_op jit(solution)/shard_map/ppermute | solution.py:74
  75.7 29.4 %collective-permute-start.9 = (bf16[40,4352]{1,0:T(8,128)(2,1)S(1)}, bf16[40,4352]{1,0:T(8,128)(2,1)}, u32[]{:S(2)}, u32[]{:S(2)}) collective-permute-start(bf16[40,4352]{1,0:T(8,128)(2,1)S(1)} %copy-done.52), channel_id=1, source_target_pairs={{0,3},{1,2},{2,1},{3,0},{4,7},{5,6},{6,5},{7,4},{8,11},{9,10},{10,... | collective-permute-start | bytes 1044488 | tf_op jit(solution)/shard_map/ppermute | solution.py:51
  79.2 28.9 %collective-permute-start.5 = (bf16[2,40,3968]{2,1,0:T(8,128)(2,1)S(1)}, bf16[2,40,3968]{2,1,0:T(8,128)(2,1)S(1)}, u32[]{:S(2)}, u32[]{:S(2)}) collective-permute-start(bf16[2,40,3968]{2,1,0:T(8,128)(2,1)S(1)} %slice.284), channel_id=1, source_target_pairs={{0,8},{4,12},{8,0},{12,4},{16,24},{20,28},{24,16},{28,20},{1,9},{5... | collective-permute-start | bytes 1904648 | tf_op jit(solution)/shard_map/ppermute | solution.py:46
  105.1 27.9 %collective-permute-start.6 = (bf16[2,40,3968]{2,1,0:T(8,128)(2,1)S(1)}, bf16[2,40,3968]{2,1,0:T(8,128)(2,1)S(1)}, u32[]{:S(2)}, u32[]{:S(2)}) collective-permute-start(bf16[2,40,3968]{2,1,0:T(8,128)(2,1)S(1)} %slice.285), channel_id=1, source_target_pairs={{0,16},{4,20},{8,24},{12,28},{16,0},{20,4},{24,8},{28,12},{1,17},{... | collective-permute-start | bytes 1904648 | tf_op jit(solution)/shard_map/ppermute | solution.py:46
  108.1 40.5 %collective-permute-start.8 = (bf16[40,4352]{1,0:T(8,128)(2,1)S(1)}, bf16[40,4352]{1,0:T(8,128)(2,1)S(1)}, u32[]{:S(2)}, u32[]{:S(2)}) collective-permute-start(bf16[40,4352]{1,0:T(8,128)(2,1)S(1)} %copy-done.52), channel_id=1, source_target_pairs={{0,2},{1,3},{2,0},{3,1},{4,6},{5,7},{6,4},{7,5},{8,10},{9,11},{10,... | collective-permute-start | bytes 1044488 | tf_op jit(solution)/shard_map/ppermute | solution.py:51
  158.5 141.3 %all-gather.11.cloned.1.call-start = ((), (), s32[]{:S(2)}) async-start(), calls=%async_computation.9 | async-start | bytes 2867200 | tf_op jit(solution)/shard_map/all_gather | solution.py:424
  165.0 217.6 %all-gather.13.cloned.1.call-start = ((), (), s32[]{:S(2)}) async-start(), calls=%async_computation.10 | async-start | bytes 5734400 | tf_op jit(solution)/shard_map/all_gather | solution.py:423
  167.4 45.2 %collective-permute-start.14 = (bf16[4,40,4352]{2,1,0:T(8,128)(2,1)S(1)}, bf16[4,40,4352]{2,1,0:T(8,128)(2,1)S(1)}, u32[]{:S(2)}, u32[]{:S(2)}) collective-permute-start(bf16[4,40,4352]{2,1,0:T(8,128)(2,1)S(1)} %bitcast_dynamic-update-slice_fusion.16), channel_id=1, source_target_pairs={{0,16},{4,20},{8,24},{12,28},{16,0},{20,4},{24,8},{28,12},{1,17},{... | collective-permute-start | bytes 4177928 | tf_op jit(solution)/shard_map/ppermute | solution.py:46
  169.0 43.6 %collective-permute-start.13 = (bf16[4,40,4352]{2,1,0:T(8,128)(2,1)S(1)}, bf16[4,40,4352]{2,1,0:T(8,128)(2,1)}, u32[]{:S(2)}, u32[]{:S(2)}) collective-permute-start(bf16[4,40,4352]{2,1,0:T(8,128)(2,1)S(1)} %bitcast_dynamic-update-slice_fusion.16), channel_id=1, source_target_pairs={{0,8},{4,12},{8,0},{12,4},{16,24},{20,28},{24,16},{28,20},{1,9},{5... | collective-permute-start | bytes 4177928 | tf_op jit(solution)/shard_map/ppermute | solution.py:46
  169.6 261.3 %all-gather.15.cloned.1.call-start = ((), (), s32[]{:S(2)}) async-start(), calls=%async_computation.11 | async-start | bytes 2867200 | tf_op jit(solution)/shard_map/all_gather | solution.py:424
  243.4 237.3 %reduce-scatter.5.cloned.1.call-start = ((), (), s32[]{:S(2)}) async-start(), calls=%async_computation.4 | async-start | bytes 2867200 | tf_op jit(solution)/shard_map/reduce_scatter | solution.py:521
  354.2 28.4 %collective-permute-start.35 = (bf16[2,2,40,3072]{3,2,1,0:T(8,128)(2,1)}, bf16[2,2,40,3072]{3,2,1,0:T(8,128)(2,1)S(1)}, u32[]{:S(2)}, u32[]{:S(2)}) collective-permute-start(bf16[2,2,40,3072]{3,2,1,0:T(8,128)(2,1)} %get-tuple-element.339), channel_id=1, source_target_pairs={{0,16},{4,20},{8,24},{12,28},{16,0},{20,4},{24,8},{28,12},{1,17},{... | collective-permute-start | bytes 2949128 | tf_op jit(solution)/shard_map/ppermute | solution.py:46
  413.0 153.2 %reduce-scatter.7.cloned.1.call-start = ((), (), s32[]{:S(2)}) async-start(), calls=%async_computation.5 | async-start | bytes 5734400 | tf_op jit(solution)/shard_map/reduce_scatter | solution.py:521
  459.5 35.6 %collective-permute-start.37 = (bf16[4,272,1280]{2,1,0:T(8,128)(2,1)}, bf16[4,272,1280]{2,1,0:T(8,128)(2,1)}, u32[]{:S(2)}, u32[]{:S(2)}) collective-permute-start(bf16[4,272,1280]{2,1,0:T(8,128)(2,1)} %fusion.28), channel_id=1, source_target_pairs={{0,4},{4,0},{8,12},{12,8},{16,20},{20,16},{24,28},{28,24},{1,5},{5... | collective-permute-start | bytes 8355848 | tf_op jit(solution)/shard_map/ppermute | solution.py:46
  472.0 153.2 %reduce-scatter.9.cloned.1.call-start = ((), (), s32[]{:S(2)}) async-start(), calls=%async_computation.6 | async-start | bytes 2867200 | tf_op jit(solution)/shard_map/reduce_scatter | solution.py:521
  565.7 171.1 %reduce-scatter.11.cloned.1.call-start = ((), (), s32[]{:S(2)}) async-start(), calls=%async_computation.7 | async-start | bytes 5734400 | tf_op jit(solution)/shard_map/reduce_scatter | solution.py:521
  578.4 133.2 %collective-permute-start.63 = (bf16[2,40,3072]{2,1,0:T(8,128)(2,1)}, bf16[2,40,3072]{2,1,0:T(8,128)(2,1)}, u32[]{:S(2)}, u32[]{:S(2)}) collective-permute-start(bf16[2,40,3072]{2,1,0:T(8,128)(2,1)} %get-tuple-element.364), channel_id=1, source_target_pairs={{0,1},{1,0},{2,3},{3,2},{4,5},{5,4},{6,7},{7,6},{8,9},{9,8},{10,11... | collective-permute-start | bytes 1474568 | tf_op jit(solution)/shard_map/ppermute | solution.py:51
  583.6 43.8 %collective-permute-start.49 = (bf16[2,2,40,1280]{3,2,1,0:T(8,128)(2,1)}, bf16[2,2,40,1280]{3,2,1,0:T(8,128)(2,1)}, u32[]{:S(2)}, u32[]{:S(2)}) collective-permute-start(bf16[2,2,40,1280]{3,2,1,0:T(8,128)(2,1)} %get-tuple-element.378), channel_id=1, source_target_pairs={{0,16},{4,20},{8,24},{12,28},{16,0},{20,4},{24,8},{28,12},{1,17},{... | collective-permute-start | bytes 1228808 | tf_op jit(solution)/shard_map/ppermute | solution.py:46
  585.8 41.6 %collective-permute-start.48 = (bf16[2,2,40,1280]{3,2,1,0:T(8,128)(2,1)}, bf16[2,2,40,1280]{3,2,1,0:T(8,128)(2,1)}, u32[]{:S(2)}, u32[]{:S(2)}) collective-permute-start(bf16[2,2,40,1280]{3,2,1,0:T(8,128)(2,1)} %get-tuple-element.380), channel_id=1, source_target_pairs={{0,8},{4,12},{8,0},{12,4},{16,24},{20,28},{24,16},{28,20},{1,9},{5... | collective-permute-start | bytes 1228808 | tf_op jit(solution)/shard_map/ppermute | solution.py:46
  643.2 35.8 %collective-permute-start.56 = (bf16[2,40,1280]{2,1,0:T(8,128)(2,1)}, bf16[2,40,1280]{2,1,0:T(8,128)(2,1)}, u32[]{:S(2)}, u32[]{:S(2)}) collective-permute-start(bf16[2,40,1280]{2,1,0:T(8,128)(2,1)} %get-tuple-element.396), channel_id=1, source_target_pairs={{0,8},{4,12},{8,0},{12,4},{16,24},{20,28},{24,16},{28,20},{1,9},{5... | collective-permute-start | bytes 614408 | tf_op jit(solution)/shard_map/ppermute | solution.py:46
  645.6 33.4 %collective-permute-start.55 = (bf16[2,40,1280]{2,1,0:T(8,128)(2,1)}, bf16[2,40,1280]{2,1,0:T(8,128)(2,1)}, u32[]{:S(2)}, u32[]{:S(2)}) collective-permute-start(bf16[2,40,1280]{2,1,0:T(8,128)(2,1)} %get-tuple-element.398), channel_id=1, source_target_pairs={{0,16},{4,20},{8,24},{12,28},{16,0},{20,4},{24,8},{28,12},{1,17},{... | collective-permute-start | bytes 614408 | tf_op jit(solution)/shard_map/ppermute | solution.py:46
  667.9 103.6 %collective-permute-start.52 = (bf16[256,1280]{1,0:T(8,128)(2,1)}, bf16[256,1280]{1,0:T(8,128)(2,1)}, u32[]{:S(2)}, u32[]{:S(2)}) collective-permute-start(bf16[256,1280]{1,0:T(8,128)(2,1)} %get-tuple-element.332), channel_id=1, source_target_pairs={{3,0},{7,4},{11,8},{15,12},{19,16},{23,20},{27,24},{31,28}} | collective-permute-start | bytes 1966088 | tf_op jit(solution)/shard_map/ppermute | solution.py:654
  707.6 64.2 %collective-permute-start.51 = (bf16[256,1280]{1,0:T(8,128)(2,1)}, bf16[256,1280]{1,0:T(8,128)(2,1)}, u32[]{:S(2)}, u32[]{:S(2)}) collective-permute-start(bf16[256,1280]{1,0:T(8,128)(2,1)} %get-tuple-element.333), channel_id=1, source_target_pairs={{2,0},{3,1},{6,4},{7,5},{10,8},{11,9},{14,12},{15,13},{18,16},{19,... | collective-permute-start | bytes 1966088 | tf_op jit(solution)/shard_map/ppermute | solution.py:654
  711.6 60.2 %collective-permute-start.50 = (bf16[256,1280]{1,0:T(8,128)(2,1)}, bf16[256,1280]{1,0:T(8,128)(2,1)}, u32[]{:S(2)}, u32[]{:S(2)}) collective-permute-start(bf16[256,1280]{1,0:T(8,128)(2,1)} %get-tuple-element.334), channel_id=1, source_target_pairs={{1,0},{2,1},{3,2},{5,4},{6,5},{7,6},{9,8},{10,9},{11,10},{13,12},{... | collective-permute-start | bytes 1966088 | tf_op jit(solution)/shard_map/ppermute | solution.py:654
  731.4 31.5 %collective-permute-start.66 = (bf16[2,40,1408]{2,1,0:T(8,128)(2,1)}, bf16[2,40,1408]{2,1,0:T(8,128)(2,1)}, u32[]{:S(2)}, u32[]{:S(2)}) collective-permute-start(bf16[2,40,1408]{2,1,0:T(8,128)(2,1)} %get-tuple-element.394), channel_id=1, source_target_pairs={{0,16},{4,20},{8,24},{12,28},{16,0},{20,4},{24,8},{28,12},{1,17},{... | collective-permute-start | bytes 675848 | tf_op jit(solution)/shard_map/ppermute | solution.py:46
  762.9 29.4 %collective-permute-start.69 = (bf16[2,40,1280]{2,1,0:T(8,128)(2,1)}, bf16[2,40,1280]{2,1,0:T(8,128)(2,1)}, u32[]{:S(2)}, u32[]{:S(2)}) collective-permute-start(bf16[2,40,1280]{2,1,0:T(8,128)(2,1)} %dynamic-slice_bitcast_fusion.60), channel_id=1, source_target_pairs={{0,1},{1,0},{2,3},{3,2},{4,5},{5,4},{6,7},{7,6},{8,9},{9,8},{10,11... | collective-permute-start | bytes 614408 | tf_op jit(solution)/shard_map/ppermute | solution.py:51
  767.6 31.8 %collective-permute-start.68 = (bf16[40,3072]{1,0:T(8,128)(2,1)}, bf16[40,3072]{1,0:T(8,128)(2,1)}, u32[]{:S(2)}, u32[]{:S(2)}) collective-permute-start(bf16[40,3072]{1,0:T(8,128)(2,1)} %dynamic-slice_bitcast_fusion.52), channel_id=1, source_target_pairs={{0,2},{1,3},{2,0},{3,1},{4,6},{5,7},{6,4},{7,5},{8,10},{9,11},{10,... | collective-permute-start | bytes 737288 | tf_op jit(solution)/shard_map/ppermute | solution.py:51
  (163 other events, 1847.4 us)
Sparse Core Ops, SparseCore 0:
  158.6 84.5 all-gather.8
  245.3 47.8 all-gather.10
  294.8 86.0 all-gather.12
  382.9 47.8 all-gather.14
  433.6 45.8 reduce-scatter.4
  481.7 82.5 reduce-scatter.6
  567.4 57.8 reduce-scatter.8
  628.1 103.4 reduce-scatter.10
